TPU v7x, 128 devices: a whole 4x4x4 slice. The times are simulated.
128 devices in a mesh: lat: 8 (over y, x_lo), lon: 16 (over z, x_hi, core).
Axes of the slice: x: 4 (x_hi: 2, x_lo: 2; x = x_hi * 2 + x_lo), y: 4, z: 4, core: 2. Of those that a mesh axis runs over, the one named last changes fastest.
Arguments:
- state: bfloat16 [76, 128, 4096], P(None, 'lat', 'lon'), may hold values from -6 to 6
- enc_weight: bfloat16 [76, 256], replicated, may hold values from -0.625 to 0.625
- kernels: float32 [2, 3, 3, 256], replicated, may hold values from -2 to 2
- gains: float32 [2, 256], replicated, may hold values from 0.5 to 2
- up_weight: bfloat16 [2, 256, 1024], replicated, may hold values from -0.375 to 0.375
- down_weight: bfloat16 [2, 1024, 256], replicated, may hold values from -0.1875 to 0.1875
- dec_weight: bfloat16 [256, 76], replicated, may hold values from -0.375 to 0.375
- obs_values: float32 [128, 128, 12, 76], P(('lat', 'lon')), may hold values from -6 to 6
- obs_cells: int32 [128, 128, 12], P(('lat', 'lon')), may hold values from 0 to 4095, as said below
- obs_depth: int32 [128, 128, 12], P(('lat', 'lon')), may hold values from 0 to 76, as said below
Outputs:
- gradient: float32 [76, 128, 4096], P(None, 'lat', 'lon')
Inputs may be any that keep to these rules, and one draw needn't show every extreme that they name: `obs_cells`: A cell of the owner block, row-major over its 16 x 256 cells; cells may repeat. `obs_depth`: 0 marks an empty slot; the live slots of each source and owner come first; some owner receives 12 live profiles from every source.
All inputs are finite; a program needn't handle non-finite values.
Results may differ from a plain program's by a relative error of at most 0.017.
Values may be sent and summed in bfloat16 or wider, within the bound.
No kernel may reach another device: no remote copies, remote signals or barrier semaphores. Data moves between devices by JAX's collectives and lax.ppermute only.
A program may use at most 128 MiB of HBM per device.

v0:
```python
import functools
import math

import jax
import jax.numpy as jnp
from jax import lax
from jax.experimental import pallas as pl
from jax.experimental.pallas import tpu as pltpu
from jax.sharding import PartitionSpec as P

EPSILON = 1e-06
SQRT_TWO_PI = math.sqrt(2.0 / math.pi)
CUBIC = SQRT_TWO_PI * 0.044715
BF = jnp.bfloat16
F32 = jnp.float32

LAT = 16
LON = 256
HID = 256
EXP = 1024
LANES = 128
SIDE = 8
WIDE = LON + 2 * SIDE
SUBL = 16
COLS = WIDE // SUBL
HALO = 4
R = 2
M = R * WIDE
CHUNK = 256
HIGH0 = LAT + 2 * HALO - 2
HIGH1 = HIGH0 - 2
HIGH2 = HIGH1 - 2
TAPE = HIGH2 * WIDE


def sds(shape, dtype):
    return jax.ShapeDtypeStruct(shape, dtype)


def vmem():
    return pl.BlockSpec(memory_space=pltpu.VMEM)


def anywhere():
    return pl.BlockSpec(memory_space=pl.ANY)


def turn(value, shift):
    return pltpu.roll(value.astype(F32), shift, 0).astype(value.dtype)


def convolve(rows, taps):
    out = []
    for r in range(len(rows) - 2):
        part = [
            taps[e] * rows[r] + taps[3 + e] * rows[r + 1] + taps[6 + e] * rows[r + 2]
            for e in range(3)
        ]
        first = turn(part[0][COLS - 1], 1)
        last = turn(part[2][0], SUBL - 1)
        west = jnp.concatenate([first[None], part[0][:-1]], axis=0)
        east = jnp.concatenate([part[2][1:], last[None]], axis=0)
        out.append(part[1] + west + east)
    return out


def fill_taps(tap_ref, kernel_ref, b, flip):
    for a in range(3):
        for e in range(3):
            row = kernel_ref[b, a, e : e + 1, :]
            at = (2 - a) * 3 + 2 - e if flip else a * 3 + e
            tap_ref[at] = jnp.broadcast_to(row, (SUBL, HID)).astype(BF)


def taps_of(tap_ref):
    return [tap_ref[t] for t in range(9)]


def flat(rows):
    return jnp.concatenate([row.reshape(WIDE, HID) for row in rows], axis=0)


def twice(value):
    return jnp.concatenate([value, value], axis=1)


def gelu_pair(pre):
    v = pre.astype(BF)
    u = v * v
    t = jnp.tanh(v * (u * CUBIC + SQRT_TWO_PI))
    w = 1.0 + t
    return v * w, w * (1.0 + (v * (u * (3.0 * CUBIC) + SQRT_TWO_PI)) * (1.0 - t))


def times_transposed(left, right):
    return lax.dot_general(left, right, (((1,), (1,)), ((), ())), preferred_element_type=F32)


def normalize(spatial, mean_ref):
    square = (spatial * spatial).astype(BF)
    mean = jnp.dot(square, mean_ref[...], preferred_element_type=F32)
    inv = lax.rsqrt(mean + EPSILON)
    return inv, spatial * twice(inv.astype(BF))


def forward(b, hat, gain_ref, up_ref, down_ref, act_ref, slope_ref):
    normed = hat * gain_ref[b : b + 1, :].astype(BF)
    for j in range(EXP // CHUNK):
        cut = slice(j * CHUNK, (j + 1) * CHUNK)
        pre = jnp.dot(normed, up_ref[b, :, cut], preferred_element_type=F32)
        act, slope = gelu_pair(pre)
        act_ref[:, cut] = act
        slope_ref[:, cut] = slope
    return 0.5 * jnp.dot(act_ref[...], down_ref[b], preferred_element_type=F32)


def backward(b, grad_s, hat, inv, gain_ref, up_ref, down_ref, act_ref, slope_ref, mean_ref):
    for j in range(EXP // CHUNK):
        cut = slice(j * CHUNK, (j + 1) * CHUNK)
        grad_g = times_transposed(grad_s, down_ref[b, cut, :])
        act_ref[:, cut] = grad_g.astype(BF) * slope_ref[:, cut]
    weighted = times_transposed(act_ref[...], up_ref[b]) * (0.5 * gain_ref[b : b + 1, :])
    hat = hat.astype(F32)
    product = (weighted * hat).astype(BF)
    projection = jnp.dot(product, mean_ref[...], preferred_element_type=F32)
    return twice(inv) * (weighted - hat * twice(projection))


def row_mask(first):
    row = lax.axis_index("lat") * LAT + first
    ok = jnp.logical_and(row >= 0, row < lax.axis_size("lat") * LAT)
    return jnp.where(ok, 1.0, 0.0).astype(F32)


def store_rows(ref, base, value, first=None):
    for r in range(R):
        part = value[r * WIDE : (r + 1) * WIDE]
        if first is not None:
            part = part * row_mask(first + r)
        ref[base + r] = part.astype(BF).reshape(COLS, SUBL, HID)


def from_natural(ref):
    return jnp.concatenate([ref[pl.ds(t, SUBL, stride=COLS), :] for t in range(COLS)], axis=0)


def forward_kernel(
    left_ref, main_ref, right_ref, kernel_ref, gain_ref, up_ref, down_ref,
    out_ref, tape_hbm, hat_hbm, inv_hbm,
    hidden, natural, taps, mean_ref, act, slope, hats, invs, sem,
):
    fill_taps(taps, kernel_ref, 0, False)
    mean_ref[...] = jnp.full((HID, LANES), 1.0 / HID, BF)

    @pl.loop(0, LAT + 2 * HALO)
    def _(i):
        for half in range(2):
            lanes = slice(half * LANES, (half + 1) * LANES)
            natural[half, 0:SIDE, :] = left_ref[i, :, lanes].astype(F32)
            natural[half, SIDE : SIDE + LON, :] = main_ref[i, :, lanes].astype(F32)
            natural[half, SIDE + LON : WIDE, :] = right_ref[i, :, lanes].astype(F32)
            row = from_natural(natural.at[half]).astype(BF)
            hidden[i, :, :, lanes] = row.reshape(COLS, SUBL, LANES)

    def copies(i, slot):
        at = pl.ds(pl.multiple_of((i - 1) * M, 16), M)
        return [
            pltpu.make_async_copy(slope.at[slot], tape_hbm.at[at], sem.at[slot, 0]),
            pltpu.make_async_copy(hats.at[slot], hat_hbm.at[at], sem.at[slot, 1]),
            pltpu.make_async_copy(invs.at[slot], inv_hbm.at[at], sem.at[slot, 2]),
        ]

    steps = HIGH0 // R

    @pl.loop(0, steps)
    def _(i):
        slot = lax.rem(i, 3)

        @pl.when(i >= 4)
        def _():
            for copy in copies(i - 3, slot):
                copy.wait()

        rows = [hidden[i * R + a] for a in range(R + 2)]
        inv, hat = normalize(flat(convolve(rows, taps_of(taps))), mean_ref)
        hats[slot] = hat
        invs[slot] = inv
        branch = forward(0, hat, gain_ref, up_ref, down_ref, act, slope.at[slot])
        store_rows(out_ref, i * R, flat(rows[1:-1]).astype(F32) + branch, i * R + 1 - HALO)

        @pl.when(jnp.logical_and(i >= 1, i < steps - 1))
        def _():
            for copy in copies(i, slot):
                copy.start()

    for i in range(steps - 3, steps - 1):
        for copy in copies(i, i % 3):
            copy.wait()


def main_kernel(
    levels,
    hidden_ref, left_ref, main_ref, right_ref, kernel_ref, gain_ref, up_ref, down_ref,
    dec_ref, enc_ref, tape_hbm, hat_hbm, inv_hbm,
    out_ref,
    taps, mean_ref, natural, act, slope, adjoint, grad_d1, grad_d0, grad1, tape, hats, invs, gathered,
    sem,
):
    copies = [
        pltpu.make_async_copy(tape_hbm, tape, sem.at[0]),
        pltpu.make_async_copy(hat_hbm, hats, sem.at[1]),
        pltpu.make_async_copy(inv_hbm, invs, sem.at[2]),
    ]
    for copy in copies:
        copy.start()
    mean_ref[...] = jnp.full((HID, LANES), 1.0 / HID, BF)
    fill_taps(taps.at[0], kernel_ref, 1, False)
    fill_taps(taps.at[1], kernel_ref, 1, True)
    fill_taps(taps.at[2], kernel_ref, 0, True)

    @pl.loop(0, HIGH1 // R)
    def _(i):
        rows = [hidden_ref[i * R + a] for a in range(R + 2)]
        inv, hat = normalize(flat(convolve(rows, taps_of(taps.at[0]))), mean_ref)
        branch = forward(1, hat, gain_ref, up_ref, down_ref, act, slope)
        final = (flat(rows[1:-1]).astype(F32) + branch).astype(BF)
        model = jnp.dot(final, dec_ref[...], preferred_element_type=F32)
        fields = []
        for r in range(R):
            pair = []
            for half in range(2):
                lanes = slice(half * LANES, (half + 1) * LANES)
                place = natural.at[2 * r + half]
                place[0:SIDE, :] = left_ref[i * R + r, :, lanes]
                place[SIDE : SIDE + LON, :] = main_ref[i * R + r, :, lanes]
                place[SIDE + LON : WIDE, :] = right_ref[i * R + r, :, lanes]
                pair.append(from_natural(place))
            fields.append((pair[1], pair[0]))
        counts = jnp.concatenate([f[0] for f in fields], axis=0)
        sums = jnp.concatenate([f[1] for f in fields], axis=0)
        adj = (counts[:, :levels] * model - sums[:, :levels]).astype(BF)
        for r in range(R):
            adjoint[i * R + r] = adj[r * WIDE : (r + 1) * WIDE]
        grad_s = times_transposed(adj, dec_ref[...]).astype(BF)
        grad_d = backward(
            1, grad_s, hat, inv, gain_ref, up_ref, down_ref, act, slope, mean_ref
        )
        store_rows(grad_d1, i * R, grad_d)

    for copy in copies:
        copy.wait()

    @pl.loop(0, HIGH2 // R)
    def _(i):
        rows = [grad_d1[i * R + a] for a in range(R + 2)]
        adj = jnp.concatenate([adjoint[i * R + 1 + r] for r in range(R)], axis=0)
        grad = times_transposed(adj, dec_ref[...])
        grad = grad + flat(convolve(rows, taps_of(taps.at[1]))).astype(F32)
        grad_s = grad.astype(BF)
        store_rows(grad1, i * R, grad_s)
        at = pl.ds(pl.multiple_of(i * M, 16), M)
        grad_d = backward(
            0, grad_s, hats[at], invs[at], gain_ref, up_ref, down_ref, act, tape.at[at], mean_ref
        )
        store_rows(grad_d0, i * R, grad_d, i * R - 1)

    @pl.loop(0, LAT // R)
    def _(i):
        rows = [grad_d0[i * R + a] for a in range(R + 2)]
        conv = convolve(rows, taps_of(taps.at[2]))
        for r in range(R):
            total = conv[r].astype(F32) + grad1[i * R + 1 + r].astype(F32)
            halves = []
            for half in range(2):
                place = natural.at[2 * r + half]
                for t in range(COLS):
                    place[pl.ds(t, SUBL, stride=COLS), :] = total[
                        t, :, half * LANES : (half + 1) * LANES
                    ]
                halves.append(place[SIDE : SIDE + LON, :].astype(BF))
            result = times_transposed(enc_ref[...], jnp.concatenate(halves, axis=1))
            for half in range(2):
                gathered[half, pl.ds(i * R + r, enc_ref.shape[0], stride=LAT), :] = result[
                    :, half * LANES : (half + 1) * LANES
                ]

    for half in range(2):
        out_ref[:, half * LANES : (half + 1) * LANES] = gathered[half]


def place_observations(levels, table_ref, out_ref, hot_ref, row_ref, value_ref):
    @pl.when(pl.program_id(0) == 0)
    def _():
        table = table_ref[...]
        flipped = jnp.transpose(table.astype(F32))
        slots = flipped.shape[1]
        column = flipped[levels + 1 : levels + 2, :]
        iota = lax.broadcasted_iota(jnp.int32, (LON, slots), 0).astype(F32)
        hot_ref[...] = jnp.where(iota == column, 1.0, 0.0).astype(BF)
        row_ref[...] = jnp.broadcast_to(flipped[levels : levels + 1, :], (16, slots))
        depth = table[:, levels + 2 : levels + 3].astype(F32)
        lane = lax.broadcasted_iota(jnp.int32, table.shape, 1)
        mask = jnp.where(lane.astype(F32) < depth, 1.0, 0.0)
        value_ref[:, :LANES] = (table.astype(F32) * mask).astype(BF)
        value_ref[:, LANES:] = mask.astype(BF)

    here = pl.program_id(0).astype(F32)
    keep = jnp.where(row_ref[0:1, :] == here, 1.0, 0.0).astype(BF)
    out_ref[0] = jnp.dot(hot_ref[...] * keep, value_ref[...], preferred_element_type=F32)


def pair_shift(low, high, axis, wrap):
    peers = lax.axis_size(axis)
    up = [(i, (i + 1) % peers) for i in range(peers if wrap else peers - 1)]
    down = [(j, i) for i, j in up]
    return lax.ppermute(high, axis, up), lax.ppermute(low, axis, down)


def kernel_params(limit):
    return pltpu.CompilerParams(vmem_limit_bytes=limit * 1024 * 1024)


def params():
    return pltpu.CompilerParams(
        dimension_semantics=("arbitrary",), vmem_limit_bytes=32 * 1024 * 1024
    )


def whole(shape):
    return pl.BlockSpec(shape, lambda *_: (0,) * len(shape))


def body(
    state, enc_weight, kernels, gains, up_weight, down_weight, dec_weight,
    obs_values, obs_cells, obs_depth,
):
    channels = state.shape[0]
    levels = dec_weight.shape[1]
    owners, slots = obs_cells.shape[1:]

    cells = obs_cells[0]
    tags = jnp.stack([cells // LON, cells % LON, obs_depth[0]], axis=-1).astype(BF)
    packed = jnp.concatenate([obs_values[0].astype(BF), tags], axis=-1)
    packed = jnp.pad(packed, ((0, 0), (0, 16 - slots), (0, LANES - levels - 3)))
    table = lax.all_to_all(packed, ("lat", "lon"), split_axis=0, concat_axis=0, tiled=True)

    top, bottom = pair_shift(state[:, :HALO], state[:, LAT - HALO :], "lat", False)
    tall = jnp.concatenate([top, state, bottom], axis=1)
    main = lax.dot_general(
        tall, enc_weight, (((0,), (0,)), ((), ())), preferred_element_type=F32
    ).astype(BF)
    left, right = pair_shift(main[:, :SIDE], main[:, LON - SIDE :], "lon", True)

    mlp = 2 * WIDE * HID * EXP * 2
    hidden, tape, hat, inv = pl.pallas_call(
        forward_kernel,
        out_shape=[
            sds((HIGH0, COLS, SUBL, HID), BF),
            sds((TAPE, EXP), BF),
            sds((TAPE, HID), BF),
            sds((TAPE, LANES), F32),
        ],
        in_specs=[vmem()] * 7,
        out_specs=[vmem()] + [anywhere()] * 3,
        scratch_shapes=[
            pltpu.VMEM((LAT + 2 * HALO, COLS, SUBL, HID), BF),
            pltpu.VMEM((2, WIDE, LANES), F32),
            pltpu.VMEM((9, SUBL, HID), BF),
            pltpu.VMEM((HID, LANES), BF),
            pltpu.VMEM((M, EXP), BF),
            pltpu.VMEM((3, M, EXP), BF),
            pltpu.VMEM((3, M, HID), BF),
            pltpu.VMEM((3, M, LANES), F32),
            pltpu.SemaphoreType.DMA((3, 3)),
        ],
        compiler_params=kernel_params(40),
        cost_estimate=pl.CostEstimate(
            flops=mlp * HIGH0, bytes_accessed=TAPE * EXP * 2, transcendentals=0
        ),
        name="forward_zero",
    )(left, main, right, kernels, gains, up_weight, down_weight)

    table = table.reshape(owners * 16, LANES)
    field = pl.pallas_call(
        functools.partial(place_observations, levels),
        out_shape=sds((LAT, LON, 2 * LANES), F32),
        grid=(LAT,),
        in_specs=[whole(table.shape)],
        out_specs=pl.BlockSpec((1, LON, 2 * LANES), lambda s: (s, 0, 0)),
        scratch_shapes=[
            pltpu.VMEM((LON, owners * 16), BF),
            pltpu.VMEM((16, owners * 16), F32),
            pltpu.VMEM((owners * 16, 2 * LANES), BF),
        ],
        compiler_params=params(),
        cost_estimate=pl.CostEstimate(
            flops=2 * LAT * LON * owners * 16 * 256, bytes_accessed=2**22, transcendentals=0
        ),
        name="place_observations",
    )(table)
    f_top, f_bottom = pair_shift(field[:2], field[LAT - 2 :], "lat", False)
    field = jnp.concatenate([f_top, field, f_bottom], axis=0)
    f_left, f_right = pair_shift(field[:, :SIDE], field[:, LON - SIDE :], "lon", True)

    gradient = pl.pallas_call(
        functools.partial(main_kernel, levels),
        out_shape=sds((channels * LAT, LON), F32),
        in_specs=[vmem()] * 10 + [anywhere()] * 3,
        out_specs=vmem(),
        scratch_shapes=[
            pltpu.VMEM((3, 9, SUBL, HID), BF),
            pltpu.VMEM((HID, LANES), BF),
            pltpu.VMEM((2 * R, WIDE, LANES), F32),
            pltpu.VMEM((M, EXP), BF),
            pltpu.VMEM((M, EXP), BF),
            pltpu.VMEM((HIGH1, WIDE, levels), BF),
            pltpu.VMEM((HIGH1, COLS, SUBL, HID), BF),
            pltpu.VMEM((HIGH2, COLS, SUBL, HID), BF),
            pltpu.VMEM((HIGH2, COLS, SUBL, HID), BF),
            pltpu.VMEM((TAPE, EXP), BF),
            pltpu.VMEM((TAPE, HID), BF),
            pltpu.VMEM((TAPE, LANES), F32),
            pltpu.VMEM((2, channels * LAT, LANES), F32),
            pltpu.SemaphoreType.DMA((3,)),
        ],
        compiler_params=kernel_params(52),
        cost_estimate=pl.CostEstimate(
            flops=mlp * (2 * HIGH1 + HIGH2), bytes_accessed=TAPE * EXP * 2, transcendentals=0
        ),
        name="forward_one_and_adjoint",
    )(
        hidden, f_left, field, f_right, kernels, gains, up_weight, down_weight, dec_weight,
        enc_weight, tape, hat, inv,
    )
    return gradient.reshape(channels, LAT, LON)


def solution(mesh):
    in_specs = (
        P(None, "lat", "lon"),
        P(),
        P(),
        P(),
        P(),
        P(),
        P(),
        P(("lat", "lon"), None, None, None),
        P(("lat", "lon"), None, None),
        P(("lat", "lon"), None, None),
    )
    out_specs = P(None, "lat", "lon")
    return jax.shard_map(body, mesh=mesh, in_specs=in_specs, out_specs=out_specs, check_vma=False)
```

profile of v0, /device:TPU:1, one launch (start us, length us, event | category | flops | bytes accessed | tf_op | source)
XLA Modules:
  0.0 131.7 jit_solution(16091447750358970307)
XLA Ops:
  0.0 0.8 fusion.20
  0.8 0.7 fusion.19
  2.9 1.5 %copy.53 = bf16[1,128,12,76]{3,2,1,0:T(8,128)(2,1)S(1)} copy(f32[1,128,12,76]{1,0,3,2:T(1,128)} %param.17) | data formatting | bytes 700416 | tf_op args[7]
  4.5 1.7 %fusion.13 = bf16[128,16,128]{2,1,0:T(8,128)(2,1)} fusion(bf16[128,12,1]{2,1,0:T(8,128)(2,1)S(1)} %copy.57, bf16[128,12,1]{2,1,0:T(8,128)(2,1)S(1)} %copy.56, bf16[128,12,1]{2,1,0:T(8,128)(2,1)S(1)} %copy.55, bf16[128,12,76]{2,1,0:T(8,128)(2,1)S(1)} %bitcast.25), kind=kLoop, calls=%fused_computation.17 | loop fusion | flops 4980736 | bytes 766976 | tf_op jit(solution)/shard_map/concatenate | solution.py:343
  6.2 11.5 %all-to-all-start = ((bf16[128,16,128]{2,1,0:T(8,128)(2,1)}), bf16[128,16,128]{2,1,0:T(8,128)(2,1)S(1)}, u32[]{:S(2)}, u32[]{:S(2)}) async-start(bf16[128,16,128]{2,1,0:T(8,128)(2,1)} %fusion.13), calls=%async_computation | async-start | bytes 1048576 | tf_op jit(solution)/shard_map/all_to_all | solution.py:345
  17.9 3.3 %collective-permute-start = (bf16[76,4,256]{2,0,1:T(8,128)(2,1)S(1)}, bf16[76,4,256]{2,0,1:T(8,128)(2,1)S(1)}, u32[]{:S(2)}, u32[]{:S(2)}) collective-permute-start(bf16[76,4,256]{2,0,1:T(8,128)(2,1)S(1)} %get-tuple-element.21), channel_id=1, source_target_pairs={{0,16},{16,32},{32,48},{48,64},{64,80},{80,96},{96,112},{1,17},{17... | collective-permute-start | bytes 466952 | tf_op jit(solution)/shard_map/ppermute | solution.py:316
  21.2 1.3 collective-permute-start.1
  22.7 8.6 %all-to-all-done = bf16[128,16,128]{2,1,0:T(8,128)(2,1)S(1)} async-done(((bf16[128,16,128]{2,1,0:T(8,128)(2,1)}), bf16[128,16,128]{2,1,0:T(8,128)(2,1)S(1)}, u32[]{:S(2)}, u32[]{:S(2)}) %all-to-all-start) | async-done | bytes 524320 | tf_op jit(solution)/shard_map/all_to_all | solution.py:345
  31.3 7.8 %place_observations.1 = f32[16,256,256]{2,1,0:T(8,128)S(1)} custom-call(bf16[2048,128]{1,0:T(8,128)(2,1)S(1)} %bitcast.24), custom_call_target="tpu_custom_call" | custom-call | flops 4294967296 | bytes 4194304 | tf_op jit(solution)/shard_map/place_observations/pallas_call | solution.py:384
  39.3 1.9 %collective-permute-start.4 = (f32[2,256,256]{2,1,0:T(8,128)S(1)}, f32[2,256,256]{2,1,0:T(8,128)S(1)}, u32[]{:S(2)}, u32[]{:S(2)}) collective-permute-start(f32[2,256,256]{2,1,0:T(8,128)S(1)} %get-tuple-element.17), channel_id=1, source_target_pairs={{0,16},{16,32},{32,48},{48,64},{64,80},{80,96},{96,112},{1,17},{17... | collective-permute-start | bytes 1572872 | tf_op jit(solution)/shard_map/ppermute | solution.py:316
  41.2 1.3 collective-permute-start.5
  42.5 1.0 convolution_convert_fusion.main_ref
  43.6 1.9 %collective-permute-start.3 = (bf16[24,8,256]{2,1,0:T(8,128)(2,1)S(1)}, bf16[24,8,256]{2,1,0:T(8,128)(2,1)S(1)}, u32[]{:S(2)}, u32[]{:S(2)}) collective-permute-start(bf16[24,8,256]{2,1,0:T(8,128)(2,1)S(1)} %get-tuple-element.19), channel_id=1, source_target_pairs={{1,0},{2,1},{3,2},{4,3},{5,4},{6,5},{7,6},{8,7},{9,8},{10,9},{11,1... | collective-permute-start | bytes 294920 | tf_op jit(solution)/shard_map/ppermute | solution.py:316
  45.5 1.6 %collective-permute-start.2 = (bf16[24,8,256]{2,1,0:T(8,128)(2,1)S(1)}, bf16[24,8,256]{2,1,0:T(8,128)(2,1)S(1)}, u32[]{:S(2)}, u32[]{:S(2)}) collective-permute-start(bf16[24,8,256]{2,1,0:T(8,128)(2,1)S(1)} %get-tuple-element.20), channel_id=1, source_target_pairs={{0,1},{1,2},{2,3},{3,4},{4,5},{5,6},{6,7},{7,8},{8,9},{9,10},{10,1... | collective-permute-start | bytes 294920 | tf_op jit(solution)/shard_map/ppermute | solution.py:316
  47.1 3.7 %collective-permute-done.4 = f32[2,256,256]{2,1,0:T(8,128)S(1)} collective-permute-done((f32[2,256,256]{2,1,0:T(8,128)S(1)}, f32[2,256,256]{2,1,0:T(8,128)S(1)}, u32[]{:S(2)}, u32[]{:S(2)}) %collective-permute-start.4) | collective-permute-done | bytes 524320 | tf_op jit(solution)/shard_map/ppermute | solution.py:316
  50.8 13.2 %collective-permute-done.5 = f32[2,256,256]{2,1,0:T(8,128)S(1)} collective-permute-done((f32[2,256,256]{2,1,0:T(8,128)S(1)}, f32[2,256,256]{2,1,0:T(8,128)S(1)}, u32[]{:S(2)}, u32[]{:S(2)}) %collective-permute-start.5) | collective-permute-done | bytes 524320 | tf_op jit(solution)/shard_map/ppermute | solution.py:316
  64.0 0.5 pad_maximum_fusion.main_ref
  64.5 3.6 %collective-permute-start.7 = (f32[20,8,256]{2,1,0:T(8,128)S(1)}, f32[20,8,256]{2,1,0:T(8,128)S(1)}, u32[]{:S(2)}, u32[]{:S(2)}) collective-permute-start(f32[20,8,256]{2,1,0:T(8,128)S(1)} %get-tuple-element.15), channel_id=1, source_target_pairs={{1,0},{2,1},{3,2},{4,3},{5,4},{6,5},{7,6},{8,7},{9,8},{10,9},{11,1... | collective-permute-start | bytes 491528 | tf_op jit(solution)/shard_map/ppermute | solution.py:316
  68.1 1.2 collective-permute-start.6
  69.4 14.4 %forward_zero.1 = (bf16[22,17,16,256]{3,2,1,0:T(8,128)(2,1)S(1)}, bf16[4896,1024]{1,0:T(8,128)(2,1)}, bf16[4896,256]{1,0:T(8,128)(2,1)S(1)}, f32[4896,128]{1,0:T(8,128)S(1)}) custom-call(bf16[24,8,256]{2,1,0:T(8,128)(2,1)S(1)} %collective-permute-done.2.left_ref, bf16[24,256,256]{2,1,0:T(8,128)(2,1)S(1)} %convolution_convert_fusion.main_ref, ...), custom_call_target="tpu_custom_call" | custom-call | flops 6274678784 | bytes 10027008 | tf_op jit(solution)/shard_map/forward_zero/pallas_call | solution.py:355
  83.8 1.6 %copy-done.4 = bf16[22,17,16,256]{3,2,1,0:T(8,128)(2,1)} copy-done((bf16[22,17,16,256]{3,2,1,0:T(8,128)(2,1)}, bf16[22,17,16,256]{3,2,1,0:T(8,128)(2,1)S(1)}, u32[]{:S(2)}) %copy-start.4) | copy-done | bytes 3063832
  85.4 1.4 %copy-done.5 = bf16[4896,256]{1,0:T(8,128)(2,1)} copy-done((bf16[4896,256]{1,0:T(8,128)(2,1)}, bf16[4896,256]{1,0:T(8,128)(2,1)S(1)}, u32[]{:S(2)}) %copy-start.5) | copy-done | bytes 2506776
  86.9 1.5 %copy-done.6 = f32[4896,128]{1,0:T(8,128)} copy-done((f32[4896,128]{1,0:T(8,128)}, f32[4896,128]{1,0:T(8,128)S(1)}, u32[]{:S(2)}) %copy-start.6) | copy-done | bytes 2506776
  88.4 43.1 %forward_one_and_adjoint.1 = f32[1216,256]{1,0:T(8,128)} custom-call(bf16[22,17,16,256]{3,2,1,0:T(8,128)(2,1)} %copy-done.4, f32[20,8,256]{2,1,0:T(8,128)S(1)} %collective-permute-done.6.left_ref, f32[20,256,256]{2,1,0:T(8,128)} %copy-done.7, f32[20,8,256]{2,1,0:T(8,128)S(1)} %collective-permute-done.7.right_ref, f32[2,3,3,256]{3,2,1,0:T(4,128)S(1)} %copy.52.kernel_ref, ...), custom_call_target="tpu_custom_call" | custom-call | flops 16542334976 | bytes 10027008 | tf_op jit(solution)/shard_map/forward_one_and_adjoint/pallas_call | solution.py:405
  (36 shorter events, 1.9 us)
Async XLA Ops:
  0.0 17.7 %copy-start.8 = (bf16[76,16,256]{2,1,0:T(8,128)(2,1)S(1)}, bf16[76,16,256]{2,1,0:T(8,128)(2,1)}, u32[]{:S(2)}) copy-start(bf16[76,16,256]{2,1,0:T(8,128)(2,1)} %param.10) | copy-start | bytes 1867780
  0.0 22.5 %copy-start.10 = (f32[2,3,3,256]{3,0,2,1:T(2,128)S(1)}, f32[2,3,3,256]{3,0,2,1:T(2,128)}, u32[]{:S(2)}) copy-start(f32[2,3,3,256]{3,0,2,1:T(2,128)} %param.12) | copy-start | bytes 55300
  0.0 22.6 %copy-start.9 = (bf16[256,76]{0,1:T(8,128)(2,1)S(1)}, bf16[256,76]{0,1:T(8,128)(2,1)}, u32[]{:S(2)}) copy-start(bf16[256,76]{0,1:T(8,128)(2,1)} %param.16) | copy-start | bytes 116740
  6.2 25.1 %all-to-all-start = ((bf16[128,16,128]{2,1,0:T(8,128)(2,1)}), bf16[128,16,128]{2,1,0:T(8,128)(2,1)S(1)}, u32[]{:S(2)}, u32[]{:S(2)}) async-start(bf16[128,16,128]{2,1,0:T(8,128)(2,1)} %fusion.13), calls=%async_computation | async-start | bytes 1048576 | tf_op jit(solution)/shard_map/all_to_all | solution.py:345
  17.9 24.6 %collective-permute-start = (bf16[76,4,256]{2,0,1:T(8,128)(2,1)S(1)}, bf16[76,4,256]{2,0,1:T(8,128)(2,1)S(1)}, u32[]{:S(2)}, u32[]{:S(2)}) collective-permute-start(bf16[76,4,256]{2,0,1:T(8,128)(2,1)S(1)} %get-tuple-element.21), channel_id=1, source_target_pairs={{0,16},{16,32},{32,48},{48,64},{64,80},{80,96},{96,112},{1,17},{17... | collective-permute-start | bytes 466952 | tf_op jit(solution)/shard_map/ppermute | solution.py:316
  21.2 21.3 %collective-permute-start.1 = (bf16[76,4,256]{2,0,1:T(8,128)(2,1)S(1)}, bf16[76,4,256]{2,0,1:T(8,128)(2,1)S(1)}, u32[]{:S(2)}, u32[]{:S(2)}) collective-permute-start(bf16[76,4,256]{2,0,1:T(8,128)(2,1)S(1)} %get-tuple-element.22), channel_id=1, source_target_pairs={{16,0},{32,16},{48,32},{64,48},{80,64},{96,80},{112,96},{17,1},{33... | collective-permute-start | bytes 466952 | tf_op jit(solution)/shard_map/ppermute | solution.py:316
  31.3 11.2 %copy-start = (bf16[76,256]{1,0:T(8,128)(2,1)S(1)}, bf16[76,256]{1,0:T(8,128)(2,1)}, u32[]{:S(2)}) copy-start(bf16[76,256]{1,0:T(8,128)(2,1)} %enc_ref.1) | copy-start | bytes 116740
  39.3 11.6 %collective-permute-start.4 = (f32[2,256,256]{2,1,0:T(8,128)S(1)}, f32[2,256,256]{2,1,0:T(8,128)S(1)}, u32[]{:S(2)}, u32[]{:S(2)}) collective-permute-start(f32[2,256,256]{2,1,0:T(8,128)S(1)} %get-tuple-element.17), channel_id=1, source_target_pairs={{0,16},{16,32},{32,48},{48,64},{64,80},{80,96},{96,112},{1,17},{17... | collective-permute-start | bytes 1572872 | tf_op jit(solution)/shard_map/ppermute | solution.py:316
  41.2 22.8 %collective-permute-start.5 = (f32[2,256,256]{2,1,0:T(8,128)S(1)}, f32[2,256,256]{2,1,0:T(8,128)S(1)}, u32[]{:S(2)}, u32[]{:S(2)}) collective-permute-start(f32[2,256,256]{2,1,0:T(8,128)S(1)} %get-tuple-element.18), channel_id=1, source_target_pairs={{16,0},{32,16},{48,32},{64,48},{80,64},{96,80},{112,96},{17,1},{33... | collective-permute-start | bytes 1572872 | tf_op jit(solution)/shard_map/ppermute | solution.py:316
  43.6 25.8 %collective-permute-start.3 = (bf16[24,8,256]{2,1,0:T(8,128)(2,1)S(1)}, bf16[24,8,256]{2,1,0:T(8,128)(2,1)S(1)}, u32[]{:S(2)}, u32[]{:S(2)}) collective-permute-start(bf16[24,8,256]{2,1,0:T(8,128)(2,1)S(1)} %get-tuple-element.19), channel_id=1, source_target_pairs={{1,0},{2,1},{3,2},{4,3},{5,4},{6,5},{7,6},{8,7},{9,8},{10,9},{11,1... | collective-permute-start | bytes 294920 | tf_op jit(solution)/shard_map/ppermute | solution.py:316
  45.5 23.9 %copy-start.1 = (bf16[2,256,1024]{2,1,0:T(8,128)(2,1)S(1)}, bf16[2,256,1024]{2,1,0:T(8,128)(2,1)}, u32[]{:S(2)}) copy-start(bf16[2,256,1024]{2,1,0:T(8,128)(2,1)} %up_ref.3) | copy-start | bytes 3145732
  45.5 23.9 %copy-start.2 = (bf16[2,1024,256]{2,1,0:T(8,128)(2,1)S(1)}, bf16[2,1024,256]{2,1,0:T(8,128)(2,1)}, u32[]{:S(2)}) copy-start(bf16[2,1024,256]{2,1,0:T(8,128)(2,1)} %down_ref.3) | copy-start | bytes 3145732
  45.5 23.9 %copy-start.3 = (f32[2,256]{1,0:T(2,128)S(1)}, f32[2,256]{1,0:T(2,128)}, u32[]{:S(2)}) copy-start(f32[2,256]{1,0:T(2,128)} %gain_ref.3) | copy-start | bytes 6148
  45.5 23.9 %collective-permute-start.2 = (bf16[24,8,256]{2,1,0:T(8,128)(2,1)S(1)}, bf16[24,8,256]{2,1,0:T(8,128)(2,1)S(1)}, u32[]{:S(2)}, u32[]{:S(2)}) collective-permute-start(bf16[24,8,256]{2,1,0:T(8,128)(2,1)S(1)} %get-tuple-element.20), channel_id=1, source_target_pairs={{0,1},{1,2},{2,3},{3,4},{4,5},{5,6},{6,7},{7,8},{8,9},{9,10},{10,1... | collective-permute-start | bytes 294920 | tf_op jit(solution)/shard_map/ppermute | solution.py:316
  64.5 4.9 %copy-start.7 = (f32[20,256,256]{2,1,0:T(8,128)}, f32[20,256,256]{2,1,0:T(8,128)S(1)}, u32[]{:S(2)}) copy-start(f32[20,256,256]{2,1,0:T(8,128)S(1)} %pad_maximum_fusion.main_ref) | copy-start | bytes 15728644
  64.5 23.9 %collective-permute-start.7 = (f32[20,8,256]{2,1,0:T(8,128)S(1)}, f32[20,8,256]{2,1,0:T(8,128)S(1)}, u32[]{:S(2)}, u32[]{:S(2)}) collective-permute-start(f32[20,8,256]{2,1,0:T(8,128)S(1)} %get-tuple-element.15), channel_id=1, source_target_pairs={{1,0},{2,1},{3,2},{4,3},{5,4},{6,5},{7,6},{8,7},{9,8},{10,9},{11,1... | collective-permute-start | bytes 491528 | tf_op jit(solution)/shard_map/ppermute | solution.py:316
  68.1 20.3 %collective-permute-start.6 = (f32[20,8,256]{2,1,0:T(8,128)S(1)}, f32[20,8,256]{2,1,0:T(8,128)S(1)}, u32[]{:S(2)}, u32[]{:S(2)}) collective-permute-start(f32[20,8,256]{2,1,0:T(8,128)S(1)} %get-tuple-element.16), channel_id=1, source_target_pairs={{0,1},{1,2},{2,3},{3,4},{4,5},{5,6},{6,7},{7,8},{8,9},{9,10},{10,1... | collective-permute-start | bytes 491528 | tf_op jit(solution)/shard_map/ppermute | solution.py:316
  83.8 1.6 %copy-start.4 = (bf16[22,17,16,256]{3,2,1,0:T(8,128)(2,1)}, bf16[22,17,16,256]{3,2,1,0:T(8,128)(2,1)S(1)}, u32[]{:S(2)}) copy-start(bf16[22,17,16,256]{3,2,1,0:T(8,128)(2,1)S(1)} %get-tuple-element.9.hidden_ref) | copy-start | bytes 9191428
  85.4 1.4 %copy-start.5 = (bf16[4896,256]{1,0:T(8,128)(2,1)}, bf16[4896,256]{1,0:T(8,128)(2,1)S(1)}, u32[]{:S(2)}) copy-start(bf16[4896,256]{1,0:T(8,128)(2,1)S(1)} %get-tuple-element.11.hat_hbm) | copy-start | bytes 7520260
  86.9 1.5 %copy-start.6 = (f32[4896,128]{1,0:T(8,128)}, f32[4896,128]{1,0:T(8,128)S(1)}, u32[]{:S(2)}) copy-start(f32[4896,128]{1,0:T(8,128)S(1)} %get-tuple-element.12.inv_hbm) | copy-start | bytes 7520260
where the time goes:
time: 132 us
  Pallas kernels  65.3 us (49%)
  starting transfers between devices  27.7 us (21%)
  waiting for transfers between devices  25.6 us (19%)
  local copies, waits for them, and re-layouts  7.96 us (6%)
  other arithmetic  3.69 us (3%)
    pallas_call x1, Pallas kernels, body(): pl.pallas_call(functools.partial(main_kernel, levels), out_shape=sds((cha...  43.1 us
    ppermute x8, waiting for transfers between devices, pair_shift(): return (lax.ppermute(high, axis, up), lax.ppermute(low, axis, down))  16.9 us
    ppermute x8, starting transfers between devices, pair_shift(): return (lax.ppermute(high, axis, up), lax.ppermute(low, axis, down))  16.2 us
    pallas_call x1, Pallas kernels, body(): pl.pallas_call(forward_kernel, out_shape=[sds((HIGH0, COLS, SUBL, HID), B...  14.4 us
    all_to_all x1, starting transfers between devices, body(): lax.all_to_all(packed, ('lat', 'lon'), split_axis=0, concat_axis=0, tiled...  11.5 us
    all_to_all x1, waiting for transfers between devices, body(): lax.all_to_all(packed, ('lat', 'lon'), split_axis=0, concat_axis=0, tiled...  8.63 us
    pallas_call x1, Pallas kernels, body(): pl.pallas_call(functools.partial(place_observations, levels), out_shape=s...  7.84 us
    unnamed x26, local copies, waits for them, and re-layouts  6.46 us
  transfers between devices with their start and end apart: 9, of which 3 were waited for; matrix products, arithmetic and copies ran while one was open for 1% of the time, Pallas kernels for 17%

commit v1 on v0

--- a/solution.py
+++ b/solution.py
@@ -145,6 +145,7 @@
 
 
 def forward_kernel(
+    first, count,
     left_ref, main_ref, right_ref, kernel_ref, gain_ref, up_ref, down_ref,
     out_ref, tape_hbm, hat_hbm, inv_hbm,
     hidden, natural, taps, mean_ref, act, slope, hats, invs, sem,
@@ -152,31 +153,33 @@
     fill_taps(taps, kernel_ref, 0, False)
     mean_ref[...] = jnp.full((HID, LANES), 1.0 / HID, BF)
 
-    @pl.loop(0, LAT + 2 * HALO)
+    @pl.loop(0, count + 2)
     def _(i):
         for half in range(2):
             lanes = slice(half * LANES, (half + 1) * LANES)
-            natural[half, 0:SIDE, :] = left_ref[i, :, lanes].astype(F32)
-            natural[half, SIDE : SIDE + LON, :] = main_ref[i, :, lanes].astype(F32)
-            natural[half, SIDE + LON : WIDE, :] = right_ref[i, :, lanes].astype(F32)
+            natural[half, 0:SIDE, :] = left_ref[first + i, :, lanes].astype(F32)
+            natural[half, SIDE : SIDE + LON, :] = main_ref[first + i, :, lanes].astype(F32)
+            natural[half, SIDE + LON : WIDE, :] = right_ref[first + i, :, lanes].astype(F32)
             row = from_natural(natural.at[half]).astype(BF)
             hidden[i, :, :, lanes] = row.reshape(COLS, SUBL, LANES)
 
+    steps = count // R
+    taped = max(1 - first // R, 0)
+    ends = min((HIGH0 - first) // R - 1, steps)
+
     def copies(i, slot):
-        at = pl.ds(pl.multiple_of((i - 1) * M, 16), M)
+        at = pl.ds(pl.multiple_of((i - taped) * M, 16), M)
         return [
             pltpu.make_async_copy(slope.at[slot], tape_hbm.at[at], sem.at[slot, 0]),
             pltpu.make_async_copy(hats.at[slot], hat_hbm.at[at], sem.at[slot, 1]),
             pltpu.make_async_copy(invs.at[slot], inv_hbm.at[at], sem.at[slot, 2]),
         ]
 
-    steps = HIGH0 // R
-
     @pl.loop(0, steps)
     def _(i):
         slot = lax.rem(i, 3)
 
-        @pl.when(i >= 4)
+        @pl.when(i >= taped + 3)
         def _():
             for copy in copies(i - 3, slot):
                 copy.wait()
@@ -186,58 +189,80 @@
         hats[slot] = hat
         invs[slot] = inv
         branch = forward(0, hat, gain_ref, up_ref, down_ref, act, slope.at[slot])
-        store_rows(out_ref, i * R, flat(rows[1:-1]).astype(F32) + branch, i * R + 1 - HALO)
-
-        @pl.when(jnp.logical_and(i >= 1, i < steps - 1))
+        total = flat(rows[1:-1]).astype(F32) + branch
+        store_rows(out_ref, i * R, total, first + i * R + 1 - HALO)
+
+        @pl.when(jnp.logical_and(i >= taped, i < ends))
         def _():
             for copy in copies(i, slot):
                 copy.start()
 
-    for i in range(steps - 3, steps - 1):
+    for i in range(max(taped, steps - 3), ends):
         for copy in copies(i, i % 3):
             copy.wait()
 
 
 def main_kernel(
     levels,
-    hidden_ref, left_ref, main_ref, right_ref, kernel_ref, gain_ref, up_ref, down_ref,
-    dec_ref, enc_ref, tape_hbm, hat_hbm, inv_hbm,
+    above_ref, below_ref, left_ref, main_ref, right_ref, kernel_ref, gain_ref, up_ref, down_ref,
+    dec_ref, enc_ref, hidden_a, tape_a, hat_a, inv_a, hidden_b, tape_b, hat_b, inv_b,
     out_ref,
-    taps, mean_ref, natural, act, slope, adjoint, grad_d1, grad_d0, grad1, tape, hats, invs, gathered,
-    sem,
+    hidden, taps, mean_ref, natural, act, slope, adjoint, grad_d1, grad_d0, grad1,
+    tape, hats, invs, gathered, sem,
 ):
+    rows_a = hidden_a.shape[0]
+    cells_a = tape_a.shape[0]
+    early = [
+        pltpu.make_async_copy(hidden_a, hidden.at[:rows_a], sem.at[0]),
+        pltpu.make_async_copy(hidden_b, hidden.at[rows_a:], sem.at[1]),
+    ]
     copies = [
-        pltpu.make_async_copy(tape_hbm, tape, sem.at[0]),
-        pltpu.make_async_copy(hat_hbm, hats, sem.at[1]),
-        pltpu.make_async_copy(inv_hbm, invs, sem.at[2]),
+        pltpu.make_async_copy(tape_a, tape.at[:cells_a], sem.at[2]),
+        pltpu.make_async_copy(tape_b, tape.at[cells_a:], sem.at[3]),
+        pltpu.make_async_copy(hat_a, hats.at[:cells_a], sem.at[4]),
+        pltpu.make_async_copy(hat_b, hats.at[cells_a:], sem.at[5]),
+        pltpu.make_async_copy(inv_a, invs.at[:cells_a], sem.at[6]),
+        pltpu.make_async_copy(inv_b, invs.at[cells_a:], sem.at[7]),
     ]
-    for copy in copies:
+    for copy in early + copies:
         copy.start()
     mean_ref[...] = jnp.full((HID, LANES), 1.0 / HID, BF)
     fill_taps(taps.at[0], kernel_ref, 1, False)
     fill_taps(taps.at[1], kernel_ref, 1, True)
     fill_taps(taps.at[2], kernel_ref, 0, True)
+    for copy in early:
+        copy.wait()
+    last = HIGH1 // R - 1
 
     @pl.loop(0, HIGH1 // R)
     def _(i):
-        rows = [hidden_ref[i * R + a] for a in range(R + 2)]
+        for edge, ref in ((0, above_ref), (last, below_ref)):
+
+            @pl.when(i == edge)
+            def _():
+                for r in range(R):
+                    for half in range(2):
+                        lanes = slice(half * LANES, (half + 1) * LANES)
+                        natural[2 * r + half] = ref[r, :, lanes].astype(F32)
+
+        @pl.when(jnp.logical_and(i > 0, i < last))
+        def _():
+            for r in range(R):
+                for half in range(2):
+                    lanes = slice(half * LANES, (half + 1) * LANES)
+                    place = natural.at[2 * r + half]
+                    row = (i - 1) * R + r
+                    place[0:SIDE, :] = left_ref[row, :, lanes].astype(F32)
+                    place[SIDE : SIDE + LON, :] = main_ref[row, :, lanes]
+                    place[SIDE + LON : WIDE, :] = right_ref[row, :, lanes].astype(F32)
+
+        rows = [hidden[i * R + a] for a in range(R + 2)]
         inv, hat = normalize(flat(convolve(rows, taps_of(taps.at[0]))), mean_ref)
         branch = forward(1, hat, gain_ref, up_ref, down_ref, act, slope)
         final = (flat(rows[1:-1]).astype(F32) + branch).astype(BF)
         model = jnp.dot(final, dec_ref[...], preferred_element_type=F32)
-        fields = []
-        for r in range(R):
-            pair = []
-            for half in range(2):
-                lanes = slice(half * LANES, (half + 1) * LANES)
-                place = natural.at[2 * r + half]
-                place[0:SIDE, :] = left_ref[i * R + r, :, lanes]
-                place[SIDE : SIDE + LON, :] = main_ref[i * R + r, :, lanes]
-                place[SIDE + LON : WIDE, :] = right_ref[i * R + r, :, lanes]
-                pair.append(from_natural(place))
-            fields.append((pair[1], pair[0]))
-        counts = jnp.concatenate([f[0] for f in fields], axis=0)
-        sums = jnp.concatenate([f[1] for f in fields], axis=0)
+        sums = jnp.concatenate([from_natural(natural.at[2 * r]) for r in range(R)], axis=0)
+        counts = jnp.concatenate([from_natural(natural.at[2 * r + 1]) for r in range(R)], axis=0)
         adj = (counts[:, :levels] * model - sums[:, :levels]).astype(BF)
         for r in range(R):
             adjoint[i * R + r] = adj[r * WIDE : (r + 1) * WIDE]
@@ -288,25 +313,66 @@
         out_ref[:, half * LANES : (half + 1) * LANES] = gathered[half]
 
 
-def place_observations(levels, table_ref, out_ref, hot_ref, row_ref, value_ref):
-    @pl.when(pl.program_id(0) == 0)
-    def _():
-        table = table_ref[...]
-        flipped = jnp.transpose(table.astype(F32))
-        slots = flipped.shape[1]
-        column = flipped[levels + 1 : levels + 2, :]
-        iota = lax.broadcasted_iota(jnp.int32, (LON, slots), 0).astype(F32)
-        hot_ref[...] = jnp.where(iota == column, 1.0, 0.0).astype(BF)
-        row_ref[...] = jnp.broadcast_to(flipped[levels : levels + 1, :], (16, slots))
-        depth = table[:, levels + 2 : levels + 3].astype(F32)
-        lane = lax.broadcasted_iota(jnp.int32, table.shape, 1)
-        mask = jnp.where(lane.astype(F32) < depth, 1.0, 0.0)
-        value_ref[:, :LANES] = (table.astype(F32) * mask).astype(BF)
-        value_ref[:, LANES:] = mask.astype(BF)
-
-    here = pl.program_id(0).astype(F32)
-    keep = jnp.where(row_ref[0:1, :] == here, 1.0, 0.0).astype(BF)
-    out_ref[0] = jnp.dot(hot_ref[...] * keep, value_ref[...], preferred_element_type=F32)
+def pack_observations(value_ref, cell_ref, depth_ref, out_ref, flipped, spread):
+    used = value_ref.shape[0]
+    slots = cell_ref.shape[0]
+    cells = cell_ref[...]
+    row = lax.shift_right_logical(cells, LON.bit_length() - 1)
+    flipped[:used] = value_ref[...]
+    flipped[used : used + slots] = row.astype(F32)
+    flipped[used + slots : used + 2 * slots] = (cells - row * LON).astype(F32)
+    flipped[used + 2 * slots : used + 3 * slots] = depth_ref[...].astype(F32)
+    flipped[used + 3 * slots :] = jnp.zeros_like(flipped[used + 3 * slots :])
+    for k in range(8):
+        block = jnp.transpose(flipped[k * LANES : (k + 1) * LANES, :])
+        spread[pl.ds(k, LANES, stride=8), :] = block
+    out_ref[...] = spread[...].reshape(LANES, 8, LANES).astype(BF)
+
+
+def place_observations(
+    slots, levels, table_ref,
+    field_ref, top_ref, bottom_ref, left_ref, right_ref,
+    spread, wide, hot, row_ref, values,
+):
+    spread[...] = table_ref[...].astype(F32).reshape(LANES * 8, LANES)
+    for k in range(8):
+        wide[:, k * LANES : (k + 1) * LANES] = spread[pl.ds(k, LANES, stride=8), :]
+    used = slots * levels
+    base = used // LANES * LANES
+    tags = jnp.transpose(wide[:, base : base + LANES])
+    lane = lax.broadcasted_iota(jnp.int32, (LANES, levels), 1).astype(F32)
+    column = lax.broadcasted_iota(jnp.int32, (LON, LANES), 0).astype(F32)
+    at = used - base
+    values[...] = jnp.zeros_like(values)
+    for q in range(slots):
+        part = slice(q * LANES, (q + 1) * LANES)
+        depth = wide[:, used + 2 * slots + q : used + 2 * slots + q + 1]
+        mask = jnp.where(lane < depth, 1.0, 0.0)
+        values[part, :levels] = (wide[:, q * levels : (q + 1) * levels] * mask).astype(BF)
+        values[part, LANES : LANES + levels] = mask.astype(BF)
+        row_ref[0:1, part] = tags[at + q : at + q + 1, :]
+        where = tags[at + slots + q : at + slots + q + 1, :]
+        hot[:, part] = jnp.where(column == where, 1.0, 0.0).astype(BF)
+
+    group = 4
+
+    @pl.loop(0, LAT // group)
+    def _(i):
+        here = [
+            jnp.where(row_ref[0:1, :] == (i * group + r).astype(F32), 1.0, 0.0).astype(BF)
+            for r in range(group)
+        ]
+        left = jnp.concatenate([hot[...] * keep for keep in here], axis=0)
+        total = jnp.dot(left, values[...], preferred_element_type=F32)
+        for r in range(group):
+            row = total[r * LON : (r + 1) * LON]
+            field_ref[i * group + r] = row
+            left_ref[i * group + r] = row[:SIDE].astype(BF)
+            right_ref[i * group + r] = row[LON - SIDE :].astype(BF)
+
+    for r in range(R):
+        top_ref[r] = field_ref[r].astype(BF)
+        bottom_ref[r] = field_ref[LAT - R + r].astype(BF)
 
 
 def pair_shift(low, high, axis, wrap):
@@ -318,16 +384,6 @@
 
 def kernel_params(limit):
     return pltpu.CompilerParams(vmem_limit_bytes=limit * 1024 * 1024)
-
-
-def params():
-    return pltpu.CompilerParams(
-        dimension_semantics=("arbitrary",), vmem_limit_bytes=32 * 1024 * 1024
-    )
-
-
-def whole(shape):
-    return pl.BlockSpec(shape, lambda *_: (0,) * len(shape))
 
 
 def body(
@@ -338,13 +394,24 @@
     levels = dec_weight.shape[1]
     owners, slots = obs_cells.shape[1:]
 
-    cells = obs_cells[0]
-    tags = jnp.stack([cells // LON, cells % LON, obs_depth[0]], axis=-1).astype(BF)
-    packed = jnp.concatenate([obs_values[0].astype(BF), tags], axis=-1)
-    packed = jnp.pad(packed, ((0, 0), (0, 16 - slots), (0, LANES - levels - 3)))
+    edges = lax.optimization_barrier((state[:, :HALO], state[:, LAT - HALO :], obs_cells))
+    top, bottom = pair_shift(edges[0], edges[1], "lat", False)
+
+    packed = pl.pallas_call(
+        pack_observations,
+        out_shape=sds((owners, 8, LANES), BF),
+        in_specs=[vmem()] * 3,
+        out_specs=vmem(),
+        scratch_shapes=[pltpu.VMEM((8 * LANES, LANES), F32)] * 2,
+        compiler_params=kernel_params(16),
+        name="pack_observations",
+    )(
+        obs_values[0].transpose(1, 2, 0).reshape(slots * levels, owners),
+        edges[2][0].T,
+        obs_depth[0].T,
+    )
     table = lax.all_to_all(packed, ("lat", "lon"), split_axis=0, concat_axis=0, tiled=True)
 
-    top, bottom = pair_shift(state[:, :HALO], state[:, LAT - HALO :], "lat", False)
     tall = jnp.concatenate([top, state, bottom], axis=1)
     main = lax.dot_general(
         tall, enc_weight, (((0,), (0,)), ((), ())), preferred_element_type=F32
@@ -352,62 +419,81 @@
     left, right = pair_shift(main[:, :SIDE], main[:, LON - SIDE :], "lon", True)
 
     mlp = 2 * WIDE * HID * EXP * 2
-    hidden, tape, hat, inv = pl.pallas_call(
-        forward_kernel,
+
+    def forward_zero(first, count, left, main, right):
+        cells = min(count, HIGH0 - R - first, first + count - R) * WIDE
+        return pl.pallas_call(
+            functools.partial(forward_kernel, first, count),
+            out_shape=[
+                sds((count, COLS, SUBL, HID), BF),
+                sds((cells, EXP), BF),
+                sds((cells, HID), BF),
+                sds((cells, LANES), F32),
+            ],
+            in_specs=[vmem()] * 7,
+            out_specs=[vmem()] + [anywhere()] * 3,
+            scratch_shapes=[
+                pltpu.VMEM((count + 2, COLS, SUBL, HID), BF),
+                pltpu.VMEM((2, WIDE, LANES), F32),
+                pltpu.VMEM((9, SUBL, HID), BF),
+                pltpu.VMEM((HID, LANES), BF),
+                pltpu.VMEM((M, EXP), BF),
+                pltpu.VMEM((3, M, EXP), BF),
+                pltpu.VMEM((3, M, HID), BF),
+                pltpu.VMEM((3, M, LANES), F32),
+                pltpu.SemaphoreType.DMA((3, 3)),
+            ],
+            compiler_params=kernel_params(24),
+            cost_estimate=pl.CostEstimate(
+                flops=mlp * count * 3, bytes_accessed=cells * EXP * 2, transcendentals=0
+            ),
+            name="forward_zero",
+        )(left, main, right, kernels, gains, up_weight, down_weight)
+
+    field, f_top, f_bottom, f_left, f_right = pl.pallas_call(
+        functools.partial(place_observations, slots, levels),
         out_shape=[
-            sds((HIGH0, COLS, SUBL, HID), BF),
-            sds((TAPE, EXP), BF),
-            sds((TAPE, HID), BF),
-            sds((TAPE, LANES), F32),
+            sds((LAT, LON, 2 * LANES), F32),
+            sds((R, LON, 2 * LANES), BF),
+            sds((R, LON, 2 * LANES), BF),
+            sds((LAT, SIDE, 2 * LANES), BF),
+            sds((LAT, SIDE, 2 * LANES), BF),
         ],
-        in_specs=[vmem()] * 7,
-        out_specs=[vmem()] + [anywhere()] * 3,
+        in_specs=[vmem()],
+        out_specs=[vmem()] * 5,
         scratch_shapes=[
-            pltpu.VMEM((LAT + 2 * HALO, COLS, SUBL, HID), BF),
-            pltpu.VMEM((2, WIDE, LANES), F32),
-            pltpu.VMEM((9, SUBL, HID), BF),
-            pltpu.VMEM((HID, LANES), BF),
-            pltpu.VMEM((M, EXP), BF),
-            pltpu.VMEM((3, M, EXP), BF),
-            pltpu.VMEM((3, M, HID), BF),
-            pltpu.VMEM((3, M, LANES), F32),
-            pltpu.SemaphoreType.DMA((3, 3)),
+            pltpu.VMEM((8 * LANES, LANES), F32),
+            pltpu.VMEM((LANES, 8 * LANES), F32),
+            pltpu.VMEM((LON, slots * LANES), BF),
+            pltpu.VMEM((8, slots * LANES), F32),
+            pltpu.VMEM((slots * LANES, 2 * LANES), BF),
         ],
-        compiler_params=kernel_params(40),
+        compiler_params=kernel_params(24),
         cost_estimate=pl.CostEstimate(
-            flops=mlp * HIGH0, bytes_accessed=TAPE * EXP * 2, transcendentals=0
-        ),
-        name="forward_zero",
-    )(left, main, right, kernels, gains, up_weight, down_weight)
-
-    table = table.reshape(owners * 16, LANES)
-    field = pl.pallas_call(
-        functools.partial(place_observations, levels),
-        out_shape=sds((LAT, LON, 2 * LANES), F32),
-        grid=(LAT,),
-        in_specs=[whole(table.shape)],
-        out_specs=pl.BlockSpec((1, LON, 2 * LANES), lambda s: (s, 0, 0)),
-        scratch_shapes=[
-            pltpu.VMEM((LON, owners * 16), BF),
-            pltpu.VMEM((16, owners * 16), F32),
-            pltpu.VMEM((owners * 16, 2 * LANES), BF),
-        ],
-        compiler_params=params(),
-        cost_estimate=pl.CostEstimate(
-            flops=2 * LAT * LON * owners * 16 * 256, bytes_accessed=2**22, transcendentals=0
+            flops=2 * LAT * LON * slots * LANES * 256, bytes_accessed=2**22, transcendentals=0
         ),
         name="place_observations",
     )(table)
-    f_top, f_bottom = pair_shift(field[:2], field[LAT - 2 :], "lat", False)
-    field = jnp.concatenate([f_top, field, f_bottom], axis=0)
-    f_left, f_right = pair_shift(field[:, :SIDE], field[:, LON - SIDE :], "lon", True)
+
+    west, east = pair_shift(f_left, f_right, "lon", True)
+    first_rows = 12
+    main, f_left = lax.optimization_barrier((main, f_left))
+    part_a = forward_zero(0, first_rows, left, main, right)
+    west, east, main, hidden_a = lax.optimization_barrier((west, east, main, part_a[0]))
+    part_a = [hidden_a] + list(part_a[1:])
+    low = jnp.concatenate([west[:R], f_top, east[:R]], axis=1)
+    high = jnp.concatenate([west[LAT - R :], f_bottom, east[LAT - R :]], axis=1)
+    above, below = pair_shift(low, high, "lat", False)
+    main, low = lax.optimization_barrier((main, low))
+    part_b = forward_zero(first_rows, HIGH0 - first_rows, left, main, right)
 
     gradient = pl.pallas_call(
         functools.partial(main_kernel, levels),
         out_shape=sds((channels * LAT, LON), F32),
-        in_specs=[vmem()] * 10 + [anywhere()] * 3,
+        in_specs=[vmem()] * 11 + [anywhere()] * 8,
         out_specs=vmem(),
         scratch_shapes=[
+            pltpu.VMEM((HIGH0, COLS, SUBL, HID), BF),
             pltpu.VMEM((3, 9, SUBL, HID), BF),
             pltpu.VMEM((HID, LANES), BF),
             pltpu.VMEM((2 * R, WIDE, LANES), F32),
@@ -421,16 +507,16 @@
             pltpu.VMEM((TAPE, HID), BF),
             pltpu.VMEM((TAPE, LANES), F32),
             pltpu.VMEM((2, channels * LAT, LANES), F32),
-            pltpu.SemaphoreType.DMA((3,)),
+            pltpu.SemaphoreType.DMA((8,)),
         ],
-        compiler_params=kernel_params(52),
+        compiler_params=kernel_params(40),
         cost_estimate=pl.CostEstimate(
             flops=mlp * (2 * HIGH1 + HIGH2), bytes_accessed=TAPE * EXP * 2, transcendentals=0
         ),
         name="forward_one_and_adjoint",
     )(
-        hidden, f_left, field, f_right, kernels, gains, up_weight, down_weight, dec_weight,
-        enc_weight, tape, hat, inv,
+        above, below, west, field, east, kernels, gains, up_weight, down_weight, dec_weight,
+        enc_weight, *part_a, *part_b,
     )
     return gradient.reshape(channels, LAT, LON)
 

time: 132 us -> 114 us (0.86)
  waiting for transfers between devices: 25.6 us -> 4.41 us
  other arithmetic: 3.69 us -> 0.04 us
  starting transfers between devices: 27.7 us -> 30.2 us
  Pallas kernels: 65.3 us -> 67 us
    ppermute x8, waiting for transfers between devices: 16.9 us -> 0.02 us  [pair_shift(): return (lax.ppermute(high, axis, up), lax.ppermute(low, axis, down))]
    all_to_all x1, waiting for transfers between devices: 8.63 us -> 4.38 us  [body(): lax.all_to_all(packed, ('lat', 'lon'), split_axis=0, concat_axis=0, tiled...]
    pallas_call x2 -> x4, Pallas kernels: 22.2 us -> 24.4 us  [the longest x2 17.7 us: forward_zero(): pl.pallas_call(functools.partial(forward_kernel, first, count), out_shape...]
    concatenate x2, other arithmetic: 2.19 us -> 0.04 us  [the longest x1 0.02 us: body(): low = jnp.concatenate([west[:R], f_top, east[:R]], axis=1)]
    unnamed x26 -> x30, local copies, waits for them, and re-layouts: 6.46 us -> 8.43 us
    another operation x3 -> x0, other arithmetic: 1.5 us -> none  [the longest x1 0.76 us: body(): jnp.stack([cells // LON, cells % LON, obs_depth[0]], axis=-1).astype(BF)]
    all_to_all x1, starting transfers between devices: 11.5 us -> 13 us  [body(): lax.all_to_all(packed, ('lat', 'lon'), split_axis=0, concat_axis=0, tiled...]
    another operation x3 -> x0, local copies, waits for them, and re-layouts: 1.36 us -> none
  transfers between devices with their start and end apart: 9 -> 9, of which waited for: 3 -> 1; matrix products, arithmetic and copies ran while one was open for 1% -> 4% of each run, Pallas kernels for 17% -> 22%
where the time goes in v1:
time: 114 us; the launch traced here: 113 us
  Pallas kernels  67 us (59%)
  starting transfers between devices  30.2 us (26%)
  local copies, waits for them, and re-layouts  9.17 us (8%)
  waiting for transfers between devices  4.41 us (4%)
  matrix products  2.21 us (2%)
    pallas_call x1, Pallas kernels, body(): pl.pallas_call(functools.partial(main_kernel, levels), out_shape=sds((cha...  42.5 us
    pallas_call x2, Pallas kernels, forward_zero(): pl.pallas_call(functools.partial(forward_kernel, first, count), out_shape...  17.7 us
    ppermute x8, starting transfers between devices, pair_shift(): return (lax.ppermute(high, axis, up), lax.ppermute(low, axis, down))  17.2 us
    all_to_all x1, starting transfers between devices, body(): lax.all_to_all(packed, ('lat', 'lon'), split_axis=0, concat_axis=0, tiled...  13 us
    unnamed x30, local copies, waits for them, and re-layouts  8.43 us
    pallas_call x1, Pallas kernels, body(): pl.pallas_call(functools.partial(place_observations, slots, levels), out_...  5.76 us
    all_to_all x1, waiting for transfers between devices, body(): lax.all_to_all(packed, ('lat', 'lon'), split_axis=0, concat_axis=0, tiled...  4.38 us
  transfers between devices with their start and end apart: 9, of which 1 were waited for; matrix products, arithmetic and copies ran while one was open for 4% of the time, Pallas kernels for 22%

profile of v1, /device:TPU:1, one launch (start us, length us, event | category | flops | bytes accessed | tf_op | source)
XLA Modules:
  0.0 113.4 jit_solution(751864298696135461)
XLA Ops:
  0.0 1.3 %copy.11 = bf16[76,16,256]{2,0,1:T(8,128)(2,1)S(1)} copy(bf16[76,16,256]{2,1,0:T(8,128)(2,1)} %param.10) | data formatting | bytes 1245184 | tf_op args[0]
  1.3 0.0 copy-start.7
  1.4 4.0 %collective-permute-start.2 = (bf16[76,4,256]{2,0,1:T(8,128)(2,1)S(1)}, bf16[76,4,256]{2,0,1:T(8,128)(2,1)S(1)}, u32[]{:S(2)}, u32[]{:S(2)}) collective-permute-start(bf16[76,4,256]{2,0,1:T(8,128)(2,1)S(1)} %get-tuple-element.30), channel_id=1, source_target_pairs={{0,16},{16,32},{32,48},{48,64},{64,80},{80,96},{96,112},{1,17},{17... | collective-permute-start | bytes 466952 | tf_op jit(solution)/shard_map/ppermute | solution.py:382
  5.3 1.3 %collective-permute-start.3 = (bf16[76,4,256]{2,0,1:T(8,128)(2,1)S(1)}, bf16[76,4,256]{2,0,1:T(8,128)(2,1)}, u32[]{:S(2)}, u32[]{:S(2)}) collective-permute-start(bf16[76,4,256]{2,0,1:T(8,128)(2,1)S(1)} %get-tuple-element.31), channel_id=1, source_target_pairs={{16,0},{32,16},{48,32},{64,48},{80,64},{96,80},{112,96},{17,1},{33... | collective-permute-start | bytes 466952 | tf_op jit(solution)/shard_map/ppermute | solution.py:382
  6.6 0.7 copy.26
  7.3 1.1 copy.24
  8.5 0.9 pack_observations.1
  9.4 13.0 %all-to-all-start = ((bf16[128,8,128]{2,1,0:T(8,128)(2,1)}), bf16[128,8,128]{2,1,0:T(8,128)(2,1)S(1)}, u32[]{:S(2)}, u32[]{:S(2)}) async-start(bf16[128,8,128]{2,1,0:T(8,128)(2,1)} %pack_observations.1), calls=%async_computation | async-start | bytes 524288 | tf_op jit(solution)/shard_map/all_to_all | solution.py:413
  22.4 0.1 copy.17.dec_ref
  22.6 0.7 copy-done.8
  23.2 2.2 %convolution_convert_fusion.main_ref = bf16[24,256,256]{2,1,0:T(8,128)(2,1)S(1)} fusion(bf16[76,4,256]{2,0,1:T(8,128)(2,1)} %collective-permute-done.3, bf16[76,16,256]{2,0,1:T(8,128)(2,1)} %copy-done.7, bf16[76,4,256]{2,0,1:T(8,128)(2,1)} %copy-done.8, bf16[76,256]{1,0:T(8,128)(2,1)S(1)} %copy-done), kind=kOutput, calls=%fused_computation | convolution fusion | flops 241582080 | bytes 4118528 | tf_op jit(solution)/shard_map/dot_general | solution.py:416
  25.5 0.7 fusion.7
  26.1 3.1 %collective-permute-start.4 = (bf16[24,8,256]{2,1,0:T(8,128)(2,1)}, bf16[24,8,256]{2,1,0:T(8,128)(2,1)}, u32[]{:S(2)}, u32[]{:S(2)}) collective-permute-start(bf16[24,8,256]{2,1,0:T(8,128)(2,1)} %get-tuple-element.50), channel_id=1, source_target_pairs={{0,1},{1,2},{2,3},{3,4},{4,5},{5,6},{6,7},{7,8},{8,9},{9,10},{10,1... | collective-permute-start | bytes 294920 | tf_op jit(solution)/shard_map/ppermute | solution.py:382
  29.3 4.4 %all-to-all-done.table_ref = bf16[128,8,128]{2,1,0:T(8,128)(2,1)S(1)} async-done(((bf16[128,8,128]{2,1,0:T(8,128)(2,1)}), bf16[128,8,128]{2,1,0:T(8,128)(2,1)S(1)}, u32[]{:S(2)}, u32[]{:S(2)}) %all-to-all-start) | async-done | bytes 262176 | tf_op jit(solution)/shard_map/all_to_all | solution.py:413
  33.7 5.8 %place_observations.1 = (f32[16,256,256]{2,1,0:T(8,128)S(1)}, bf16[2,256,256]{2,1,0:T(8,128)(2,1)S(1)}, bf16[2,256,256]{2,1,0:T(8,128)(2,1)S(1)}, bf16[16,8,256]{2,1,0:T(8,128)(2,1)S(1)}, bf16[16,8,256]{2,1,0:T(8,128)(2,1)S(1)}) custom-call(bf16[128,8,128]{2,1,0:T(8,128)(2,1)S(1)} %all-to-all-done.table_ref), custom_call_target="tpu_custom_call" | custom-call | flops 3221225472 | bytes 4194304 | tf_op jit(solution)/shard_map/place_observations/pallas_call | solution.py:453
  39.4 0.8 collective-permute-start.1
  40.2 2.6 %collective-permute-start = (bf16[16,8,256]{2,1,0:T(8,128)(2,1)S(1)}, bf16[16,8,256]{2,1,0:T(8,128)(2,1)S(1)}, u32[]{:S(2)}, u32[]{:S(2)}) collective-permute-start(bf16[16,8,256]{2,1,0:T(8,128)(2,1)S(1)} %get-tuple-element.28), channel_id=1, source_target_pairs={{0,1},{1,2},{2,3},{3,4},{4,5},{5,6},{6,7},{7,8},{8,9},{9,10},{10,1... | collective-permute-start | bytes 196616 | tf_op jit(solution)/shard_map/ppermute | solution.py:382
  42.8 9.6 %forward_zero.2 = (bf16[12,17,16,256]{3,2,1,0:T(8,128)(2,1)S(1)}, bf16[2720,1024]{1,0:T(8,128)(2,1)S(1)}, bf16[2720,256]{1,0:T(8,128)(2,1)S(1)}, f32[2720,128]{1,0:T(8,128)S(1)}) custom-call(bf16[24,8,256]{2,1,0:T(8,128)(2,1)} %collective-permute-done.4.left_ref, bf16[24,256,256]{2,1,0:T(8,128)(2,1)S(1)} %convolution_convert_fusion.main_ref, ...), custom_call_target="tpu_custom_call" | custom-call | flops 10267656192 | bytes 5570560 | tf_op jit(solution)/shard_map/forward_zero/pallas_call | solution.py:425
  52.4 2.4 %copy-done.6 = bf16[2720,1024]{1,0:T(8,128)(2,1)} copy-done((bf16[2720,1024]{1,0:T(8,128)(2,1)}, bf16[2720,1024]{1,0:T(8,128)(2,1)S(1)}, u32[]{:S(2)}) %copy-start.6) | copy-done | bytes 5570584
  54.9 1.3 %collective-permute-start.7 = (bf16[2,272,256]{2,1,0:T(8,128)(2,1)S(1)}, bf16[2,272,256]{2,1,0:T(8,128)(2,1)S(1)}, u32[]{:S(2)}, u32[]{:S(2)}) collective-permute-start(bf16[2,272,256]{2,1,0:T(8,128)(2,1)S(1)} %pad_maximum_fusion.1), channel_id=1, source_target_pairs={{16,0},{32,16},{48,32},{64,48},{80,64},{96,80},{112,96},{17,1},{33... | collective-permute-start | bytes 835592 | tf_op jit(solution)/shard_map/ppermute | solution.py:382
  56.2 4.2 %collective-permute-start.6 = (bf16[2,272,256]{2,1,0:T(8,128)(2,1)S(1)}, bf16[2,272,256]{2,1,0:T(8,128)(2,1)S(1)}, u32[]{:S(2)}, u32[]{:S(2)}) collective-permute-start(bf16[2,272,256]{2,1,0:T(8,128)(2,1)S(1)} %pad_maximum_fusion), channel_id=1, source_target_pairs={{0,16},{16,32},{32,48},{48,64},{64,80},{80,96},{96,112},{1,17},{17... | collective-permute-start | bytes 835592 | tf_op jit(solution)/shard_map/ppermute | solution.py:382
  60.4 8.1 %forward_zero.3 = (bf16[10,17,16,256]{3,2,1,0:T(8,128)(2,1)S(1)}, bf16[2176,1024]{1,0:T(8,128)(2,1)S(1)}, bf16[2176,256]{1,0:T(8,128)(2,1)S(1)}, f32[2176,128]{1,0:T(8,128)S(1)}) custom-call(bf16[24,8,256]{2,1,0:T(8,128)(2,1)} %collective-permute-done.4.left_ref, bf16[24,256,256]{2,1,0:T(8,128)(2,1)S(1)} %convolution_convert_fusion.main_ref, ...), custom_call_target="tpu_custom_call" | custom-call | flops 8556380160 | bytes 4456448 | tf_op jit(solution)/shard_map/forward_zero/pallas_call | solution.py:425
  68.6 2.1 %copy-done.5 = bf16[2176,1024]{1,0:T(8,128)(2,1)} copy-done((bf16[2176,1024]{1,0:T(8,128)(2,1)}, bf16[2176,1024]{1,0:T(8,128)(2,1)S(1)}, u32[]{:S(2)}) %copy-start.5) | copy-done | bytes 4456472
  70.7 42.5 %forward_one_and_adjoint.1 = f32[1216,256]{1,0:T(8,128)} custom-call(bf16[2,272,256]{2,1,0:T(8,128)(2,1)S(1)} %collective-permute-done.6.above_ref, bf16[2,272,256]{2,1,0:T(8,128)(2,1)S(1)} %collective-permute-done.7.below_ref, bf16[16,8,256]{2,1,0:T(8,128)(2,1)S(1)} %collective-permute-done.left_ref, f32[16,256,256]{2,1,0:T(8,128)} %copy-done.4, ...), custom_call_target="tpu_custom_call" | custom-call | flops 16542334976 | bytes 10027008 | tf_op jit(solution)/shard_map/forward_one_and_adjoint/pallas_call | solution.py:490
  (36 shorter events, 0.2 us)
Async XLA Ops:
  0.0 8.4 %copy-start.11 = (s32[1,128,12]{1,0,2:T(1,128)S(1)}, s32[1,128,12]{1,0,2:T(1,128)}, u32[]{:S(2)}) copy-start(s32[1,128,12]{1,0,2:T(1,128)} %param.19) | copy-start | bytes 18436
  0.0 22.4 %copy-start.10 = (f32[2,3,3,256]{3,0,2,1:T(2,128)S(1)}, f32[2,3,3,256]{3,0,2,1:T(2,128)}, u32[]{:S(2)}) copy-start(f32[2,3,3,256]{3,0,2,1:T(2,128)} %param.12) | copy-start | bytes 55300
  0.0 22.4 %copy-start.9 = (bf16[256,76]{0,1:T(8,128)(2,1)S(1)}, bf16[256,76]{0,1:T(8,128)(2,1)}, u32[]{:S(2)}) copy-start(bf16[256,76]{0,1:T(8,128)(2,1)} %param.16) | copy-start | bytes 116740
  0.0 23.2 %copy-start = (bf16[76,256]{1,0:T(8,128)(2,1)S(1)}, bf16[76,256]{1,0:T(8,128)(2,1)}, u32[]{:S(2)}) copy-start(bf16[76,256]{1,0:T(8,128)(2,1)} %enc_ref.1) | copy-start | bytes 116740
  1.3 7.1 %copy-start.7 = (bf16[76,16,256]{2,0,1:T(8,128)(2,1)}, bf16[76,16,256]{2,0,1:T(8,128)(2,1)S(1)}, u32[]{:S(2)}) copy-start(bf16[76,16,256]{2,0,1:T(8,128)(2,1)S(1)} %copy.11) | copy-start | bytes 1867780
  1.4 21.2 %collective-permute-start.2 = (bf16[76,4,256]{2,0,1:T(8,128)(2,1)S(1)}, bf16[76,4,256]{2,0,1:T(8,128)(2,1)S(1)}, u32[]{:S(2)}, u32[]{:S(2)}) collective-permute-start(bf16[76,4,256]{2,0,1:T(8,128)(2,1)S(1)} %get-tuple-element.30), channel_id=1, source_target_pairs={{0,16},{16,32},{32,48},{48,64},{64,80},{80,96},{96,112},{1,17},{17... | collective-permute-start | bytes 466952 | tf_op jit(solution)/shard_map/ppermute | solution.py:382
  5.3 17.9 %collective-permute-start.3 = (bf16[76,4,256]{2,0,1:T(8,128)(2,1)S(1)}, bf16[76,4,256]{2,0,1:T(8,128)(2,1)}, u32[]{:S(2)}, u32[]{:S(2)}) collective-permute-start(bf16[76,4,256]{2,0,1:T(8,128)(2,1)S(1)} %get-tuple-element.31), channel_id=1, source_target_pairs={{16,0},{32,16},{48,32},{64,48},{80,64},{96,80},{112,96},{17,1},{33... | collective-permute-start | bytes 466952 | tf_op jit(solution)/shard_map/ppermute | solution.py:382
  9.4 24.3 %all-to-all-start = ((bf16[128,8,128]{2,1,0:T(8,128)(2,1)}), bf16[128,8,128]{2,1,0:T(8,128)(2,1)S(1)}, u32[]{:S(2)}, u32[]{:S(2)}) async-start(bf16[128,8,128]{2,1,0:T(8,128)(2,1)} %pack_observations.1), calls=%async_computation | async-start | bytes 524288 | tf_op jit(solution)/shard_map/all_to_all | solution.py:413
  22.6 0.7 copy-start.8
  26.1 16.6 %collective-permute-start.4 = (bf16[24,8,256]{2,1,0:T(8,128)(2,1)}, bf16[24,8,256]{2,1,0:T(8,128)(2,1)}, u32[]{:S(2)}, u32[]{:S(2)}) collective-permute-start(bf16[24,8,256]{2,1,0:T(8,128)(2,1)} %get-tuple-element.50), channel_id=1, source_target_pairs={{0,1},{1,2},{2,3},{3,4},{4,5},{5,6},{6,7},{7,8},{8,9},{9,10},{10,1... | collective-permute-start | bytes 294920 | tf_op jit(solution)/shard_map/ppermute | solution.py:382
  29.3 13.5 %copy-start.3 = (f32[2,256]{1,0:T(2,128)S(1)}, f32[2,256]{1,0:T(2,128)}, u32[]{:S(2)}) copy-start(f32[2,256]{1,0:T(2,128)} %gain_ref.5) | copy-start | bytes 6148
  29.3 13.5 %collective-permute-start.5 = (bf16[24,8,256]{2,1,0:T(8,128)(2,1)}, bf16[24,8,256]{2,1,0:T(8,128)(2,1)}, u32[]{:S(2)}, u32[]{:S(2)}) collective-permute-start(bf16[24,8,256]{2,1,0:T(8,128)(2,1)} %get-tuple-element.49), channel_id=1, source_target_pairs={{1,0},{2,1},{3,2},{4,3},{5,4},{6,5},{7,6},{8,7},{9,8},{10,9},{11,1... | collective-permute-start | bytes 294920 | tf_op jit(solution)/shard_map/ppermute | solution.py:382
  33.7 9.1 %copy-start.1 = (bf16[2,256,1024]{2,1,0:T(8,128)(2,1)S(1)}, bf16[2,256,1024]{2,1,0:T(8,128)(2,1)}, u32[]{:S(2)}) copy-start(bf16[2,256,1024]{2,1,0:T(8,128)(2,1)} %up_ref.5) | copy-start | bytes 3145732
  33.7 9.1 %copy-start.2 = (bf16[2,1024,256]{2,1,0:T(8,128)(2,1)S(1)}, bf16[2,1024,256]{2,1,0:T(8,128)(2,1)}, u32[]{:S(2)}) copy-start(bf16[2,1024,256]{2,1,0:T(8,128)(2,1)} %down_ref.5) | copy-start | bytes 3145732
  39.4 13.0 %copy-start.4 = (f32[16,256,256]{2,1,0:T(8,128)}, f32[16,256,256]{2,1,0:T(8,128)S(1)}, u32[]{:S(2)}) copy-start(f32[16,256,256]{2,1,0:T(8,128)S(1)} %get-tuple-element.38.main_ref) | copy-start | bytes 12582916
  39.4 15.4 %collective-permute-start.1 = (bf16[16,8,256]{2,1,0:T(8,128)(2,1)S(1)}, bf16[16,8,256]{2,1,0:T(8,128)(2,1)S(1)}, u32[]{:S(2)}, u32[]{:S(2)}) collective-permute-start(bf16[16,8,256]{2,1,0:T(8,128)(2,1)S(1)} %get-tuple-element.29), channel_id=1, source_target_pairs={{1,0},{2,1},{3,2},{4,3},{5,4},{6,5},{7,6},{8,7},{9,8},{10,9},{11,1... | collective-permute-start | bytes 196616 | tf_op jit(solution)/shard_map/ppermute | solution.py:382
  40.2 14.6 %collective-permute-start = (bf16[16,8,256]{2,1,0:T(8,128)(2,1)S(1)}, bf16[16,8,256]{2,1,0:T(8,128)(2,1)S(1)}, u32[]{:S(2)}, u32[]{:S(2)}) collective-permute-start(bf16[16,8,256]{2,1,0:T(8,128)(2,1)S(1)} %get-tuple-element.28), channel_id=1, source_target_pairs={{0,1},{1,2},{2,3},{3,4},{4,5},{5,6},{6,7},{7,8},{8,9},{9,10},{10,1... | collective-permute-start | bytes 196616 | tf_op jit(solution)/shard_map/ppermute | solution.py:382
  52.4 2.4 %copy-start.6 = (bf16[2720,1024]{1,0:T(8,128)(2,1)}, bf16[2720,1024]{1,0:T(8,128)(2,1)S(1)}, u32[]{:S(2)}) copy-start(bf16[2720,1024]{1,0:T(8,128)(2,1)S(1)} %get-tuple-element.40.tape_a) | copy-start | bytes 16711684
  54.9 15.8 %collective-permute-start.7 = (bf16[2,272,256]{2,1,0:T(8,128)(2,1)S(1)}, bf16[2,272,256]{2,1,0:T(8,128)(2,1)S(1)}, u32[]{:S(2)}, u32[]{:S(2)}) collective-permute-start(bf16[2,272,256]{2,1,0:T(8,128)(2,1)S(1)} %pad_maximum_fusion.1), channel_id=1, source_target_pairs={{16,0},{32,16},{48,32},{64,48},{80,64},{96,80},{112,96},{17,1},{33... | collective-permute-start | bytes 835592 | tf_op jit(solution)/shard_map/ppermute | solution.py:382
  56.2 14.5 %collective-permute-start.6 = (bf16[2,272,256]{2,1,0:T(8,128)(2,1)S(1)}, bf16[2,272,256]{2,1,0:T(8,128)(2,1)S(1)}, u32[]{:S(2)}, u32[]{:S(2)}) collective-permute-start(bf16[2,272,256]{2,1,0:T(8,128)(2,1)S(1)} %pad_maximum_fusion), channel_id=1, source_target_pairs={{0,16},{16,32},{32,48},{48,64},{64,80},{80,96},{96,112},{1,17},{17... | collective-permute-start | bytes 835592 | tf_op jit(solution)/shard_map/ppermute | solution.py:382
  68.6 2.1 %copy-start.5 = (bf16[2176,1024]{1,0:T(8,128)(2,1)}, bf16[2176,1024]{1,0:T(8,128)(2,1)S(1)}, u32[]{:S(2)}) copy-start(bf16[2176,1024]{1,0:T(8,128)(2,1)S(1)} %get-tuple-element.46.tape_b) | copy-start | bytes 13369348

commit v2 on v1

--- a/solution.py
+++ b/solution.py
@@ -24,13 +24,17 @@
 SUBL = 16
 COLS = WIDE // SUBL
 HALO = 4
-R = 2
-M = R * WIDE
 CHUNK = 256
 HIGH0 = LAT + 2 * HALO - 2
 HIGH1 = HIGH0 - 2
 HIGH2 = HIGH1 - 2
 TAPE = HIGH2 * WIDE
+MLP = 2 * WIDE * HID * EXP * 2
+RF = 2
+RM = 4
+RB = 6
+RE = 4
+EDGE = 2
 
 
 def sds(shape, dtype):
@@ -133,7 +137,7 @@
 
 
 def store_rows(ref, base, value, first=None):
-    for r in range(R):
+    for r in range(value.shape[0] // WIDE):
         part = value[r * WIDE : (r + 1) * WIDE]
         if first is not None:
             part = part * row_mask(first + r)
@@ -163,12 +167,12 @@
             row = from_natural(natural.at[half]).astype(BF)
             hidden[i, :, :, lanes] = row.reshape(COLS, SUBL, LANES)
 
-    steps = count // R
-    taped = max(1 - first // R, 0)
-    ends = min((HIGH0 - first) // R - 1, steps)
+    steps = count // RF
+    taped = max(1 - first // RF, 0)
+    ends = min((HIGH0 - first) // RF - 1, steps)
 
     def copies(i, slot):
-        at = pl.ds(pl.multiple_of((i - taped) * M, 16), M)
+        at = pl.ds(pl.multiple_of((i - taped) * RF * WIDE, 16), RF * WIDE)
         return [
             pltpu.make_async_copy(slope.at[slot], tape_hbm.at[at], sem.at[slot, 0]),
             pltpu.make_async_copy(hats.at[slot], hat_hbm.at[at], sem.at[slot, 1]),
@@ -184,13 +188,13 @@
             for copy in copies(i - 3, slot):
                 copy.wait()
 
-        rows = [hidden[i * R + a] for a in range(R + 2)]
+        rows = [hidden[i * RF + a] for a in range(RF + 2)]
         inv, hat = normalize(flat(convolve(rows, taps_of(taps))), mean_ref)
         hats[slot] = hat
         invs[slot] = inv
         branch = forward(0, hat, gain_ref, up_ref, down_ref, act, slope.at[slot])
         total = flat(rows[1:-1]).astype(F32) + branch
-        store_rows(out_ref, i * R, total, first + i * R + 1 - HALO)
+        store_rows(out_ref, i * RF, total, first + i * RF + 1 - HALO)
 
         @pl.when(jnp.logical_and(i >= taped, i < ends))
         def _():
@@ -232,69 +236,73 @@
     fill_taps(taps.at[2], kernel_ref, 0, True)
     for copy in early:
         copy.wait()
-    last = HIGH1 // R - 1
-
-    @pl.loop(0, HIGH1 // R)
+    last = HIGH1 // RM - 1
+
+    @pl.loop(0, HIGH1 // RM)
     def _(i):
-        for edge, ref in ((0, above_ref), (last, below_ref)):
-
-            @pl.when(i == edge)
+        for r in range(RM):
+            inner = True
+            for edge, ref, at in ((0, above_ref, r), (last, below_ref, r - RM + EDGE)):
+                if 0 <= at < EDGE:
+                    inner = jnp.logical_and(inner, i != edge)
+
+                    @pl.when(i == edge)
+                    def _():
+                        for half in range(2):
+                            lanes = slice(half * LANES, (half + 1) * LANES)
+                            row = ref[at, :, lanes].astype(F32)
+                            natural[2 * r + half] = row * row_mask(i * RM + r - EDGE)
+
+            @pl.when(inner)
             def _():
-                for r in range(R):
-                    for half in range(2):
-                        lanes = slice(half * LANES, (half + 1) * LANES)
-                        natural[2 * r + half] = ref[r, :, lanes].astype(F32)
-
-        @pl.when(jnp.logical_and(i > 0, i < last))
-        def _():
-            for r in range(R):
+                row = i * RM + r - EDGE
                 for half in range(2):
                     lanes = slice(half * LANES, (half + 1) * LANES)
                     place = natural.at[2 * r + half]
-                    row = (i - 1) * R + r
                     place[0:SIDE, :] = left_ref[row, :, lanes].astype(F32)
                     place[SIDE : SIDE + LON, :] = main_ref[row, :, lanes]
                     place[SIDE + LON : WIDE, :] = right_ref[row, :, lanes].astype(F32)
 
-        rows = [hidden[i * R + a] for a in range(R + 2)]
+        rows = [hidden[i * RM + a] for a in range(RM + 2)]
         inv, hat = normalize(flat(convolve(rows, taps_of(taps.at[0]))), mean_ref)
-        branch = forward(1, hat, gain_ref, up_ref, down_ref, act, slope)
+        branch = forward(1, hat, gain_ref, up_ref, down_ref, act.at[: RM * WIDE], slope)
         final = (flat(rows[1:-1]).astype(F32) + branch).astype(BF)
         model = jnp.dot(final, dec_ref[...], preferred_element_type=F32)
-        sums = jnp.concatenate([from_natural(natural.at[2 * r]) for r in range(R)], axis=0)
-        counts = jnp.concatenate([from_natural(natural.at[2 * r + 1]) for r in range(R)], axis=0)
+        sums = jnp.concatenate([from_natural(natural.at[2 * r]) for r in range(RM)], axis=0)
+        counts = jnp.concatenate([from_natural(natural.at[2 * r + 1]) for r in range(RM)], axis=0)
         adj = (counts[:, :levels] * model - sums[:, :levels]).astype(BF)
-        for r in range(R):
-            adjoint[i * R + r] = adj[r * WIDE : (r + 1) * WIDE]
+        for r in range(RM):
+            adjoint[i * RM + r] = adj[r * WIDE : (r + 1) * WIDE]
         grad_s = times_transposed(adj, dec_ref[...]).astype(BF)
         grad_d = backward(
-            1, grad_s, hat, inv, gain_ref, up_ref, down_ref, act, slope, mean_ref
+            1, grad_s, hat, inv, gain_ref, up_ref, down_ref, act.at[: RM * WIDE], slope, mean_ref
         )
-        store_rows(grad_d1, i * R, grad_d)
+        store_rows(grad_d1, i * RM, grad_d)
 
     for copy in copies:
         copy.wait()
 
-    @pl.loop(0, HIGH2 // R)
+    @pl.loop(0, HIGH2 // RB)
     def _(i):
-        rows = [grad_d1[i * R + a] for a in range(R + 2)]
-        adj = jnp.concatenate([adjoint[i * R + 1 + r] for r in range(R)], axis=0)
+        rows = [grad_d1[i * RB + a] for a in range(RB + 2)]
+        adj = jnp.concatenate([adjoint[i * RB + 1 + r] for r in range(RB)], axis=0)
         grad = times_transposed(adj, dec_ref[...])
         grad = grad + flat(convolve(rows, taps_of(taps.at[1]))).astype(F32)
         grad_s = grad.astype(BF)
-        store_rows(grad1, i * R, grad_s)
-        at = pl.ds(pl.multiple_of(i * M, 16), M)
+        store_rows(grad1, i * RB, grad_s)
+        at = pl.ds(pl.multiple_of(i * RB * WIDE, 16), RB * WIDE)
         grad_d = backward(
-            0, grad_s, hats[at], invs[at], gain_ref, up_ref, down_ref, act, tape.at[at], mean_ref
+            0, grad_s, hats[at], invs[at], gain_ref, up_ref, down_ref, act.at[: RB * WIDE], tape.at[at],
+            mean_ref
         )
-        store_rows(grad_d0, i * R, grad_d, i * R - 1)
-
-    @pl.loop(0, LAT // R)
+        store_rows(grad_d0, i * RB, grad_d, i * RB - 1)
+
+    @pl.loop(0, LAT // RE)
     def _(i):
-        rows = [grad_d0[i * R + a] for a in range(R + 2)]
+        rows = [grad_d0[i * RE + a] for a in range(RE + 2)]
         conv = convolve(rows, taps_of(taps.at[2]))
-        for r in range(R):
-            total = conv[r].astype(F32) + grad1[i * R + 1 + r].astype(F32)
+        for r in range(RE):
+            total = conv[r].astype(F32) + grad1[i * RE + 1 + r].astype(F32)
             halves = []
             for half in range(2):
                 place = natural.at[2 * r + half]
@@ -305,7 +313,7 @@
                 halves.append(place[SIDE : SIDE + LON, :].astype(BF))
             result = times_transposed(enc_ref[...], jnp.concatenate(halves, axis=1))
             for half in range(2):
-                gathered[half, pl.ds(i * R + r, enc_ref.shape[0], stride=LAT), :] = result[
+                gathered[half, pl.ds(i * RE + r, enc_ref.shape[0], stride=LAT), :] = result[
                     :, half * LANES : (half + 1) * LANES
                 ]
 
@@ -370,20 +378,82 @@
             left_ref[i * group + r] = row[:SIDE].astype(BF)
             right_ref[i * group + r] = row[LON - SIDE :].astype(BF)
 
-    for r in range(R):
+    for r in range(EDGE):
         top_ref[r] = field_ref[r].astype(BF)
-        bottom_ref[r] = field_ref[LAT - R + r].astype(BF)
-
-
-def pair_shift(low, high, axis, wrap):
+        bottom_ref[r] = field_ref[LAT - EDGE + r].astype(BF)
+
+
+def pair_shift(low, high, axis):
     peers = lax.axis_size(axis)
-    up = [(i, (i + 1) % peers) for i in range(peers if wrap else peers - 1)]
+    up = [(i, (i + 1) % peers) for i in range(peers)]
     down = [(j, i) for i, j in up]
     return lax.ppermute(high, axis, up), lax.ppermute(low, axis, down)
 
 
 def kernel_params(limit):
     return pltpu.CompilerParams(vmem_limit_bytes=limit * 1024 * 1024)
+
+
+def forward_call(first, count, *operands):
+    cells = min(count, HIGH0 - 2 - first, first + count - 2) * WIDE
+    return pl.pallas_call(
+        functools.partial(forward_kernel, first, count),
+        out_shape=[
+            sds((count, COLS, SUBL, HID), BF),
+            sds((cells, EXP), BF),
+            sds((cells, HID), BF),
+            sds((cells, LANES), F32),
+        ],
+        in_specs=[vmem()] * 7,
+        out_specs=[vmem()] + [anywhere()] * 3,
+        scratch_shapes=[
+            pltpu.VMEM((count + 2, COLS, SUBL, HID), BF),
+            pltpu.VMEM((2, WIDE, LANES), F32),
+            pltpu.VMEM((9, SUBL, HID), BF),
+            pltpu.VMEM((HID, LANES), BF),
+            pltpu.VMEM((RF * WIDE, EXP), BF),
+            pltpu.VMEM((3, RF * WIDE, EXP), BF),
+            pltpu.VMEM((3, RF * WIDE, HID), BF),
+            pltpu.VMEM((3, RF * WIDE, LANES), F32),
+            pltpu.SemaphoreType.DMA((3, 3)),
+        ],
+        compiler_params=kernel_params(62),
+        cost_estimate=pl.CostEstimate(
+            flops=MLP * count * 3, bytes_accessed=cells * EXP * 2, transcendentals=0
+        ),
+        name="forward_zero",
+    )(*operands)
+
+
+def main_call(channels, levels, *operands):
+    return pl.pallas_call(
+        functools.partial(main_kernel, levels),
+        out_shape=sds((channels * LAT, LON), F32),
+        in_specs=[vmem()] * 11 + [anywhere()] * 8,
+        out_specs=vmem(),
+        scratch_shapes=[
+            pltpu.VMEM((HIGH0, COLS, SUBL, HID), BF),
+            pltpu.VMEM((3, 9, SUBL, HID), BF),
+            pltpu.VMEM((HID, LANES), BF),
+            pltpu.VMEM((2 * max(RM, RE), WIDE, LANES), F32),
+            pltpu.VMEM((max(RM, RB) * WIDE, EXP), BF),
+            pltpu.VMEM((RM * WIDE, EXP), BF),
+            pltpu.VMEM((HIGH1, WIDE, levels), BF),
+            pltpu.VMEM((HIGH1, COLS, SUBL, HID), BF),
+            pltpu.VMEM((HIGH2, COLS, SUBL, HID), BF),
+            pltpu.VMEM((HIGH2, COLS, SUBL, HID), BF),
+            pltpu.VMEM((TAPE, EXP), BF),
+            pltpu.VMEM((TAPE, HID), BF),
+            pltpu.VMEM((TAPE, LANES), F32),
+            pltpu.VMEM((2, channels * LAT, LANES), F32),
+            pltpu.SemaphoreType.DMA((8,)),
+        ],
+        compiler_params=kernel_params(48),
+        cost_estimate=pl.CostEstimate(
+            flops=MLP * (2 * HIGH1 + HIGH2), bytes_accessed=TAPE * EXP * 2, transcendentals=0
+        ),
+        name="forward_one_and_adjoint",
+    )(*operands)
 
 
 def body(
@@ -395,7 +465,7 @@
     owners, slots = obs_cells.shape[1:]
 
     edges = lax.optimization_barrier((state[:, :HALO], state[:, LAT - HALO :], obs_cells))
-    top, bottom = pair_shift(edges[0], edges[1], "lat", False)
+    top, bottom = pair_shift(edges[0], edges[1], "lat")
 
     packed = pl.pallas_call(
         pack_observations,
@@ -412,50 +482,21 @@
     )
     table = lax.all_to_all(packed, ("lat", "lon"), split_axis=0, concat_axis=0, tiled=True)
 
+    band = lax.axis_index("lat")
+    top = jnp.where(band > 0, top, 0)
+    bottom = jnp.where(band < lax.axis_size("lat") - 1, bottom, 0)
     tall = jnp.concatenate([top, state, bottom], axis=1)
     main = lax.dot_general(
         tall, enc_weight, (((0,), (0,)), ((), ())), preferred_element_type=F32
     ).astype(BF)
-    left, right = pair_shift(main[:, :SIDE], main[:, LON - SIDE :], "lon", True)
-
-    mlp = 2 * WIDE * HID * EXP * 2
-
-    def forward_zero(first, count, left, main, right):
-        cells = min(count, HIGH0 - R - first, first + count - R) * WIDE
-        return pl.pallas_call(
-            functools.partial(forward_kernel, first, count),
-            out_shape=[
-                sds((count, COLS, SUBL, HID), BF),
-                sds((cells, EXP), BF),
-                sds((cells, HID), BF),
-                sds((cells, LANES), F32),
-            ],
-            in_specs=[vmem()] * 7,
-            out_specs=[vmem()] + [anywhere()] * 3,
-            scratch_shapes=[
-                pltpu.VMEM((count + 2, COLS, SUBL, HID), BF),
-                pltpu.VMEM((2, WIDE, LANES), F32),
-                pltpu.VMEM((9, SUBL, HID), BF),
-                pltpu.VMEM((HID, LANES), BF),
-                pltpu.VMEM((M, EXP), BF),
-                pltpu.VMEM((3, M, EXP), BF),
-                pltpu.VMEM((3, M, HID), BF),
-                pltpu.VMEM((3, M, LANES), F32),
-                pltpu.SemaphoreType.DMA((3, 3)),
-            ],
-            compiler_params=kernel_params(24),
-            cost_estimate=pl.CostEstimate(
-                flops=mlp * count * 3, bytes_accessed=cells * EXP * 2, transcendentals=0
-            ),
-            name="forward_zero",
-        )(left, main, right, kernels, gains, up_weight, down_weight)
+    left, right = pair_shift(main[:, :SIDE], main[:, LON - SIDE :], "lon")
 
     field, f_top, f_bottom, f_left, f_right = pl.pallas_call(
         functools.partial(place_observations, slots, levels),
         out_shape=[
             sds((LAT, LON, 2 * LANES), F32),
-            sds((R, LON, 2 * LANES), BF),
-            sds((R, LON, 2 * LANES), BF),
+            sds((EDGE, LON, 2 * LANES), BF),
+            sds((EDGE, LON, 2 * LANES), BF),
             sds((LAT, SIDE, 2 * LANES), BF),
             sds((LAT, SIDE, 2 * LANES), BF),
         ],
@@ -475,48 +516,25 @@
         name="place_observations",
     )(table)
 
-    west, east = pair_shift(f_left, f_right, "lon", True)
+    west, east = pair_shift(f_left, f_right, "lon")
     first_rows = 12
     main, f_left = lax.optimization_barrier((main, f_left))
-    part_a = forward_zero(0, first_rows, left, main, right)
+    part_a = forward_call(
+        0, first_rows, left, main, right, kernels, gains, up_weight, down_weight
+    )
     west, east, main, hidden_a = lax.optimization_barrier((west, east, main, part_a[0]))
     part_a = [hidden_a] + list(part_a[1:])
-    low = jnp.concatenate([west[:R], f_top, east[:R]], axis=1)
-    high = jnp.concatenate([west[LAT - R :], f_bottom, east[LAT - R :]], axis=1)
-    above, below = pair_shift(low, high, "lat", False)
+    low = jnp.concatenate([west[:EDGE], f_top, east[:EDGE]], axis=1)
+    high = jnp.concatenate([west[LAT - EDGE :], f_bottom, east[LAT - EDGE :]], axis=1)
+    above, below = pair_shift(low, high, "lat")
     main, low = lax.optimization_barrier((main, low))
-    part_b = forward_zero(first_rows, HIGH0 - first_rows, left, main, right)
-
-    gradient = pl.pallas_call(
-        functools.partial(main_kernel, levels),
-        out_shape=sds((channels * LAT, LON), F32),
-        in_specs=[vmem()] * 11 + [anywhere()] * 8,
-        out_specs=vmem(),
-        scratch_shapes=[
-            pltpu.VMEM((HIGH0, COLS, SUBL, HID), BF),
-            pltpu.VMEM((3, 9, SUBL, HID), BF),
-            pltpu.VMEM((HID, LANES), BF),
-            pltpu.VMEM((2 * R, WIDE, LANES), F32),
-            pltpu.VMEM((M, EXP), BF),
-            pltpu.VMEM((M, EXP), BF),
-            pltpu.VMEM((HIGH1, WIDE, levels), BF),
-            pltpu.VMEM((HIGH1, COLS, SUBL, HID), BF),
-            pltpu.VMEM((HIGH2, COLS, SUBL, HID), BF),
-            pltpu.VMEM((HIGH2, COLS, SUBL, HID), BF),
-            pltpu.VMEM((TAPE, EXP), BF),
-            pltpu.VMEM((TAPE, HID), BF),
-            pltpu.VMEM((TAPE, LANES), F32),
-            pltpu.VMEM((2, channels * LAT, LANES), F32),
-            pltpu.SemaphoreType.DMA((8,)),
-        ],
-        compiler_params=kernel_params(40),
-        cost_estimate=pl.CostEstimate(
-            flops=mlp * (2 * HIGH1 + HIGH2), bytes_accessed=TAPE * EXP * 2, transcendentals=0
-        ),
-        name="forward_one_and_adjoint",
-    )(
-        above, below, west, field, east, kernels, gains, up_weight, down_weight, dec_weight,
-        enc_weight, *part_a, *part_b,
+    part_b = forward_call(
+        first_rows, HIGH0 - first_rows, left, main, right, kernels, gains, up_weight, down_weight
+    )
+
+    gradient = main_call(
+        channels, levels, above, below, west, field, east, kernels, gains, up_weight,
+        down_weight, dec_weight, enc_weight, *part_a, *part_b,
     )
     return gradient.reshape(channels, LAT, LON)
 

time: 114 us -> 112 us (0.982)
  starting transfers between devices: 30.2 us -> 23.2 us
  waiting for transfers between devices: 4.41 us -> 7.59 us
  local copies, waits for them, and re-layouts: 9.17 us -> 10.9 us
  other arithmetic: 0.04 us -> 1.55 us
  matrix products: 2.21 us -> 1.01 us
    ppermute x8, starting transfers between devices: 17.2 us -> 12.5 us  [pair_shift(): return (lax.ppermute(high, axis, up), lax.ppermute(low, axis, down))]
    unnamed x30 -> x34, local copies, waits for them, and re-layouts: 8.43 us -> 10.9 us
    all_to_all x1, starting transfers between devices: 13 us -> 10.7 us  [body(): lax.all_to_all(packed, ('lat', 'lon'), split_axis=0, concat_axis=0, tiled...]
    all_to_all x1, waiting for transfers between devices: 4.38 us -> 6.16 us  [body(): lax.all_to_all(packed, ('lat', 'lon'), split_axis=0, concat_axis=0, tiled...]
    concatenate x2, other arithmetic: 0.04 us -> 1.51 us  [the longest x1 0.76 us: body(): low = jnp.concatenate([west[:EDGE], f_top, east[:EDGE]], axis=1)]
    ppermute x8, waiting for transfers between devices: 0.02 us -> 1.43 us  [pair_shift(): return (lax.ppermute(high, axis, up), lax.ppermute(low, axis, down))]
    dot_general x1, matrix products: 2.21 us -> 1.01 us  [body(): lax.dot_general(tall, enc_weight, (((0,), (0,)), ((), ())), preferred_ele...]
  transfers between devices with their start and end apart: 9 -> 9, of which waited for: 1 -> 2; matrix products, arithmetic and copies ran while one was open for 4% -> 4% of each run, Pallas kernels for 22% -> 26%
where the time goes in v2:
time: 112 us
  Pallas kernels  67.4 us (60%)
  starting transfers between devices  23.2 us (21%)
  local copies, waits for them, and re-layouts  10.9 us (10%)
  waiting for transfers between devices  7.59 us (7%)
  other arithmetic  1.55 us (1%)
    pallas_call x1, Pallas kernels, main_call(): pl.pallas_call(functools.partial(main_kernel, levels), out_shape=sds((cha...  38.5 us
    pallas_call x2, Pallas kernels, forward_call(): pl.pallas_call(functools.partial(forward_kernel, first, count), out_shape...  22.3 us
    ppermute x8, starting transfers between devices, pair_shift(): return (lax.ppermute(high, axis, up), lax.ppermute(low, axis, down))  12.5 us
    unnamed x34, local copies, waits for them, and re-layouts  10.9 us
    all_to_all x1, starting transfers between devices, body(): lax.all_to_all(packed, ('lat', 'lon'), split_axis=0, concat_axis=0, tiled...  10.7 us
    all_to_all x1, waiting for transfers between devices, body(): lax.all_to_all(packed, ('lat', 'lon'), split_axis=0, concat_axis=0, tiled...  6.16 us
    pallas_call x1, Pallas kernels, body(): pl.pallas_call(functools.partial(place_observations, slots, levels), out_...  5.75 us
  transfers between devices with their start and end apart: 9, of which 2 were waited for; matrix products, arithmetic and copies ran while one was open for 4% of the time, Pallas kernels for 26%

profile of v2, /device:TPU:1, one launch (start us, length us, event | category | flops | bytes accessed | tf_op | source)
XLA Modules:
  0.0 112.1 jit_solution(16779131832332737291)
XLA Ops:
  0.0 1.3 %copy.11 = bf16[76,16,256]{2,0,1:T(8,128)(2,1)S(1)} copy(bf16[76,16,256]{2,1,0:T(8,128)(2,1)} %param.10) | data formatting | bytes 1245184 | tf_op args[0]
  1.4 4.6 %collective-permute-start.3 = (bf16[76,4,256]{2,0,1:T(8,128)(2,1)S(1)}, bf16[76,4,256]{2,0,1:T(8,128)(2,1)S(1)}, u32[]{:S(2)}, u32[]{:S(2)}) collective-permute-start(bf16[76,4,256]{2,0,1:T(8,128)(2,1)S(1)} %get-tuple-element.31), channel_id=1, source_target_pairs={{16,0},{32,16},{48,32},{64,48},{80,64},{96,80},{112,96},{0,112},{1... | collective-permute-start | bytes 466952 | tf_op jit(solution)/shard_map/ppermute | solution.py:390
  5.9 0.7 copy.26
  6.6 1.1 copy.24
  7.7 0.9 pack_observations.1
  8.7 10.7 %all-to-all-start = ((bf16[128,8,128]{2,1,0:T(8,128)(2,1)}), bf16[128,8,128]{2,1,0:T(8,128)(2,1)S(1)}, u32[]{:S(2)}, u32[]{:S(2)}) async-start(bf16[128,8,128]{2,1,0:T(8,128)(2,1)} %pack_observations.1), calls=%async_computation | async-start | bytes 524288 | tf_op jit(solution)/shard_map/all_to_all | solution.py:483
  20.2 1.0 convolution_convert_fusion.main_ref
  21.3 3.2 %collective-permute-start.4 = (bf16[24,8,256]{2,1,0:T(8,128)(2,1)S(1)}, bf16[24,8,256]{2,1,0:T(8,128)(2,1)S(1)}, u32[]{:S(2)}, u32[]{:S(2)}) collective-permute-start(bf16[24,8,256]{2,1,0:T(8,128)(2,1)S(1)} %get-tuple-element.50), channel_id=1, source_target_pairs={{0,1},{1,2},{2,3},{3,4},{4,5},{5,6},{6,7},{7,8},{8,9},{9,10},{10,1... | collective-permute-start | bytes 294920 | tf_op jit(solution)/shard_map/ppermute | solution.py:390
  24.5 6.2 %all-to-all-done.table_ref = bf16[128,8,128]{2,1,0:T(8,128)(2,1)S(1)} async-done(((bf16[128,8,128]{2,1,0:T(8,128)(2,1)}), bf16[128,8,128]{2,1,0:T(8,128)(2,1)S(1)}, u32[]{:S(2)}, u32[]{:S(2)}) %all-to-all-start) | async-done | bytes 262176 | tf_op jit(solution)/shard_map/all_to_all | solution.py:483
  30.6 5.8 %place_observations.1 = (f32[16,256,256]{2,1,0:T(8,128)S(1)}, bf16[2,256,256]{2,1,0:T(8,128)(2,1)S(1)}, bf16[2,256,256]{2,1,0:T(8,128)(2,1)S(1)}, bf16[16,8,256]{2,1,0:T(8,128)(2,1)S(1)}, bf16[16,8,256]{2,1,0:T(8,128)(2,1)S(1)}) custom-call(bf16[128,8,128]{2,1,0:T(8,128)(2,1)S(1)} %all-to-all-done.table_ref), custom_call_target="tpu_custom_call" | custom-call | flops 3221225472 | bytes 4194304 | tf_op jit(solution)/shard_map/place_observations/pallas_call | solution.py:494
  36.4 2.1 %copy-done.5 = f32[16,256,256]{2,1,0:T(8,128)} copy-done((f32[16,256,256]{2,1,0:T(8,128)}, f32[16,256,256]{2,1,0:T(8,128)S(1)}, u32[]{:S(2)}) %copy-start.5) | copy-done | bytes 4194328
  38.5 0.7 collective-permute-start.1
  39.2 2.5 %collective-permute-start = (bf16[16,8,256]{2,1,0:T(8,128)(2,1)S(1)}, bf16[16,8,256]{2,1,0:T(8,128)(2,1)S(1)}, u32[]{:S(2)}, u32[]{:S(2)}) collective-permute-start(bf16[16,8,256]{2,1,0:T(8,128)(2,1)S(1)} %get-tuple-element.28), channel_id=1, source_target_pairs={{0,1},{1,2},{2,3},{3,4},{4,5},{5,6},{6,7},{7,8},{8,9},{9,10},{10,1... | collective-permute-start | bytes 196616 | tf_op jit(solution)/shard_map/ppermute | solution.py:390
  42.4 0.6 copy-done.13
  43.0 12.3 %forward_zero.2 = (bf16[12,17,16,256]{3,2,1,0:T(8,128)(2,1)}, bf16[2720,1024]{1,0:T(8,128)(2,1)}, bf16[2720,256]{1,0:T(8,128)(2,1)}, f32[2720,128]{1,0:T(8,128)}) custom-call(bf16[24,8,256]{2,1,0:T(8,128)(2,1)} %copy-done.12, bf16[24,256,256]{2,1,0:T(8,128)(2,1)} %copy-done.8, bf16[24,8,256]{2,1,0:T(8,128)(2,1)} %copy-done.13, ...), custom_call_target="tpu_custom_call" | custom-call | flops 10267656192 | bytes 5570560 | tf_op jit(solution)/shard_map/forward_zero/pallas_call | solution.py:399
  55.4 0.8 pad_maximum_fusion.1
  56.1 0.8 collective-permute-start.7
  57.0 0.7 pad_maximum_fusion
  58.3 10.0 %forward_zero.3 = (bf16[10,17,16,256]{3,2,1,0:T(8,128)(2,1)}, bf16[2176,1024]{1,0:T(8,128)(2,1)}, bf16[2176,256]{1,0:T(8,128)(2,1)}, f32[2176,128]{1,0:T(8,128)}) custom-call(bf16[24,8,256]{2,1,0:T(8,128)(2,1)} %copy-done.12, bf16[24,256,256]{2,1,0:T(8,128)(2,1)} %copy-done.8, bf16[24,8,256]{2,1,0:T(8,128)(2,1)} %copy-done.13, ...), custom_call_target="tpu_custom_call" | custom-call | flops 8556380160 | bytes 4456448 | tf_op jit(solution)/shard_map/forward_zero/pallas_call | solution.py:399
  68.3 1.4 %collective-permute-done.6.above_ref = bf16[2,272,256]{2,1,0:T(8,128)(2,1)S(1)} collective-permute-done((bf16[2,272,256]{2,1,0:T(8,128)(2,1)}, bf16[2,272,256]{2,1,0:T(8,128)(2,1)S(1)}, u32[]{:S(2)}, u32[]{:S(2)}) %collective-permute-start.6) | collective-permute-done | bytes 278560 | tf_op jit(solution)/shard_map/ppermute | solution.py:390
  69.8 1.2 %copy-done.3 = bf16[2,1024,256]{2,1,0:T(8,128)(2,1)S(1)} copy-done((bf16[2,1024,256]{2,1,0:T(8,128)(2,1)S(1)}, bf16[2,1024,256]{2,1,0:T(8,128)(2,1)}, u32[]{:S(2)}) %copy-start.3) | copy-done | bytes 1048600
  71.0 1.2 %copy-done.6 = bf16[2176,256]{1,0:T(8,128)(2,1)S(1)} copy-done((bf16[2176,256]{1,0:T(8,128)(2,1)S(1)}, bf16[2176,256]{1,0:T(8,128)(2,1)}, u32[]{:S(2)}) %copy-start.6) | copy-done | bytes 1114136
  72.2 1.2 %copy-done.7 = f32[2176,128]{1,0:T(8,128)S(1)} copy-done((f32[2176,128]{1,0:T(8,128)S(1)}, f32[2176,128]{1,0:T(8,128)}, u32[]{:S(2)}) %copy-start.7) | copy-done | bytes 1114136
  73.5 38.5 %forward_one_and_adjoint.1 = f32[1216,256]{1,0:T(8,128)} custom-call(bf16[2,272,256]{2,1,0:T(8,128)(2,1)S(1)} %collective-permute-done.6.above_ref, bf16[2,272,256]{2,1,0:T(8,128)(2,1)} %collective-permute-done.7.below_ref, bf16[16,8,256]{2,1,0:T(8,128)(2,1)S(1)} %collective-permute-done.left_ref, f32[16,256,256]{2,1,0:T(8,128)} %copy-done.5, ...), custom_call_target="tpu_custom_call" | custom-call | flops 16542334976 | bytes 10027008 | tf_op jit(solution)/shard_map/forward_one_and_adjoint/pallas_call | solution.py:429
  (42 shorter events, 2.2 us)
Async XLA Ops:
  0.0 7.7 %copy-start.11 = (s32[1,128,12]{1,0,2:T(1,128)S(1)}, s32[1,128,12]{1,0,2:T(1,128)}, u32[]{:S(2)}) copy-start(s32[1,128,12]{1,0,2:T(1,128)} %param.19) | copy-start | bytes 18436
  0.0 19.4 %copy-start.10 = (f32[2,3,3,256]{3,0,2,1:T(2,128)S(1)}, f32[2,3,3,256]{3,0,2,1:T(2,128)}, u32[]{:S(2)}) copy-start(f32[2,3,3,256]{3,0,2,1:T(2,128)} %param.12) | copy-start | bytes 55300
  0.0 20.0 %copy-start.9 = (bf16[256,76]{0,1:T(8,128)(2,1)S(1)}, bf16[256,76]{0,1:T(8,128)(2,1)}, u32[]{:S(2)}) copy-start(bf16[256,76]{0,1:T(8,128)(2,1)} %param.16) | copy-start | bytes 116740
  0.0 20.2 %copy-start = (bf16[76,256]{1,0:T(8,128)(2,1)S(1)}, bf16[76,256]{1,0:T(8,128)(2,1)}, u32[]{:S(2)}) copy-start(bf16[76,256]{1,0:T(8,128)(2,1)} %enc_ref.1) | copy-start | bytes 116740
  1.4 18.8 %collective-permute-start.3 = (bf16[76,4,256]{2,0,1:T(8,128)(2,1)S(1)}, bf16[76,4,256]{2,0,1:T(8,128)(2,1)S(1)}, u32[]{:S(2)}, u32[]{:S(2)}) collective-permute-start(bf16[76,4,256]{2,0,1:T(8,128)(2,1)S(1)} %get-tuple-element.31), channel_id=1, source_target_pairs={{16,0},{32,16},{48,32},{64,48},{80,64},{96,80},{112,96},{0,112},{1... | collective-permute-start | bytes 466952 | tf_op jit(solution)/shard_map/ppermute | solution.py:390
  5.9 14.2 %collective-permute-start.2 = (bf16[76,4,256]{2,0,1:T(8,128)(2,1)S(1)}, bf16[76,4,256]{2,0,1:T(8,128)(2,1)S(1)}, u32[]{:S(2)}, u32[]{:S(2)}) collective-permute-start(bf16[76,4,256]{2,0,1:T(8,128)(2,1)S(1)} %get-tuple-element.30), channel_id=1, source_target_pairs={{0,16},{16,32},{32,48},{48,64},{64,80},{80,96},{96,112},{112,0},{1... | collective-permute-start | bytes 466952 | tf_op jit(solution)/shard_map/ppermute | solution.py:390
  8.7 22.0 %all-to-all-start = ((bf16[128,8,128]{2,1,0:T(8,128)(2,1)}), bf16[128,8,128]{2,1,0:T(8,128)(2,1)S(1)}, u32[]{:S(2)}, u32[]{:S(2)}) async-start(bf16[128,8,128]{2,1,0:T(8,128)(2,1)} %pack_observations.1), calls=%async_computation | async-start | bytes 524288 | tf_op jit(solution)/shard_map/all_to_all | solution.py:483
  21.2 3.2 %copy-start.8 = (bf16[24,256,256]{2,1,0:T(8,128)(2,1)}, bf16[24,256,256]{2,1,0:T(8,128)(2,1)S(1)}, u32[]{:S(2)}) copy-start(bf16[24,256,256]{2,1,0:T(8,128)(2,1)S(1)} %convolution_convert_fusion.main_ref) | copy-start | bytes 9437188
  21.3 20.5 %collective-permute-start.4 = (bf16[24,8,256]{2,1,0:T(8,128)(2,1)S(1)}, bf16[24,8,256]{2,1,0:T(8,128)(2,1)S(1)}, u32[]{:S(2)}, u32[]{:S(2)}) collective-permute-start(bf16[24,8,256]{2,1,0:T(8,128)(2,1)S(1)} %get-tuple-element.50), channel_id=1, source_target_pairs={{0,1},{1,2},{2,3},{3,4},{4,5},{5,6},{6,7},{7,8},{8,9},{9,10},{10,1... | collective-permute-start | bytes 294920 | tf_op jit(solution)/shard_map/ppermute | solution.py:390
  24.5 17.3 %collective-permute-start.5 = (bf16[24,8,256]{2,1,0:T(8,128)(2,1)S(1)}, bf16[24,8,256]{2,1,0:T(8,128)(2,1)S(1)}, u32[]{:S(2)}, u32[]{:S(2)}) collective-permute-start(bf16[24,8,256]{2,1,0:T(8,128)(2,1)S(1)} %get-tuple-element.49), channel_id=1, source_target_pairs={{1,0},{2,1},{3,2},{4,3},{5,4},{6,5},{7,6},{8,7},{9,8},{10,9},{11,1... | collective-permute-start | bytes 294920 | tf_op jit(solution)/shard_map/ppermute | solution.py:390
  36.4 2.1 %copy-start.5 = (f32[16,256,256]{2,1,0:T(8,128)}, f32[16,256,256]{2,1,0:T(8,128)S(1)}, u32[]{:S(2)}) copy-start(f32[16,256,256]{2,1,0:T(8,128)S(1)} %get-tuple-element.38.main_ref) | copy-start | bytes 12582916
  38.5 16.9 %collective-permute-start.1 = (bf16[16,8,256]{2,1,0:T(8,128)(2,1)S(1)}, bf16[16,8,256]{2,1,0:T(8,128)(2,1)S(1)}, u32[]{:S(2)}, u32[]{:S(2)}) collective-permute-start(bf16[16,8,256]{2,1,0:T(8,128)(2,1)S(1)} %get-tuple-element.29), channel_id=1, source_target_pairs={{1,0},{2,1},{3,2},{4,3},{5,4},{6,5},{7,6},{8,7},{9,8},{10,9},{11,1... | collective-permute-start | bytes 196616 | tf_op jit(solution)/shard_map/ppermute | solution.py:390
  39.2 16.1 %collective-permute-start = (bf16[16,8,256]{2,1,0:T(8,128)(2,1)S(1)}, bf16[16,8,256]{2,1,0:T(8,128)(2,1)S(1)}, u32[]{:S(2)}, u32[]{:S(2)}) collective-permute-start(bf16[16,8,256]{2,1,0:T(8,128)(2,1)S(1)} %get-tuple-element.28), channel_id=1, source_target_pairs={{0,1},{1,2},{2,3},{3,4},{4,5},{5,6},{6,7},{7,8},{8,9},{9,10},{10,1... | collective-permute-start | bytes 196616 | tf_op jit(solution)/shard_map/ppermute | solution.py:390
  41.7 0.6 copy-start.12
  42.4 0.6 copy-start.13
  56.1 12.2 %collective-permute-start.7 = (bf16[2,272,256]{2,1,0:T(8,128)(2,1)}, bf16[2,272,256]{2,1,0:T(8,128)(2,1)}, u32[]{:S(2)}, u32[]{:S(2)}) collective-permute-start(bf16[2,272,256]{2,1,0:T(8,128)(2,1)} %pad_maximum_fusion.1), channel_id=1, source_target_pairs={{16,0},{32,16},{48,32},{64,48},{80,64},{96,80},{112,96},{0,112},{1... | collective-permute-start | bytes 835592 | tf_op jit(solution)/shard_map/ppermute | solution.py:390
  57.7 12.0 %copy-start.1 = (f32[2,3,3,256]{3,2,1,0:T(4,128)S(1)}, f32[2,3,3,256]{3,2,1,0:T(4,128)}, u32[]{:S(2)}) copy-start(f32[2,3,3,256]{3,2,1,0:T(4,128)} %copy.14.kernel_ref) | copy-start | bytes 55300
  57.7 12.0 %copy-start.2 = (bf16[2,256,1024]{2,1,0:T(8,128)(2,1)S(1)}, bf16[2,256,1024]{2,1,0:T(8,128)(2,1)}, u32[]{:S(2)}) copy-start(bf16[2,256,1024]{2,1,0:T(8,128)(2,1)} %up_ref.5) | copy-start | bytes 3145732
  57.7 12.0 %copy-start.4 = (f32[2,256]{1,0:T(2,128)S(1)}, f32[2,256]{1,0:T(2,128)}, u32[]{:S(2)}) copy-start(f32[2,256]{1,0:T(2,128)} %gain_ref.5) | copy-start | bytes 6148
  57.7 12.0 %collective-permute-start.6 = (bf16[2,272,256]{2,1,0:T(8,128)(2,1)}, bf16[2,272,256]{2,1,0:T(8,128)(2,1)S(1)}, u32[]{:S(2)}, u32[]{:S(2)}) collective-permute-start(bf16[2,272,256]{2,1,0:T(8,128)(2,1)} %pad_maximum_fusion), channel_id=1, source_target_pairs={{0,16},{16,32},{32,48},{48,64},{64,80},{80,96},{96,112},{112,0},{1... | collective-permute-start | bytes 835592 | tf_op jit(solution)/shard_map/ppermute | solution.py:390
  69.7 1.2 %copy-start.3 = (bf16[2,1024,256]{2,1,0:T(8,128)(2,1)S(1)}, bf16[2,1024,256]{2,1,0:T(8,128)(2,1)}, u32[]{:S(2)}) copy-start(bf16[2,1024,256]{2,1,0:T(8,128)(2,1)} %down_ref.5) | copy-start | bytes 3145732
  71.0 1.2 %copy-start.6 = (bf16[2176,256]{1,0:T(8,128)(2,1)S(1)}, bf16[2176,256]{1,0:T(8,128)(2,1)}, u32[]{:S(2)}) copy-start(bf16[2176,256]{1,0:T(8,128)(2,1)} %get-tuple-element.47.hat_b) | copy-start | bytes 3342340
  72.2 1.2 %copy-start.7 = (f32[2176,128]{1,0:T(8,128)S(1)}, f32[2176,128]{1,0:T(8,128)}, u32[]{:S(2)}) copy-start(f32[2176,128]{1,0:T(8,128)} %get-tuple-element.48.inv_b) | copy-start | bytes 3342340

commit v3 on v2

--- a/solution.py
+++ b/solution.py
@@ -150,10 +150,12 @@
 
 def forward_kernel(
     first, count,
-    left_ref, main_ref, right_ref, kernel_ref, gain_ref, up_ref, down_ref,
-    out_ref, tape_hbm, hat_hbm, inv_hbm,
-    hidden, natural, taps, mean_ref, act, slope, hats, invs, sem,
+    left_ref, main_ref, right_ref, kernel_ref, gain_ref, up_ref, down_ref, *rest
 ):
+    (
+        out_all, tape_all, hat_all, inv_all,
+        hidden, natural, taps, mean_ref, act, slope, hats, invs, outs, sem,
+    ) = rest[-14:]
     fill_taps(taps, kernel_ref, 0, False)
     mean_ref[...] = jnp.full((HID, LANES), 1.0 / HID, BF)
 
@@ -171,17 +173,26 @@
     taped = max(1 - first // RF, 0)
     ends = min((HIGH0 - first) // RF - 1, steps)
 
+    def kept(i, slot):
+        at = pl.ds(first + i * RF, RF)
+        return [pltpu.make_async_copy(outs.at[slot], out_all.at[at], sem.at[slot, 3])]
+
     def copies(i, slot):
-        at = pl.ds(pl.multiple_of((i - taped) * RF * WIDE, 16), RF * WIDE)
+        at = pl.ds(pl.multiple_of((first // RF + i - 1) * RF * WIDE, 16), RF * WIDE)
         return [
-            pltpu.make_async_copy(slope.at[slot], tape_hbm.at[at], sem.at[slot, 0]),
-            pltpu.make_async_copy(hats.at[slot], hat_hbm.at[at], sem.at[slot, 1]),
-            pltpu.make_async_copy(invs.at[slot], inv_hbm.at[at], sem.at[slot, 2]),
+            pltpu.make_async_copy(slope.at[slot], tape_all.at[at], sem.at[slot, 0]),
+            pltpu.make_async_copy(hats.at[slot], hat_all.at[at], sem.at[slot, 1]),
+            pltpu.make_async_copy(invs.at[slot], inv_all.at[at], sem.at[slot, 2]),
         ]
 
     @pl.loop(0, steps)
     def _(i):
         slot = lax.rem(i, 3)
+
+        @pl.when(i >= 3)
+        def _():
+            for copy in kept(i - 3, slot):
+                copy.wait()
 
         @pl.when(i >= taped + 3)
         def _():
@@ -194,13 +205,18 @@
         invs[slot] = inv
         branch = forward(0, hat, gain_ref, up_ref, down_ref, act, slope.at[slot])
         total = flat(rows[1:-1]).astype(F32) + branch
-        store_rows(out_ref, i * RF, total, first + i * RF + 1 - HALO)
+        store_rows(outs.at[slot], 0, total, first + i * RF + 1 - HALO)
+        for copy in kept(i, slot):
+            copy.start()
 
         @pl.when(jnp.logical_and(i >= taped, i < ends))
         def _():
             for copy in copies(i, slot):
                 copy.start()
 
+    for i in range(steps - 3, steps):
+        for copy in kept(i, i % 3):
+            copy.wait()
     for i in range(max(taped, steps - 3), ends):
         for copy in copies(i, i % 3):
             copy.wait()
@@ -209,33 +225,14 @@
 def main_kernel(
     levels,
     above_ref, below_ref, left_ref, main_ref, right_ref, kernel_ref, gain_ref, up_ref, down_ref,
-    dec_ref, enc_ref, hidden_a, tape_a, hat_a, inv_a, hidden_b, tape_b, hat_b, inv_b,
+    dec_ref, enc_ref, hidden, tape, hats, invs,
     out_ref,
-    hidden, taps, mean_ref, natural, act, slope, adjoint, grad_d1, grad_d0, grad1,
-    tape, hats, invs, gathered, sem,
+    taps, mean_ref, natural, act, slope, adjoint, grad_d1, grad_d0, grad1, gathered,
 ):
-    rows_a = hidden_a.shape[0]
-    cells_a = tape_a.shape[0]
-    early = [
-        pltpu.make_async_copy(hidden_a, hidden.at[:rows_a], sem.at[0]),
-        pltpu.make_async_copy(hidden_b, hidden.at[rows_a:], sem.at[1]),
-    ]
-    copies = [
-        pltpu.make_async_copy(tape_a, tape.at[:cells_a], sem.at[2]),
-        pltpu.make_async_copy(tape_b, tape.at[cells_a:], sem.at[3]),
-        pltpu.make_async_copy(hat_a, hats.at[:cells_a], sem.at[4]),
-        pltpu.make_async_copy(hat_b, hats.at[cells_a:], sem.at[5]),
-        pltpu.make_async_copy(inv_a, invs.at[:cells_a], sem.at[6]),
-        pltpu.make_async_copy(inv_b, invs.at[cells_a:], sem.at[7]),
-    ]
-    for copy in early + copies:
-        copy.start()
     mean_ref[...] = jnp.full((HID, LANES), 1.0 / HID, BF)
     fill_taps(taps.at[0], kernel_ref, 1, False)
     fill_taps(taps.at[1], kernel_ref, 1, True)
     fill_taps(taps.at[2], kernel_ref, 0, True)
-    for copy in early:
-        copy.wait()
     last = HIGH1 // RM - 1
 
     @pl.loop(0, HIGH1 // RM)
@@ -278,9 +275,6 @@
             1, grad_s, hat, inv, gain_ref, up_ref, down_ref, act.at[: RM * WIDE], slope, mean_ref
         )
         store_rows(grad_d1, i * RM, grad_d)
-
-    for copy in copies:
-        copy.wait()
 
     @pl.loop(0, HIGH2 // RB)
     def _(i):
@@ -395,17 +389,17 @@
 
 
 def forward_call(first, count, *operands):
-    cells = min(count, HIGH0 - 2 - first, first + count - 2) * WIDE
+    whole = len(operands) - 7
     return pl.pallas_call(
         functools.partial(forward_kernel, first, count),
         out_shape=[
-            sds((count, COLS, SUBL, HID), BF),
-            sds((cells, EXP), BF),
-            sds((cells, HID), BF),
-            sds((cells, LANES), F32),
+            sds((HIGH0, COLS, SUBL, HID), BF),
+            sds((TAPE, EXP), BF),
+            sds((TAPE, HID), BF),
+            sds((TAPE, LANES), F32),
         ],
-        in_specs=[vmem()] * 7,
-        out_specs=[vmem()] + [anywhere()] * 3,
+        in_specs=[vmem()] * 7 + [anywhere()] * whole,
+        out_specs=[anywhere()] * 4,
         scratch_shapes=[
             pltpu.VMEM((count + 2, COLS, SUBL, HID), BF),
             pltpu.VMEM((2, WIDE, LANES), F32),
@@ -415,11 +409,13 @@
             pltpu.VMEM((3, RF * WIDE, EXP), BF),
             pltpu.VMEM((3, RF * WIDE, HID), BF),
             pltpu.VMEM((3, RF * WIDE, LANES), F32),
-            pltpu.SemaphoreType.DMA((3, 3)),
+            pltpu.VMEM((3, RF, COLS, SUBL, HID), BF),
+            pltpu.SemaphoreType.DMA((3, 4)),
         ],
-        compiler_params=kernel_params(62),
+        input_output_aliases={7 + k: k for k in range(whole)},
+        compiler_params=kernel_params(16),
         cost_estimate=pl.CostEstimate(
-            flops=MLP * count * 3, bytes_accessed=cells * EXP * 2, transcendentals=0
+            flops=MLP * count * 3, bytes_accessed=TAPE * EXP * 2, transcendentals=0
         ),
         name="forward_zero",
     )(*operands)
@@ -429,10 +425,9 @@
     return pl.pallas_call(
         functools.partial(main_kernel, levels),
         out_shape=sds((channels * LAT, LON), F32),
-        in_specs=[vmem()] * 11 + [anywhere()] * 8,
+        in_specs=[vmem()] * 15,
         out_specs=vmem(),
         scratch_shapes=[
-            pltpu.VMEM((HIGH0, COLS, SUBL, HID), BF),
             pltpu.VMEM((3, 9, SUBL, HID), BF),
             pltpu.VMEM((HID, LANES), BF),
             pltpu.VMEM((2 * max(RM, RE), WIDE, LANES), F32),
@@ -442,13 +437,9 @@
             pltpu.VMEM((HIGH1, COLS, SUBL, HID), BF),
             pltpu.VMEM((HIGH2, COLS, SUBL, HID), BF),
             pltpu.VMEM((HIGH2, COLS, SUBL, HID), BF),
-            pltpu.VMEM((TAPE, EXP), BF),
-            pltpu.VMEM((TAPE, HID), BF),
-            pltpu.VMEM((TAPE, LANES), F32),
             pltpu.VMEM((2, channels * LAT, LANES), F32),
-            pltpu.SemaphoreType.DMA((8,)),
         ],
-        compiler_params=kernel_params(48),
+        compiler_params=kernel_params(24),
         cost_estimate=pl.CostEstimate(
             flops=MLP * (2 * HIGH1 + HIGH2), bytes_accessed=TAPE * EXP * 2, transcendentals=0
         ),
@@ -517,24 +508,24 @@
     )(table)
 
     west, east = pair_shift(f_left, f_right, "lon")
-    first_rows = 12
+    first_rows = 10
     main, f_left = lax.optimization_barrier((main, f_left))
     part_a = forward_call(
         0, first_rows, left, main, right, kernels, gains, up_weight, down_weight
     )
-    west, east, main, hidden_a = lax.optimization_barrier((west, east, main, part_a[0]))
-    part_a = [hidden_a] + list(part_a[1:])
+    west, east, main, *part_a = lax.optimization_barrier((west, east, main, *part_a))
     low = jnp.concatenate([west[:EDGE], f_top, east[:EDGE]], axis=1)
     high = jnp.concatenate([west[LAT - EDGE :], f_bottom, east[LAT - EDGE :]], axis=1)
     above, below = pair_shift(low, high, "lat")
     main, low = lax.optimization_barrier((main, low))
-    part_b = forward_call(
-        first_rows, HIGH0 - first_rows, left, main, right, kernels, gains, up_weight, down_weight
+    forward = forward_call(
+        first_rows, HIGH0 - first_rows, left, main, right, kernels, gains, up_weight, down_weight,
+        *part_a,
     )
 
     gradient = main_call(
         channels, levels, above, below, west, field, east, kernels, gains, up_weight,
-        down_weight, dec_weight, enc_weight, *part_a, *part_b,
+        down_weight, dec_weight, enc_weight, *forward,
     )
     return gradient.reshape(channels, LAT, LON)
 

time: 112 us -> 96 us (0.86)
  Pallas kernels: 67.4 us -> 59 us
  local copies, waits for them, and re-layouts: 10.9 us -> 3.97 us
  other arithmetic: 1.55 us -> 0.08 us
    unnamed x34 -> x22, local copies, waits for them, and re-layouts: 10.9 us -> 3.23 us
    pallas_call x1, Pallas kernels: 38.5 us -> 34 us  [main_call(): pl.pallas_call(functools.partial(main_kernel, levels), out_shape=sds((cha...]
    pallas_call x2, Pallas kernels: 22.3 us -> 18.3 us  [forward_call(): pl.pallas_call(functools.partial(forward_kernel, first, count), out_shape...]
  transfers between devices with their start and end apart: 9 -> 9, of which waited for: 2 -> 2; matrix products, arithmetic and copies ran while one was open for 4% -> 5% of each run, Pallas kernels for 26% -> 26%
where the time goes in v3:
time: 96 us; the launch traced here: 95.7 us
  Pallas kernels  59 us (61%)
  starting transfers between devices  23.5 us (24%)
  waiting for transfers between devices  6.84 us (7%)
  local copies, waits for them, and re-layouts  3.97 us (4%)
  matrix products  2.1 us (2%)
    pallas_call x1, Pallas kernels, main_call(): pl.pallas_call(functools.partial(main_kernel, levels), out_shape=sds((cha...  34 us
    pallas_call x2, Pallas kernels, forward_call(): pl.pallas_call(functools.partial(forward_kernel, first, count), out_shape...  18.3 us
    ppermute x8, starting transfers between devices, pair_shift(): return (lax.ppermute(high, axis, up), lax.ppermute(low, axis, down))  12.8 us
    all_to_all x1, starting transfers between devices, body(): lax.all_to_all(packed, ('lat', 'lon'), split_axis=0, concat_axis=0, tiled...  10.7 us
    pallas_call x1, Pallas kernels, body(): pl.pallas_call(functools.partial(place_observations, slots, levels), out_...  5.76 us
    all_to_all x1, waiting for transfers between devices, body(): lax.all_to_all(packed, ('lat', 'lon'), split_axis=0, concat_axis=0, tiled...  5.08 us
    unnamed x22, local copies, waits for them, and re-layouts  3.23 us
    dot_general x1, matrix products, body(): lax.dot_general(tall, enc_weight, (((0,), (0,)), ((), ())), preferred_ele...  2.1 us
  transfers between devices with their start and end apart: 9, of which 2 were waited for; matrix products, arithmetic and copies ran while one was open for 5% of the time, Pallas kernels for 26%

profile of v3, /device:TPU:1, one launch (start us, length us, event | category | flops | bytes accessed | tf_op | source)
XLA Modules:
  0.0 95.7 jit_solution(710226773037235915)
XLA Ops:
  0.0 1.3 %copy.15 = bf16[76,16,256]{2,0,1:T(8,128)(2,1)S(1)} copy(bf16[76,16,256]{2,1,0:T(8,128)(2,1)} %param.10) | data formatting | bytes 1245184 | tf_op args[0]
  1.3 0.0 copy-start.4
  1.4 4.6 %collective-permute-start.3 = (bf16[76,4,256]{2,0,1:T(8,128)(2,1)S(1)}, bf16[76,4,256]{2,0,1:T(8,128)(2,1)S(1)}, u32[]{:S(2)}, u32[]{:S(2)}) collective-permute-start(bf16[76,4,256]{2,0,1:T(8,128)(2,1)S(1)} %get-tuple-element.34), channel_id=1, source_target_pairs={{16,0},{32,16},{48,32},{64,48},{80,64},{96,80},{112,96},{0,112},{1... | collective-permute-start | bytes 466952 | tf_op jit(solution)/shard_map/ppermute | solution.py:384
  5.9 0.0 collective-permute-start.2
  5.9 0.7 copy.30
  6.6 1.1 %copy.28 = f32[1,128,12,76]{1,3,0,2:T(8,128)S(1)} copy(f32[1,128,12,76]{1,0,3,2:T(1,128)} %param.17) | data formatting | bytes 933888
  7.8 0.9 pack_observations.1
  8.7 10.7 %all-to-all-start = ((bf16[128,8,128]{2,1,0:T(8,128)(2,1)}), bf16[128,8,128]{2,1,0:T(8,128)(2,1)S(1)}, u32[]{:S(2)}, u32[]{:S(2)}) async-start(bf16[128,8,128]{2,1,0:T(8,128)(2,1)} %pack_observations.1), calls=%async_computation | async-start | bytes 524288 | tf_op jit(solution)/shard_map/all_to_all | solution.py:474
  19.4 0.1 copy.21.dec_ref
  19.6 2.1 %convolution_convert_fusion.main_ref = bf16[24,256,256]{2,1,0:T(8,128)(2,1)S(1)} fusion(bf16[76,4,256]{2,0,1:T(8,128)(2,1)S(1)} %broadcast_select_fusion, bf16[76,16,256]{2,0,1:T(8,128)(2,1)} %copy-done.4, bf16[76,4,256]{2,0,1:T(8,128)(2,1)S(1)} %broadcast_select_fusion.1, bf16[76,256]{1,0:T(8,128)(2,1)S(1)} %copy-done), kind=kOutput, calls=%fused_computation | convolution fusion | flops 241582080 | bytes 4118528 | tf_op jit(solution)/shard_map/dot_general | solution.py:480
  21.8 0.7 fusion.7
  22.4 3.1 %collective-permute-start.4 = (bf16[24,8,256]{2,1,0:T(8,128)(2,1)}, bf16[24,8,256]{2,1,0:T(8,128)(2,1)}, u32[]{:S(2)}, u32[]{:S(2)}) collective-permute-start(bf16[24,8,256]{2,1,0:T(8,128)(2,1)} %get-tuple-element.56), channel_id=1, source_target_pairs={{0,1},{1,2},{2,3},{3,4},{4,5},{5,6},{6,7},{7,8},{8,9},{9,10},{10,1... | collective-permute-start | bytes 294920 | tf_op jit(solution)/shard_map/ppermute | solution.py:384
  25.6 0.0 collective-permute-start.5
  25.6 5.1 %all-to-all-done.table_ref = bf16[128,8,128]{2,1,0:T(8,128)(2,1)S(1)} async-done(((bf16[128,8,128]{2,1,0:T(8,128)(2,1)}), bf16[128,8,128]{2,1,0:T(8,128)(2,1)S(1)}, u32[]{:S(2)}, u32[]{:S(2)}) %all-to-all-start) | async-done | bytes 262176 | tf_op jit(solution)/shard_map/all_to_all | solution.py:474
  30.7 5.8 %place_observations.1 = (f32[16,256,256]{2,1,0:T(8,128)S(1)}, bf16[2,256,256]{2,1,0:T(8,128)(2,1)S(1)}, bf16[2,256,256]{2,1,0:T(8,128)(2,1)S(1)}, bf16[16,8,256]{2,1,0:T(8,128)(2,1)S(1)}, bf16[16,8,256]{2,1,0:T(8,128)(2,1)S(1)}) custom-call(bf16[128,8,128]{2,1,0:T(8,128)(2,1)S(1)} %all-to-all-done.table_ref), custom_call_target="tpu_custom_call" | custom-call | flops 3221225472 | bytes 4194304 | tf_op jit(solution)/shard_map/place_observations/pallas_call | solution.py:485
  36.4 0.9 collective-permute-start.1
  37.4 2.4 %collective-permute-start = (bf16[16,8,256]{2,1,0:T(8,128)(2,1)S(1)}, bf16[16,8,256]{2,1,0:T(8,128)(2,1)S(1)}, u32[]{:S(2)}, u32[]{:S(2)}) collective-permute-start(bf16[16,8,256]{2,1,0:T(8,128)(2,1)S(1)} %get-tuple-element.31), channel_id=1, source_target_pairs={{0,1},{1,2},{2,3},{3,4},{4,5},{5,6},{6,7},{7,8},{8,9},{9,10},{10,1... | collective-permute-start | bytes 196616 | tf_op jit(solution)/shard_map/ppermute | solution.py:384
  39.8 8.4 %forward_zero.2 = (bf16[22,17,16,256]{3,2,1,0:T(8,128)(2,1)S(1)}, bf16[4896,1024]{1,0:T(8,128)(2,1)S(1)}, bf16[4896,256]{1,0:T(8,128)(2,1)S(1)}, f32[4896,128]{1,0:T(8,128)S(1)}) custom-call(bf16[24,8,256]{2,1,0:T(8,128)(2,1)} %collective-permute-done.4.left_ref, bf16[24,256,256]{2,1,0:T(8,128)(2,1)S(1)} %convolution_convert_fusion.main_ref, ...), custom_call_target="tpu_custom_call" | custom-call | flops 8556380160 | bytes 10027008 | tf_op jit(solution)/shard_map/forward_zero/pallas_call | solution.py:393
  48.3 0.9 collective-permute-start.7
  49.2 0.9 collective-permute-start.6
  50.1 9.9 %forward_zero.3 = (bf16[22,17,16,256]{3,2,1,0:T(8,128)(2,1)S(1)}, bf16[4896,1024]{1,0:T(8,128)(2,1)S(1)}, bf16[4896,256]{1,0:T(8,128)(2,1)S(1)}, f32[4896,128]{1,0:T(8,128)S(1)}) custom-call(bf16[24,8,256]{2,1,0:T(8,128)(2,1)} %collective-permute-done.4.left_ref, ...), custom_call_target="tpu_custom_call", output_to_operand_aliasing={{0}: (7, {}), {1}: (8, {}), {2}: (9, {}), {3}: (10, {})} | custom-call | flops 10267656192 | bytes 10027008 | tf_op jit(solution)/shard_map/forward_zero/pallas_call | solution.py:393
  60.0 0.0 collective-permute-done.7.below_ref
  60.0 1.7 %collective-permute-done.6.above_ref = bf16[2,272,256]{2,1,0:T(8,128)(2,1)S(1)} collective-permute-done((bf16[2,272,256]{2,1,0:T(8,128)(2,1)S(1)}, bf16[2,272,256]{2,1,0:T(8,128)(2,1)S(1)}, u32[]{:S(2)}, u32[]{:S(2)}) %collective-permute-start.6) | collective-permute-done | bytes 278560 | tf_op jit(solution)/shard_map/ppermute | solution.py:384
  61.7 34.0 %forward_one_and_adjoint.1 = f32[1216,256]{1,0:T(8,128)} custom-call(bf16[2,272,256]{2,1,0:T(8,128)(2,1)S(1)} %collective-permute-done.6.above_ref, bf16[2,272,256]{2,1,0:T(8,128)(2,1)S(1)} %collective-permute-done.7.below_ref, bf16[16,8,256]{2,1,0:T(8,128)(2,1)S(1)} %collective-permute-done.left_ref, f32[16,256,256]{2,1,0:T(8,128)S(1)} %get-tuple-element.44.main_ref, ...), custom_call_target="tpu_custom_call" | custom-call | flops 16542334976 | bytes 10027008 | tf_op jit(solution)/shard_map/forward_one_and_adjoint/pallas_call | solution.py:425
  (30 shorter events, 0.2 us)
Async XLA Ops:
  0.0 7.7 %copy-start.7 = (s32[1,128,12]{1,0,2:T(1,128)S(1)}, s32[1,128,12]{1,0,2:T(1,128)}, u32[]{:S(2)}) copy-start(s32[1,128,12]{1,0,2:T(1,128)} %param.19) | copy-start | bytes 18436
  0.0 19.4 %copy-start.6 = (f32[2,3,3,256]{3,0,2,1:T(2,128)S(1)}, f32[2,3,3,256]{3,0,2,1:T(2,128)}, u32[]{:S(2)}) copy-start(f32[2,3,3,256]{3,0,2,1:T(2,128)} %param.12) | copy-start | bytes 55300
  0.0 19.4 %copy-start.5 = (bf16[256,76]{0,1:T(8,128)(2,1)S(1)}, bf16[256,76]{0,1:T(8,128)(2,1)}, u32[]{:S(2)}) copy-start(bf16[256,76]{0,1:T(8,128)(2,1)} %param.16) | copy-start | bytes 116740
  0.0 19.6 %copy-start = (bf16[76,256]{1,0:T(8,128)(2,1)S(1)}, bf16[76,256]{1,0:T(8,128)(2,1)}, u32[]{:S(2)}) copy-start(bf16[76,256]{1,0:T(8,128)(2,1)} %enc_ref.1) | copy-start | bytes 116740
  1.3 6.4 %copy-start.4 = (bf16[76,16,256]{2,0,1:T(8,128)(2,1)}, bf16[76,16,256]{2,0,1:T(8,128)(2,1)S(1)}, u32[]{:S(2)}) copy-start(bf16[76,16,256]{2,0,1:T(8,128)(2,1)S(1)} %copy.15) | copy-start | bytes 1867780
  1.4 18.2 %collective-permute-start.3 = (bf16[76,4,256]{2,0,1:T(8,128)(2,1)S(1)}, bf16[76,4,256]{2,0,1:T(8,128)(2,1)S(1)}, u32[]{:S(2)}, u32[]{:S(2)}) collective-permute-start(bf16[76,4,256]{2,0,1:T(8,128)(2,1)S(1)} %get-tuple-element.34), channel_id=1, source_target_pairs={{16,0},{32,16},{48,32},{64,48},{80,64},{96,80},{112,96},{0,112},{1... | collective-permute-start | bytes 466952 | tf_op jit(solution)/shard_map/ppermute | solution.py:384
  5.9 13.7 %collective-permute-start.2 = (bf16[76,4,256]{2,0,1:T(8,128)(2,1)S(1)}, bf16[76,4,256]{2,0,1:T(8,128)(2,1)S(1)}, u32[]{:S(2)}, u32[]{:S(2)}) collective-permute-start(bf16[76,4,256]{2,0,1:T(8,128)(2,1)S(1)} %get-tuple-element.33), channel_id=1, source_target_pairs={{0,16},{16,32},{32,48},{48,64},{64,80},{80,96},{96,112},{112,0},{1... | collective-permute-start | bytes 466952 | tf_op jit(solution)/shard_map/ppermute | solution.py:384
  8.7 22.0 %all-to-all-start = ((bf16[128,8,128]{2,1,0:T(8,128)(2,1)}), bf16[128,8,128]{2,1,0:T(8,128)(2,1)S(1)}, u32[]{:S(2)}, u32[]{:S(2)}) async-start(bf16[128,8,128]{2,1,0:T(8,128)(2,1)} %pack_observations.1), calls=%async_computation | async-start | bytes 524288 | tf_op jit(solution)/shard_map/all_to_all | solution.py:474
  22.4 17.3 %collective-permute-start.4 = (bf16[24,8,256]{2,1,0:T(8,128)(2,1)}, bf16[24,8,256]{2,1,0:T(8,128)(2,1)}, u32[]{:S(2)}, u32[]{:S(2)}) collective-permute-start(bf16[24,8,256]{2,1,0:T(8,128)(2,1)} %get-tuple-element.56), channel_id=1, source_target_pairs={{0,1},{1,2},{2,3},{3,4},{4,5},{5,6},{6,7},{7,8},{8,9},{9,10},{10,1... | collective-permute-start | bytes 294920 | tf_op jit(solution)/shard_map/ppermute | solution.py:384
  25.6 14.2 %copy-start.3 = (f32[2,256]{1,0:T(2,128)S(1)}, f32[2,256]{1,0:T(2,128)}, u32[]{:S(2)}) copy-start(f32[2,256]{1,0:T(2,128)} %gain_ref.5) | copy-start | bytes 6148
  25.6 14.2 %collective-permute-start.5 = (bf16[24,8,256]{2,1,0:T(8,128)(2,1)}, bf16[24,8,256]{2,1,0:T(8,128)(2,1)}, u32[]{:S(2)}, u32[]{:S(2)}) collective-permute-start(bf16[24,8,256]{2,1,0:T(8,128)(2,1)} %get-tuple-element.55), channel_id=1, source_target_pairs={{1,0},{2,1},{3,2},{4,3},{5,4},{6,5},{7,6},{8,7},{9,8},{10,9},{11,1... | collective-permute-start | bytes 294920 | tf_op jit(solution)/shard_map/ppermute | solution.py:384
  30.7 9.1 %copy-start.1 = (bf16[2,256,1024]{2,1,0:T(8,128)(2,1)S(1)}, bf16[2,256,1024]{2,1,0:T(8,128)(2,1)}, u32[]{:S(2)}) copy-start(bf16[2,256,1024]{2,1,0:T(8,128)(2,1)} %up_ref.5) | copy-start | bytes 3145732
  30.7 9.1 %copy-start.2 = (bf16[2,1024,256]{2,1,0:T(8,128)(2,1)S(1)}, bf16[2,1024,256]{2,1,0:T(8,128)(2,1)}, u32[]{:S(2)}) copy-start(bf16[2,1024,256]{2,1,0:T(8,128)(2,1)} %down_ref.5) | copy-start | bytes 3145732
  36.4 11.8 %collective-permute-start.1 = (bf16[16,8,256]{2,1,0:T(8,128)(2,1)S(1)}, bf16[16,8,256]{2,1,0:T(8,128)(2,1)S(1)}, u32[]{:S(2)}, u32[]{:S(2)}) collective-permute-start(bf16[16,8,256]{2,1,0:T(8,128)(2,1)S(1)} %get-tuple-element.32), channel_id=1, source_target_pairs={{1,0},{2,1},{3,2},{4,3},{5,4},{6,5},{7,6},{8,7},{9,8},{10,9},{11,1... | collective-permute-start | bytes 196616 | tf_op jit(solution)/shard_map/ppermute | solution.py:384
  37.4 10.9 %collective-permute-start = (bf16[16,8,256]{2,1,0:T(8,128)(2,1)S(1)}, bf16[16,8,256]{2,1,0:T(8,128)(2,1)S(1)}, u32[]{:S(2)}, u32[]{:S(2)}) collective-permute-start(bf16[16,8,256]{2,1,0:T(8,128)(2,1)S(1)} %get-tuple-element.31), channel_id=1, source_target_pairs={{0,1},{1,2},{2,3},{3,4},{4,5},{5,6},{6,7},{7,8},{8,9},{9,10},{10,1... | collective-permute-start | bytes 196616 | tf_op jit(solution)/shard_map/ppermute | solution.py:384
  48.3 11.7 %collective-permute-start.7 = (bf16[2,272,256]{2,1,0:T(8,128)(2,1)S(1)}, bf16[2,272,256]{2,1,0:T(8,128)(2,1)S(1)}, u32[]{:S(2)}, u32[]{:S(2)}) collective-permute-start(bf16[2,272,256]{2,1,0:T(8,128)(2,1)S(1)} %pad_maximum_fusion.1), channel_id=1, source_target_pairs={{16,0},{32,16},{48,32},{64,48},{80,64},{96,80},{112,96},{0,112},{1... | collective-permute-start | bytes 835592 | tf_op jit(solution)/shard_map/ppermute | solution.py:384
  49.2 12.5 %collective-permute-start.6 = (bf16[2,272,256]{2,1,0:T(8,128)(2,1)S(1)}, bf16[2,272,256]{2,1,0:T(8,128)(2,1)S(1)}, u32[]{:S(2)}, u32[]{:S(2)}) collective-permute-start(bf16[2,272,256]{2,1,0:T(8,128)(2,1)S(1)} %pad_maximum_fusion), channel_id=1, source_target_pairs={{0,16},{16,32},{32,48},{48,64},{64,80},{80,96},{96,112},{112,0},{1... | collective-permute-start | bytes 835592 | tf_op jit(solution)/shard_map/ppermute | solution.py:384

commit v4 on v3

--- a/solution.py
+++ b/solution.py
@@ -103,8 +103,8 @@
 def normalize(spatial, mean_ref):
     square = (spatial * spatial).astype(BF)
     mean = jnp.dot(square, mean_ref[...], preferred_element_type=F32)
-    inv = lax.rsqrt(mean + EPSILON)
-    return inv, spatial * twice(inv.astype(BF))
+    inv = lax.rsqrt(mean + EPSILON).astype(BF)
+    return inv, spatial * twice(inv)
 
 
 def forward(b, hat, gain_ref, up_ref, down_ref, act_ref, slope_ref):
@@ -124,10 +124,9 @@
         grad_g = times_transposed(grad_s, down_ref[b, cut, :])
         act_ref[:, cut] = grad_g.astype(BF) * slope_ref[:, cut]
     weighted = times_transposed(act_ref[...], up_ref[b]) * (0.5 * gain_ref[b : b + 1, :])
-    hat = hat.astype(F32)
-    product = (weighted * hat).astype(BF)
-    projection = jnp.dot(product, mean_ref[...], preferred_element_type=F32)
-    return twice(inv) * (weighted - hat * twice(projection))
+    weighted = weighted.astype(BF)
+    projection = jnp.dot(weighted * hat, mean_ref[...], preferred_element_type=F32)
+    return twice(inv) * (weighted - hat * twice(projection.astype(BF)))
 
 
 def row_mask(first):
@@ -140,7 +139,7 @@
     for r in range(value.shape[0] // WIDE):
         part = value[r * WIDE : (r + 1) * WIDE]
         if first is not None:
-            part = part * row_mask(first + r)
+            part = part * row_mask(first + r).astype(part.dtype)
         ref[base + r] = part.astype(BF).reshape(COLS, SUBL, HID)
 
 
@@ -356,7 +355,7 @@
         where = tags[at + slots + q : at + slots + q + 1, :]
         hot[:, part] = jnp.where(column == where, 1.0, 0.0).astype(BF)
 
-    group = 4
+    group = 8
 
     @pl.loop(0, LAT // group)
     def _(i):
@@ -396,7 +395,7 @@
             sds((HIGH0, COLS, SUBL, HID), BF),
             sds((TAPE, EXP), BF),
             sds((TAPE, HID), BF),
-            sds((TAPE, LANES), F32),
+            sds((TAPE, LANES), BF),
         ],
         in_specs=[vmem()] * 7 + [anywhere()] * whole,
         out_specs=[anywhere()] * 4,
@@ -408,7 +407,7 @@
             pltpu.VMEM((RF * WIDE, EXP), BF),
             pltpu.VMEM((3, RF * WIDE, EXP), BF),
             pltpu.VMEM((3, RF * WIDE, HID), BF),
-            pltpu.VMEM((3, RF * WIDE, LANES), F32),
+            pltpu.VMEM((3, RF * WIDE, LANES), BF),
             pltpu.VMEM((3, RF, COLS, SUBL, HID), BF),
             pltpu.SemaphoreType.DMA((3, 4)),
         ],

time: 96 us -> 95.9 us (level)
    pallas_call x2, Pallas kernels: 18.3 us -> 19.6 us  [forward_call(): pl.pallas_call(functools.partial(forward_kernel, first, count), out_shape...]
  transfers between devices with their start and end apart: 9 -> 9, of which waited for: 2 -> 2; matrix products, arithmetic and copies ran while one was open for 5% -> 5% of each run, Pallas kernels for 26% -> 27%
where the time goes in v4:
time: 95.9 us; the launch traced here: 95.5 us
  Pallas kernels  59.5 us (62%)
  starting transfers between devices  23.5 us (25%)
  waiting for transfers between devices  6.13 us (6%)
  local copies, waits for them, and re-layouts  3.97 us (4%)
  matrix products  2.1 us (2%)
    pallas_call x1, Pallas kernels, main_call(): pl.pallas_call(functools.partial(main_kernel, levels), out_shape=sds((cha...  33.5 us
    pallas_call x2, Pallas kernels, forward_call(): pl.pallas_call(functools.partial(forward_kernel, first, count), out_shape...  19.6 us
    ppermute x8, starting transfers between devices, pair_shift(): return (lax.ppermute(high, axis, up), lax.ppermute(low, axis, down))  12.8 us
    all_to_all x1, starting transfers between devices, body(): lax.all_to_all(packed, ('lat', 'lon'), split_axis=0, concat_axis=0, tiled...  10.7 us
    pallas_call x1, Pallas kernels, body(): pl.pallas_call(functools.partial(place_observations, slots, levels), out_...  5.44 us
    all_to_all x1, waiting for transfers between devices, body(): lax.all_to_all(packed, ('lat', 'lon'), split_axis=0, concat_axis=0, tiled...  5.08 us
    unnamed x22, local copies, waits for them, and re-layouts  3.23 us
    dot_general x1, matrix products, body(): lax.dot_general(tall, enc_weight, (((0,), (0,)), ((), ())), preferred_ele...  2.1 us
  transfers between devices with their start and end apart: 9, of which 2 were waited for; matrix products, arithmetic and copies ran while one was open for 5% of the time, Pallas kernels for 27%

profile of v4, /device:TPU:1, one launch (start us, length us, event | category | flops | bytes accessed | tf_op | source)
XLA Modules:
  0.0 95.5 jit_solution(5545564859221904248)
XLA Ops:
  0.0 1.3 %copy.15 = bf16[76,16,256]{2,0,1:T(8,128)(2,1)S(1)} copy(bf16[76,16,256]{2,1,0:T(8,128)(2,1)} %param.10) | data formatting | bytes 1245184 | tf_op args[0]
  1.3 0.0 copy-start.4
  1.4 4.6 %collective-permute-start.3 = (bf16[76,4,256]{2,0,1:T(8,128)(2,1)S(1)}, bf16[76,4,256]{2,0,1:T(8,128)(2,1)S(1)}, u32[]{:S(2)}, u32[]{:S(2)}) collective-permute-start(bf16[76,4,256]{2,0,1:T(8,128)(2,1)S(1)} %get-tuple-element.34), channel_id=1, source_target_pairs={{16,0},{32,16},{48,32},{64,48},{80,64},{96,80},{112,96},{0,112},{1... | collective-permute-start | bytes 466952 | tf_op jit(solution)/shard_map/ppermute | solution.py:383
  5.9 0.0 collective-permute-start.2
  5.9 0.7 copy.30
  6.6 1.1 %copy.28 = f32[1,128,12,76]{1,3,0,2:T(8,128)S(1)} copy(f32[1,128,12,76]{1,0,3,2:T(1,128)} %param.17) | data formatting | bytes 933888
  7.8 0.9 pack_observations.1
  8.7 10.7 %all-to-all-start = ((bf16[128,8,128]{2,1,0:T(8,128)(2,1)}), bf16[128,8,128]{2,1,0:T(8,128)(2,1)S(1)}, u32[]{:S(2)}, u32[]{:S(2)}) async-start(bf16[128,8,128]{2,1,0:T(8,128)(2,1)} %pack_observations.1), calls=%async_computation | async-start | bytes 524288 | tf_op jit(solution)/shard_map/all_to_all | solution.py:473
  19.4 0.1 copy.21.dec_ref
  19.6 2.1 %convolution_convert_fusion.main_ref = bf16[24,256,256]{2,1,0:T(8,128)(2,1)S(1)} fusion(bf16[76,4,256]{2,0,1:T(8,128)(2,1)S(1)} %broadcast_select_fusion, bf16[76,16,256]{2,0,1:T(8,128)(2,1)} %copy-done.4, bf16[76,4,256]{2,0,1:T(8,128)(2,1)S(1)} %broadcast_select_fusion.1, bf16[76,256]{1,0:T(8,128)(2,1)S(1)} %copy-done), kind=kOutput, calls=%fused_computation | convolution fusion | flops 241582080 | bytes 4118528 | tf_op jit(solution)/shard_map/dot_general | solution.py:479
  21.8 0.7 fusion.7
  22.4 3.1 %collective-permute-start.4 = (bf16[24,8,256]{2,1,0:T(8,128)(2,1)}, bf16[24,8,256]{2,1,0:T(8,128)(2,1)}, u32[]{:S(2)}, u32[]{:S(2)}) collective-permute-start(bf16[24,8,256]{2,1,0:T(8,128)(2,1)} %get-tuple-element.56), channel_id=1, source_target_pairs={{0,1},{1,2},{2,3},{3,4},{4,5},{5,6},{6,7},{7,8},{8,9},{9,10},{10,1... | collective-permute-start | bytes 294920 | tf_op jit(solution)/shard_map/ppermute | solution.py:383
  25.6 0.0 collective-permute-start.5
  25.6 5.1 %all-to-all-done.table_ref = bf16[128,8,128]{2,1,0:T(8,128)(2,1)S(1)} async-done(((bf16[128,8,128]{2,1,0:T(8,128)(2,1)}), bf16[128,8,128]{2,1,0:T(8,128)(2,1)S(1)}, u32[]{:S(2)}, u32[]{:S(2)}) %all-to-all-start) | async-done | bytes 262176 | tf_op jit(solution)/shard_map/all_to_all | solution.py:473
  30.7 5.4 %place_observations.1 = (f32[16,256,256]{2,1,0:T(8,128)S(1)}, bf16[2,256,256]{2,1,0:T(8,128)(2,1)S(1)}, bf16[2,256,256]{2,1,0:T(8,128)(2,1)S(1)}, bf16[16,8,256]{2,1,0:T(8,128)(2,1)S(1)}, bf16[16,8,256]{2,1,0:T(8,128)(2,1)S(1)}) custom-call(bf16[128,8,128]{2,1,0:T(8,128)(2,1)S(1)} %all-to-all-done.table_ref), custom_call_target="tpu_custom_call" | custom-call | flops 3221225472 | bytes 4194304 | tf_op jit(solution)/shard_map/place_observations/pallas_call | solution.py:484
  36.1 0.9 collective-permute-start.1
  37.0 2.4 %collective-permute-start = (bf16[16,8,256]{2,1,0:T(8,128)(2,1)S(1)}, bf16[16,8,256]{2,1,0:T(8,128)(2,1)S(1)}, u32[]{:S(2)}, u32[]{:S(2)}) collective-permute-start(bf16[16,8,256]{2,1,0:T(8,128)(2,1)S(1)} %get-tuple-element.31), channel_id=1, source_target_pairs={{0,1},{1,2},{2,3},{3,4},{4,5},{5,6},{6,7},{7,8},{8,9},{9,10},{10,1... | collective-permute-start | bytes 196616 | tf_op jit(solution)/shard_map/ppermute | solution.py:383
  39.5 9.0 %forward_zero.2 = (bf16[22,17,16,256]{3,2,1,0:T(8,128)(2,1)S(1)}, bf16[4896,1024]{1,0:T(8,128)(2,1)S(1)}, bf16[4896,256]{1,0:T(8,128)(2,1)S(1)}, bf16[4896,128]{1,0:T(8,128)(2,1)S(1)}) custom-call(bf16[24,8,256]{2,1,0:T(8,128)(2,1)} %collective-permute-done.4.left_ref, bf16[24,256,256]{2,1,0:T(8,128)(2,1)S(1)} %convolution_convert_fusion.main_ref, ...), custom_call_target="tpu_custom_call" | custom-call | flops 8556380160 | bytes 10027008 | tf_op jit(solution)/shard_map/forward_zero/pallas_call | solution.py:392
  48.5 0.0 collective-permute-done.1.right_ref
  48.5 0.9 collective-permute-start.7
  49.5 0.9 collective-permute-start.6
  50.3 10.6 %forward_zero.3 = (bf16[22,17,16,256]{3,2,1,0:T(8,128)(2,1)S(1)}, bf16[4896,1024]{1,0:T(8,128)(2,1)S(1)}, bf16[4896,256]{1,0:T(8,128)(2,1)S(1)}, bf16[4896,128]{1,0:T(8,128)(2,1)S(1)}) custom-call(bf16[24,8,256]{2,1,0:T(8,128)(2,1)} %collective-permute-done.4.left_ref, ...), custom_call_target="tpu_custom_call", output_to_operand_aliasing={{0}: (7, {}), {1}: (8, {}), {2}: (9, {}), {3}: (10, {})} | custom-call | flops 10267656192 | bytes 10027008 | tf_op jit(solution)/shard_map/forward_zero/pallas_call | solution.py:392
  61.0 1.0 %collective-permute-done.6.above_ref = bf16[2,272,256]{2,1,0:T(8,128)(2,1)S(1)} collective-permute-done((bf16[2,272,256]{2,1,0:T(8,128)(2,1)S(1)}, bf16[2,272,256]{2,1,0:T(8,128)(2,1)S(1)}, u32[]{:S(2)}, u32[]{:S(2)}) %collective-permute-start.6) | collective-permute-done | bytes 278560 | tf_op jit(solution)/shard_map/ppermute | solution.py:383
  62.0 33.5 %forward_one_and_adjoint.1 = f32[1216,256]{1,0:T(8,128)} custom-call(bf16[2,272,256]{2,1,0:T(8,128)(2,1)S(1)} %collective-permute-done.6.above_ref, bf16[2,272,256]{2,1,0:T(8,128)(2,1)S(1)} %collective-permute-done.7.below_ref, bf16[16,8,256]{2,1,0:T(8,128)(2,1)S(1)} %collective-permute-done.left_ref, f32[16,256,256]{2,1,0:T(8,128)S(1)} %get-tuple-element.44.main_ref, ...), custom_call_target="tpu_custom_call" | custom-call | flops 16542334976 | bytes 10027008 | tf_op jit(solution)/shard_map/forward_one_and_adjoint/pallas_call | solution.py:424
  (30 shorter events, 0.2 us)
Async XLA Ops:
  0.0 7.7 %copy-start.7 = (s32[1,128,12]{1,0,2:T(1,128)S(1)}, s32[1,128,12]{1,0,2:T(1,128)}, u32[]{:S(2)}) copy-start(s32[1,128,12]{1,0,2:T(1,128)} %param.19) | copy-start | bytes 18436
  0.0 19.4 %copy-start.6 = (f32[2,3,3,256]{3,0,2,1:T(2,128)S(1)}, f32[2,3,3,256]{3,0,2,1:T(2,128)}, u32[]{:S(2)}) copy-start(f32[2,3,3,256]{3,0,2,1:T(2,128)} %param.12) | copy-start | bytes 55300
  0.0 19.4 %copy-start.5 = (bf16[256,76]{0,1:T(8,128)(2,1)S(1)}, bf16[256,76]{0,1:T(8,128)(2,1)}, u32[]{:S(2)}) copy-start(bf16[256,76]{0,1:T(8,128)(2,1)} %param.16) | copy-start | bytes 116740
  0.0 19.6 %copy-start = (bf16[76,256]{1,0:T(8,128)(2,1)S(1)}, bf16[76,256]{1,0:T(8,128)(2,1)}, u32[]{:S(2)}) copy-start(bf16[76,256]{1,0:T(8,128)(2,1)} %enc_ref.1) | copy-start | bytes 116740
  1.3 6.4 %copy-start.4 = (bf16[76,16,256]{2,0,1:T(8,128)(2,1)}, bf16[76,16,256]{2,0,1:T(8,128)(2,1)S(1)}, u32[]{:S(2)}) copy-start(bf16[76,16,256]{2,0,1:T(8,128)(2,1)S(1)} %copy.15) | copy-start | bytes 1867780
  1.4 18.2 %collective-permute-start.3 = (bf16[76,4,256]{2,0,1:T(8,128)(2,1)S(1)}, bf16[76,4,256]{2,0,1:T(8,128)(2,1)S(1)}, u32[]{:S(2)}, u32[]{:S(2)}) collective-permute-start(bf16[76,4,256]{2,0,1:T(8,128)(2,1)S(1)} %get-tuple-element.34), channel_id=1, source_target_pairs={{16,0},{32,16},{48,32},{64,48},{80,64},{96,80},{112,96},{0,112},{1... | collective-permute-start | bytes 466952 | tf_op jit(solution)/shard_map/ppermute | solution.py:383
  5.9 13.7 %collective-permute-start.2 = (bf16[76,4,256]{2,0,1:T(8,128)(2,1)S(1)}, bf16[76,4,256]{2,0,1:T(8,128)(2,1)S(1)}, u32[]{:S(2)}, u32[]{:S(2)}) collective-permute-start(bf16[76,4,256]{2,0,1:T(8,128)(2,1)S(1)} %get-tuple-element.33), channel_id=1, source_target_pairs={{0,16},{16,32},{32,48},{48,64},{64,80},{80,96},{96,112},{112,0},{1... | collective-permute-start | bytes 466952 | tf_op jit(solution)/shard_map/ppermute | solution.py:383
  8.7 22.0 %all-to-all-start = ((bf16[128,8,128]{2,1,0:T(8,128)(2,1)}), bf16[128,8,128]{2,1,0:T(8,128)(2,1)S(1)}, u32[]{:S(2)}, u32[]{:S(2)}) async-start(bf16[128,8,128]{2,1,0:T(8,128)(2,1)} %pack_observations.1), calls=%async_computation | async-start | bytes 524288 | tf_op jit(solution)/shard_map/all_to_all | solution.py:473
  22.4 17.0 %collective-permute-start.4 = (bf16[24,8,256]{2,1,0:T(8,128)(2,1)}, bf16[24,8,256]{2,1,0:T(8,128)(2,1)}, u32[]{:S(2)}, u32[]{:S(2)}) collective-permute-start(bf16[24,8,256]{2,1,0:T(8,128)(2,1)} %get-tuple-element.56), channel_id=1, source_target_pairs={{0,1},{1,2},{2,3},{3,4},{4,5},{5,6},{6,7},{7,8},{8,9},{9,10},{10,1... | collective-permute-start | bytes 294920 | tf_op jit(solution)/shard_map/ppermute | solution.py:383
  25.6 13.9 %copy-start.3 = (f32[2,256]{1,0:T(2,128)S(1)}, f32[2,256]{1,0:T(2,128)}, u32[]{:S(2)}) copy-start(f32[2,256]{1,0:T(2,128)} %gain_ref.5) | copy-start | bytes 6148
  25.6 13.9 %collective-permute-start.5 = (bf16[24,8,256]{2,1,0:T(8,128)(2,1)}, bf16[24,8,256]{2,1,0:T(8,128)(2,1)}, u32[]{:S(2)}, u32[]{:S(2)}) collective-permute-start(bf16[24,8,256]{2,1,0:T(8,128)(2,1)} %get-tuple-element.55), channel_id=1, source_target_pairs={{1,0},{2,1},{3,2},{4,3},{5,4},{6,5},{7,6},{8,7},{9,8},{10,9},{11,1... | collective-permute-start | bytes 294920 | tf_op jit(solution)/shard_map/ppermute | solution.py:383
  30.7 8.8 %copy-start.1 = (bf16[2,256,1024]{2,1,0:T(8,128)(2,1)S(1)}, bf16[2,256,1024]{2,1,0:T(8,128)(2,1)}, u32[]{:S(2)}) copy-start(bf16[2,256,1024]{2,1,0:T(8,128)(2,1)} %up_ref.5) | copy-start | bytes 3145732
  30.7 8.8 %copy-start.2 = (bf16[2,1024,256]{2,1,0:T(8,128)(2,1)S(1)}, bf16[2,1024,256]{2,1,0:T(8,128)(2,1)}, u32[]{:S(2)}) copy-start(bf16[2,1024,256]{2,1,0:T(8,128)(2,1)} %down_ref.5) | copy-start | bytes 3145732
  36.1 12.3 %collective-permute-start.1 = (bf16[16,8,256]{2,1,0:T(8,128)(2,1)S(1)}, bf16[16,8,256]{2,1,0:T(8,128)(2,1)S(1)}, u32[]{:S(2)}, u32[]{:S(2)}) collective-permute-start(bf16[16,8,256]{2,1,0:T(8,128)(2,1)S(1)} %get-tuple-element.32), channel_id=1, source_target_pairs={{1,0},{2,1},{3,2},{4,3},{5,4},{6,5},{7,6},{8,7},{9,8},{10,9},{11,1... | collective-permute-start | bytes 196616 | tf_op jit(solution)/shard_map/ppermute | solution.py:383
  37.0 11.4 %collective-permute-start = (bf16[16,8,256]{2,1,0:T(8,128)(2,1)S(1)}, bf16[16,8,256]{2,1,0:T(8,128)(2,1)S(1)}, u32[]{:S(2)}, u32[]{:S(2)}) collective-permute-start(bf16[16,8,256]{2,1,0:T(8,128)(2,1)S(1)} %get-tuple-element.31), channel_id=1, source_target_pairs={{0,1},{1,2},{2,3},{3,4},{4,5},{5,6},{6,7},{7,8},{8,9},{9,10},{10,1... | collective-permute-start | bytes 196616 | tf_op jit(solution)/shard_map/ppermute | solution.py:383
  48.5 12.4 %collective-permute-start.7 = (bf16[2,272,256]{2,1,0:T(8,128)(2,1)S(1)}, bf16[2,272,256]{2,1,0:T(8,128)(2,1)S(1)}, u32[]{:S(2)}, u32[]{:S(2)}) collective-permute-start(bf16[2,272,256]{2,1,0:T(8,128)(2,1)S(1)} %pad_maximum_fusion.1), channel_id=1, source_target_pairs={{16,0},{32,16},{48,32},{64,48},{80,64},{96,80},{112,96},{0,112},{1... | collective-permute-start | bytes 835592 | tf_op jit(solution)/shard_map/ppermute | solution.py:383
  49.5 12.5 %collective-permute-start.6 = (bf16[2,272,256]{2,1,0:T(8,128)(2,1)S(1)}, bf16[2,272,256]{2,1,0:T(8,128)(2,1)S(1)}, u32[]{:S(2)}, u32[]{:S(2)}) collective-permute-start(bf16[2,272,256]{2,1,0:T(8,128)(2,1)S(1)} %pad_maximum_fusion), channel_id=1, source_target_pairs={{0,16},{16,32},{32,48},{48,64},{64,80},{80,96},{96,112},{112,0},{1... | collective-permute-start | bytes 835592 | tf_op jit(solution)/shard_map/ppermute | solution.py:383

commit v5 on v4

--- a/solution.py
+++ b/solution.py
@@ -103,8 +103,8 @@
 def normalize(spatial, mean_ref):
     square = (spatial * spatial).astype(BF)
     mean = jnp.dot(square, mean_ref[...], preferred_element_type=F32)
-    inv = lax.rsqrt(mean + EPSILON).astype(BF)
-    return inv, spatial * twice(inv)
+    inv = lax.rsqrt(mean + EPSILON)
+    return inv, spatial * twice(inv.astype(BF))
 
 
 def forward(b, hat, gain_ref, up_ref, down_ref, act_ref, slope_ref):
@@ -126,7 +126,7 @@
     weighted = times_transposed(act_ref[...], up_ref[b]) * (0.5 * gain_ref[b : b + 1, :])
     weighted = weighted.astype(BF)
     projection = jnp.dot(weighted * hat, mean_ref[...], preferred_element_type=F32)
-    return twice(inv) * (weighted - hat * twice(projection.astype(BF)))
+    return twice(inv.astype(BF)) * (weighted - hat * twice(projection.astype(BF)))
 
 
 def row_mask(first):
@@ -395,7 +395,7 @@
             sds((HIGH0, COLS, SUBL, HID), BF),
             sds((TAPE, EXP), BF),
             sds((TAPE, HID), BF),
-            sds((TAPE, LANES), BF),
+            sds((TAPE, LANES), F32),
         ],
         in_specs=[vmem()] * 7 + [anywhere()] * whole,
         out_specs=[anywhere()] * 4,
@@ -407,7 +407,7 @@
             pltpu.VMEM((RF * WIDE, EXP), BF),
             pltpu.VMEM((3, RF * WIDE, EXP), BF),
             pltpu.VMEM((3, RF * WIDE, HID), BF),
-            pltpu.VMEM((3, RF * WIDE, LANES), BF),
+            pltpu.VMEM((3, RF * WIDE, LANES), F32),
             pltpu.VMEM((3, RF, COLS, SUBL, HID), BF),
             pltpu.SemaphoreType.DMA((3, 4)),
         ],

time: 95.9 us -> 95.3 us (level)
  Pallas kernels: 59.5 us -> 58.2 us
    pallas_call x2, Pallas kernels: 19.6 us -> 18.3 us  [forward_call(): pl.pallas_call(functools.partial(forward_kernel, first, count), out_shape...]
  transfers between devices with their start and end apart: 9 -> 9, of which waited for: 2 -> 2; matrix products, arithmetic and copies ran while one was open for 5% -> 5% of each run, Pallas kernels for 27% -> 26%
where the time goes in v5:
time: 95.3 us; the launch traced here: 95 us
  Pallas kernels  58.2 us (61%)
  starting transfers between devices  23.5 us (25%)
  waiting for transfers between devices  6.84 us (7%)
  local copies, waits for them, and re-layouts  3.97 us (4%)
  matrix products  2.1 us (2%)
    pallas_call x1, Pallas kernels, main_call(): pl.pallas_call(functools.partial(main_kernel, levels), out_shape=sds((cha...  33.6 us
    pallas_call x2, Pallas kernels, forward_call(): pl.pallas_call(functools.partial(forward_kernel, first, count), out_shape...  18.3 us
    ppermute x8, starting transfers between devices, pair_shift(): return (lax.ppermute(high, axis, up), lax.ppermute(low, axis, down))  12.8 us
    all_to_all x1, starting transfers between devices, body(): lax.all_to_all(packed, ('lat', 'lon'), split_axis=0, concat_axis=0, tiled...  10.7 us
    pallas_call x1, Pallas kernels, body(): pl.pallas_call(functools.partial(place_observations, slots, levels), out_...  5.44 us
    all_to_all x1, waiting for transfers between devices, body(): lax.all_to_all(packed, ('lat', 'lon'), split_axis=0, concat_axis=0, tiled...  5.08 us
    unnamed x22, local copies, waits for them, and re-layouts  3.23 us
    dot_general x1, matrix products, body(): lax.dot_general(tall, enc_weight, (((0,), (0,)), ((), ())), preferred_ele...  2.1 us
  transfers between devices with their start and end apart: 9, of which 2 were waited for; matrix products, arithmetic and copies ran while one was open for 5% of the time, Pallas kernels for 26%

profile of v5, /device:TPU:1, one launch (start us, length us, event | category | flops | bytes accessed | tf_op | source)
XLA Modules:
  0.0 95.0 jit_solution(8879932043017377168)
XLA Ops:
  0.0 1.3 %copy.15 = bf16[76,16,256]{2,0,1:T(8,128)(2,1)S(1)} copy(bf16[76,16,256]{2,1,0:T(8,128)(2,1)} %param.10) | data formatting | bytes 1245184 | tf_op args[0]
  1.3 0.0 copy-start.4
  1.4 4.6 %collective-permute-start.3 = (bf16[76,4,256]{2,0,1:T(8,128)(2,1)S(1)}, bf16[76,4,256]{2,0,1:T(8,128)(2,1)S(1)}, u32[]{:S(2)}, u32[]{:S(2)}) collective-permute-start(bf16[76,4,256]{2,0,1:T(8,128)(2,1)S(1)} %get-tuple-element.34), channel_id=1, source_target_pairs={{16,0},{32,16},{48,32},{64,48},{80,64},{96,80},{112,96},{0,112},{1... | collective-permute-start | bytes 466952 | tf_op jit(solution)/shard_map/ppermute | solution.py:383
  5.9 0.7 copy.30
  6.6 1.1 %copy.28 = f32[1,128,12,76]{1,3,0,2:T(8,128)S(1)} copy(f32[1,128,12,76]{1,0,3,2:T(1,128)} %param.17) | data formatting | bytes 933888
  7.8 0.9 pack_observations.1
  8.7 10.7 %all-to-all-start = ((bf16[128,8,128]{2,1,0:T(8,128)(2,1)}), bf16[128,8,128]{2,1,0:T(8,128)(2,1)S(1)}, u32[]{:S(2)}, u32[]{:S(2)}) async-start(bf16[128,8,128]{2,1,0:T(8,128)(2,1)} %pack_observations.1), calls=%async_computation | async-start | bytes 524288 | tf_op jit(solution)/shard_map/all_to_all | solution.py:473
  19.4 0.1 copy.21.dec_ref
  19.6 0.0 collective-permute-done.2
  19.6 2.1 %convolution_convert_fusion.main_ref = bf16[24,256,256]{2,1,0:T(8,128)(2,1)S(1)} fusion(bf16[76,4,256]{2,0,1:T(8,128)(2,1)S(1)} %broadcast_select_fusion, bf16[76,16,256]{2,0,1:T(8,128)(2,1)} %copy-done.4, bf16[76,4,256]{2,0,1:T(8,128)(2,1)S(1)} %broadcast_select_fusion.1, bf16[76,256]{1,0:T(8,128)(2,1)S(1)} %copy-done), kind=kOutput, calls=%fused_computation | convolution fusion | flops 241582080 | bytes 4118528 | tf_op jit(solution)/shard_map/dot_general | solution.py:479
  21.8 0.7 fusion.7
  22.4 3.1 %collective-permute-start.4 = (bf16[24,8,256]{2,1,0:T(8,128)(2,1)}, bf16[24,8,256]{2,1,0:T(8,128)(2,1)}, u32[]{:S(2)}, u32[]{:S(2)}) collective-permute-start(bf16[24,8,256]{2,1,0:T(8,128)(2,1)} %get-tuple-element.56), channel_id=1, source_target_pairs={{0,1},{1,2},{2,3},{3,4},{4,5},{5,6},{6,7},{7,8},{8,9},{9,10},{10,1... | collective-permute-start | bytes 294920 | tf_op jit(solution)/shard_map/ppermute | solution.py:383
  25.6 5.1 %all-to-all-done.table_ref = bf16[128,8,128]{2,1,0:T(8,128)(2,1)S(1)} async-done(((bf16[128,8,128]{2,1,0:T(8,128)(2,1)}), bf16[128,8,128]{2,1,0:T(8,128)(2,1)S(1)}, u32[]{:S(2)}, u32[]{:S(2)}) %all-to-all-start) | async-done | bytes 262176 | tf_op jit(solution)/shard_map/all_to_all | solution.py:473
  30.7 5.4 %place_observations.1 = (f32[16,256,256]{2,1,0:T(8,128)S(1)}, bf16[2,256,256]{2,1,0:T(8,128)(2,1)S(1)}, bf16[2,256,256]{2,1,0:T(8,128)(2,1)S(1)}, bf16[16,8,256]{2,1,0:T(8,128)(2,1)S(1)}, bf16[16,8,256]{2,1,0:T(8,128)(2,1)S(1)}) custom-call(bf16[128,8,128]{2,1,0:T(8,128)(2,1)S(1)} %all-to-all-done.table_ref), custom_call_target="tpu_custom_call" | custom-call | flops 3221225472 | bytes 4194304 | tf_op jit(solution)/shard_map/place_observations/pallas_call | solution.py:484
  36.1 0.9 collective-permute-start.1
  37.0 2.4 %collective-permute-start = (bf16[16,8,256]{2,1,0:T(8,128)(2,1)S(1)}, bf16[16,8,256]{2,1,0:T(8,128)(2,1)S(1)}, u32[]{:S(2)}, u32[]{:S(2)}) collective-permute-start(bf16[16,8,256]{2,1,0:T(8,128)(2,1)S(1)} %get-tuple-element.31), channel_id=1, source_target_pairs={{0,1},{1,2},{2,3},{3,4},{4,5},{5,6},{6,7},{7,8},{8,9},{9,10},{10,1... | collective-permute-start | bytes 196616 | tf_op jit(solution)/shard_map/ppermute | solution.py:383
  39.4 0.0 collective-permute-done.4.left_ref
  39.4 0.0 collective-permute-done.5.right_ref
  39.5 8.4 %forward_zero.2 = (bf16[22,17,16,256]{3,2,1,0:T(8,128)(2,1)S(1)}, bf16[4896,1024]{1,0:T(8,128)(2,1)S(1)}, bf16[4896,256]{1,0:T(8,128)(2,1)S(1)}, f32[4896,128]{1,0:T(8,128)S(1)}) custom-call(bf16[24,8,256]{2,1,0:T(8,128)(2,1)} %collective-permute-done.4.left_ref, bf16[24,256,256]{2,1,0:T(8,128)(2,1)S(1)} %convolution_convert_fusion.main_ref, ...), custom_call_target="tpu_custom_call" | custom-call | flops 8556380160 | bytes 10027008 | tf_op jit(solution)/shard_map/forward_zero/pallas_call | solution.py:392
  47.9 0.9 collective-permute-start.7
  48.9 0.9 collective-permute-start.6
  49.8 9.9 %forward_zero.3 = (bf16[22,17,16,256]{3,2,1,0:T(8,128)(2,1)S(1)}, bf16[4896,1024]{1,0:T(8,128)(2,1)S(1)}, bf16[4896,256]{1,0:T(8,128)(2,1)S(1)}, f32[4896,128]{1,0:T(8,128)S(1)}) custom-call(bf16[24,8,256]{2,1,0:T(8,128)(2,1)} %collective-permute-done.4.left_ref, ...), custom_call_target="tpu_custom_call", output_to_operand_aliasing={{0}: (7, {}), {1}: (8, {}), {2}: (9, {}), {3}: (10, {})} | custom-call | flops 10267656192 | bytes 10027008 | tf_op jit(solution)/shard_map/forward_zero/pallas_call | solution.py:392
  59.7 1.7 %collective-permute-done.6.above_ref = bf16[2,272,256]{2,1,0:T(8,128)(2,1)S(1)} collective-permute-done((bf16[2,272,256]{2,1,0:T(8,128)(2,1)S(1)}, bf16[2,272,256]{2,1,0:T(8,128)(2,1)S(1)}, u32[]{:S(2)}, u32[]{:S(2)}) %collective-permute-start.6) | collective-permute-done | bytes 278560 | tf_op jit(solution)/shard_map/ppermute | solution.py:383
  61.4 33.6 %forward_one_and_adjoint.1 = f32[1216,256]{1,0:T(8,128)} custom-call(bf16[2,272,256]{2,1,0:T(8,128)(2,1)S(1)} %collective-permute-done.6.above_ref, bf16[2,272,256]{2,1,0:T(8,128)(2,1)S(1)} %collective-permute-done.7.below_ref, bf16[16,8,256]{2,1,0:T(8,128)(2,1)S(1)} %collective-permute-done.left_ref, f32[16,256,256]{2,1,0:T(8,128)S(1)} %get-tuple-element.44.main_ref, ...), custom_call_target="tpu_custom_call" | custom-call | flops 16542334976 | bytes 10027008 | tf_op jit(solution)/shard_map/forward_one_and_adjoint/pallas_call | solution.py:424
  (30 shorter events, 0.2 us)
Async XLA Ops:
  0.0 7.7 %copy-start.7 = (s32[1,128,12]{1,0,2:T(1,128)S(1)}, s32[1,128,12]{1,0,2:T(1,128)}, u32[]{:S(2)}) copy-start(s32[1,128,12]{1,0,2:T(1,128)} %param.19) | copy-start | bytes 18436
  0.0 19.4 %copy-start.6 = (f32[2,3,3,256]{3,0,2,1:T(2,128)S(1)}, f32[2,3,3,256]{3,0,2,1:T(2,128)}, u32[]{:S(2)}) copy-start(f32[2,3,3,256]{3,0,2,1:T(2,128)} %param.12) | copy-start | bytes 55300
  0.0 19.4 %copy-start.5 = (bf16[256,76]{0,1:T(8,128)(2,1)S(1)}, bf16[256,76]{0,1:T(8,128)(2,1)}, u32[]{:S(2)}) copy-start(bf16[256,76]{0,1:T(8,128)(2,1)} %param.16) | copy-start | bytes 116740
  0.0 19.6 %copy-start = (bf16[76,256]{1,0:T(8,128)(2,1)S(1)}, bf16[76,256]{1,0:T(8,128)(2,1)}, u32[]{:S(2)}) copy-start(bf16[76,256]{1,0:T(8,128)(2,1)} %enc_ref.1) | copy-start | bytes 116740
  1.3 6.4 %copy-start.4 = (bf16[76,16,256]{2,0,1:T(8,128)(2,1)}, bf16[76,16,256]{2,0,1:T(8,128)(2,1)S(1)}, u32[]{:S(2)}) copy-start(bf16[76,16,256]{2,0,1:T(8,128)(2,1)S(1)} %copy.15) | copy-start | bytes 1867780
  1.4 18.2 %collective-permute-start.3 = (bf16[76,4,256]{2,0,1:T(8,128)(2,1)S(1)}, bf16[76,4,256]{2,0,1:T(8,128)(2,1)S(1)}, u32[]{:S(2)}, u32[]{:S(2)}) collective-permute-start(bf16[76,4,256]{2,0,1:T(8,128)(2,1)S(1)} %get-tuple-element.34), channel_id=1, source_target_pairs={{16,0},{32,16},{48,32},{64,48},{80,64},{96,80},{112,96},{0,112},{1... | collective-permute-start | bytes 466952 | tf_op jit(solution)/shard_map/ppermute | solution.py:383
  5.9 13.7 %collective-permute-start.2 = (bf16[76,4,256]{2,0,1:T(8,128)(2,1)S(1)}, bf16[76,4,256]{2,0,1:T(8,128)(2,1)S(1)}, u32[]{:S(2)}, u32[]{:S(2)}) collective-permute-start(bf16[76,4,256]{2,0,1:T(8,128)(2,1)S(1)} %get-tuple-element.33), channel_id=1, source_target_pairs={{0,16},{16,32},{32,48},{48,64},{64,80},{80,96},{96,112},{112,0},{1... | collective-permute-start | bytes 466952 | tf_op jit(solution)/shard_map/ppermute | solution.py:383
  8.7 22.0 %all-to-all-start = ((bf16[128,8,128]{2,1,0:T(8,128)(2,1)}), bf16[128,8,128]{2,1,0:T(8,128)(2,1)S(1)}, u32[]{:S(2)}, u32[]{:S(2)}) async-start(bf16[128,8,128]{2,1,0:T(8,128)(2,1)} %pack_observations.1), calls=%async_computation | async-start | bytes 524288 | tf_op jit(solution)/shard_map/all_to_all | solution.py:473
  22.4 17.0 %collective-permute-start.4 = (bf16[24,8,256]{2,1,0:T(8,128)(2,1)}, bf16[24,8,256]{2,1,0:T(8,128)(2,1)}, u32[]{:S(2)}, u32[]{:S(2)}) collective-permute-start(bf16[24,8,256]{2,1,0:T(8,128)(2,1)} %get-tuple-element.56), channel_id=1, source_target_pairs={{0,1},{1,2},{2,3},{3,4},{4,5},{5,6},{6,7},{7,8},{8,9},{9,10},{10,1... | collective-permute-start | bytes 294920 | tf_op jit(solution)/shard_map/ppermute | solution.py:383
  25.6 13.9 %copy-start.3 = (f32[2,256]{1,0:T(2,128)S(1)}, f32[2,256]{1,0:T(2,128)}, u32[]{:S(2)}) copy-start(f32[2,256]{1,0:T(2,128)} %gain_ref.5) | copy-start | bytes 6148
  25.6 13.9 %collective-permute-start.5 = (bf16[24,8,256]{2,1,0:T(8,128)(2,1)}, bf16[24,8,256]{2,1,0:T(8,128)(2,1)}, u32[]{:S(2)}, u32[]{:S(2)}) collective-permute-start(bf16[24,8,256]{2,1,0:T(8,128)(2,1)} %get-tuple-element.55), channel_id=1, source_target_pairs={{1,0},{2,1},{3,2},{4,3},{5,4},{6,5},{7,6},{8,7},{9,8},{10,9},{11,1... | collective-permute-start | bytes 294920 | tf_op jit(solution)/shard_map/ppermute | solution.py:383
  30.7 8.8 %copy-start.1 = (bf16[2,256,1024]{2,1,0:T(8,128)(2,1)S(1)}, bf16[2,256,1024]{2,1,0:T(8,128)(2,1)}, u32[]{:S(2)}) copy-start(bf16[2,256,1024]{2,1,0:T(8,128)(2,1)} %up_ref.5) | copy-start | bytes 3145732
  30.7 8.8 %copy-start.2 = (bf16[2,1024,256]{2,1,0:T(8,128)(2,1)S(1)}, bf16[2,1024,256]{2,1,0:T(8,128)(2,1)}, u32[]{:S(2)}) copy-start(bf16[2,1024,256]{2,1,0:T(8,128)(2,1)} %down_ref.5) | copy-start | bytes 3145732
  36.1 11.8 %collective-permute-start.1 = (bf16[16,8,256]{2,1,0:T(8,128)(2,1)S(1)}, bf16[16,8,256]{2,1,0:T(8,128)(2,1)S(1)}, u32[]{:S(2)}, u32[]{:S(2)}) collective-permute-start(bf16[16,8,256]{2,1,0:T(8,128)(2,1)S(1)} %get-tuple-element.32), channel_id=1, source_target_pairs={{1,0},{2,1},{3,2},{4,3},{5,4},{6,5},{7,6},{8,7},{9,8},{10,9},{11,1... | collective-permute-start | bytes 196616 | tf_op jit(solution)/shard_map/ppermute | solution.py:383
  37.0 10.9 %collective-permute-start = (bf16[16,8,256]{2,1,0:T(8,128)(2,1)S(1)}, bf16[16,8,256]{2,1,0:T(8,128)(2,1)S(1)}, u32[]{:S(2)}, u32[]{:S(2)}) collective-permute-start(bf16[16,8,256]{2,1,0:T(8,128)(2,1)S(1)} %get-tuple-element.31), channel_id=1, source_target_pairs={{0,1},{1,2},{2,3},{3,4},{4,5},{5,6},{6,7},{7,8},{8,9},{9,10},{10,1... | collective-permute-start | bytes 196616 | tf_op jit(solution)/shard_map/ppermute | solution.py:383
  47.9 11.7 %collective-permute-start.7 = (bf16[2,272,256]{2,1,0:T(8,128)(2,1)S(1)}, bf16[2,272,256]{2,1,0:T(8,128)(2,1)S(1)}, u32[]{:S(2)}, u32[]{:S(2)}) collective-permute-start(bf16[2,272,256]{2,1,0:T(8,128)(2,1)S(1)} %pad_maximum_fusion.1), channel_id=1, source_target_pairs={{16,0},{32,16},{48,32},{64,48},{80,64},{96,80},{112,96},{0,112},{1... | collective-permute-start | bytes 835592 | tf_op jit(solution)/shard_map/ppermute | solution.py:383
  48.9 12.5 %collective-permute-start.6 = (bf16[2,272,256]{2,1,0:T(8,128)(2,1)S(1)}, bf16[2,272,256]{2,1,0:T(8,128)(2,1)S(1)}, u32[]{:S(2)}, u32[]{:S(2)}) collective-permute-start(bf16[2,272,256]{2,1,0:T(8,128)(2,1)S(1)} %pad_maximum_fusion), channel_id=1, source_target_pairs={{0,16},{16,32},{32,48},{48,64},{64,80},{80,96},{96,112},{112,0},{1... | collective-permute-start | bytes 835592 | tf_op jit(solution)/shard_map/ppermute | solution.py:383

commit v6 on v5

--- a/solution.py
+++ b/solution.py
@@ -507,7 +507,7 @@
     )(table)
 
     west, east = pair_shift(f_left, f_right, "lon")
-    first_rows = 10
+    first_rows = 6
     main, f_left = lax.optimization_barrier((main, f_left))
     part_a = forward_call(
         0, first_rows, left, main, right, kernels, gains, up_weight, down_weight

time: 95.3 us -> 93.8 us (0.984)
  waiting for transfers between devices: 6.84 us -> 5.28 us
    ppermute x8, waiting for transfers between devices: 1.77 us -> 0.21 us  [pair_shift(): return (lax.ppermute(high, axis, up), lax.ppermute(low, axis, down))]
where the time goes in v6:
time: 93.8 us; the launch traced here: 93.4 us
  Pallas kernels  58.2 us (62%)
  starting transfers between devices  23.5 us (25%)
  waiting for transfers between devices  5.28 us (6%)
  local copies, waits for them, and re-layouts  3.97 us (4%)
  matrix products  2.1 us (2%)
    pallas_call x1, Pallas kernels, main_call(): pl.pallas_call(functools.partial(main_kernel, levels), out_shape=sds((cha...  33.6 us
    pallas_call x2, Pallas kernels, forward_call(): pl.pallas_call(functools.partial(forward_kernel, first, count), out_shape...  18.3 us
    ppermute x8, starting transfers between devices, pair_shift(): return (lax.ppermute(high, axis, up), lax.ppermute(low, axis, down))  12.8 us
    all_to_all x1, starting transfers between devices, body(): lax.all_to_all(packed, ('lat', 'lon'), split_axis=0, concat_axis=0, tiled...  10.7 us
    pallas_call x1, Pallas kernels, body(): pl.pallas_call(functools.partial(place_observations, slots, levels), out_...  5.44 us
    all_to_all x1, waiting for transfers between devices, body(): lax.all_to_all(packed, ('lat', 'lon'), split_axis=0, concat_axis=0, tiled...  5.08 us
    unnamed x22, local copies, waits for them, and re-layouts  3.23 us
    dot_general x1, matrix products, body(): lax.dot_general(tall, enc_weight, (((0,), (0,)), ((), ())), preferred_ele...  2.1 us
  transfers between devices with their start and end apart: 9, of which 2 were waited for; matrix products, arithmetic and copies ran while one was open for 5% of the time, Pallas kernels for 26%

profile of v6, /device:TPU:1, one launch (start us, length us, event | category | flops | bytes accessed | tf_op | source)
XLA Modules:
  0.0 93.4 jit_solution(12625200631627645967)
XLA Ops:
  0.0 1.3 %copy.15 = bf16[76,16,256]{2,0,1:T(8,128)(2,1)S(1)} copy(bf16[76,16,256]{2,1,0:T(8,128)(2,1)} %param.10) | data formatting | bytes 1245184 | tf_op args[0]
  1.3 0.0 copy-start.4
  1.4 4.6 %collective-permute-start.3 = (bf16[76,4,256]{2,0,1:T(8,128)(2,1)S(1)}, bf16[76,4,256]{2,0,1:T(8,128)(2,1)S(1)}, u32[]{:S(2)}, u32[]{:S(2)}) collective-permute-start(bf16[76,4,256]{2,0,1:T(8,128)(2,1)S(1)} %get-tuple-element.34), channel_id=1, source_target_pairs={{16,0},{32,16},{48,32},{64,48},{80,64},{96,80},{112,96},{0,112},{1... | collective-permute-start | bytes 466952 | tf_op jit(solution)/shard_map/ppermute | solution.py:383
  5.9 0.0 collective-permute-start.2
  5.9 0.7 copy.30
  6.6 1.1 %copy.28 = f32[1,128,12,76]{1,3,0,2:T(8,128)S(1)} copy(f32[1,128,12,76]{1,0,3,2:T(1,128)} %param.17) | data formatting | bytes 933888
  7.8 0.9 pack_observations.1
  8.7 10.7 %all-to-all-start = ((bf16[128,8,128]{2,1,0:T(8,128)(2,1)}), bf16[128,8,128]{2,1,0:T(8,128)(2,1)S(1)}, u32[]{:S(2)}, u32[]{:S(2)}) async-start(bf16[128,8,128]{2,1,0:T(8,128)(2,1)} %pack_observations.1), calls=%async_computation | async-start | bytes 524288 | tf_op jit(solution)/shard_map/all_to_all | solution.py:473
  19.4 0.1 copy.21.dec_ref
  19.6 0.0 collective-permute-done.3
  19.6 0.0 collective-permute-done.2
  19.6 2.1 %convolution_convert_fusion.main_ref = bf16[24,256,256]{2,1,0:T(8,128)(2,1)S(1)} fusion(bf16[76,4,256]{2,0,1:T(8,128)(2,1)S(1)} %broadcast_select_fusion, bf16[76,16,256]{2,0,1:T(8,128)(2,1)} %copy-done.4, bf16[76,4,256]{2,0,1:T(8,128)(2,1)S(1)} %broadcast_select_fusion.1, bf16[76,256]{1,0:T(8,128)(2,1)S(1)} %copy-done), kind=kOutput, calls=%fused_computation | convolution fusion | flops 241582080 | bytes 4118528 | tf_op jit(solution)/shard_map/dot_general | solution.py:479
  21.8 0.7 fusion.7
  22.4 3.1 %collective-permute-start.4 = (bf16[24,8,256]{2,1,0:T(8,128)(2,1)}, bf16[24,8,256]{2,1,0:T(8,128)(2,1)}, u32[]{:S(2)}, u32[]{:S(2)}) collective-permute-start(bf16[24,8,256]{2,1,0:T(8,128)(2,1)} %get-tuple-element.56), channel_id=1, source_target_pairs={{0,1},{1,2},{2,3},{3,4},{4,5},{5,6},{6,7},{7,8},{8,9},{9,10},{10,1... | collective-permute-start | bytes 294920 | tf_op jit(solution)/shard_map/ppermute | solution.py:383
  25.6 5.1 %all-to-all-done.table_ref = bf16[128,8,128]{2,1,0:T(8,128)(2,1)S(1)} async-done(((bf16[128,8,128]{2,1,0:T(8,128)(2,1)}), bf16[128,8,128]{2,1,0:T(8,128)(2,1)S(1)}, u32[]{:S(2)}, u32[]{:S(2)}) %all-to-all-start) | async-done | bytes 262176 | tf_op jit(solution)/shard_map/all_to_all | solution.py:473
  30.7 5.4 %place_observations.1 = (f32[16,256,256]{2,1,0:T(8,128)S(1)}, bf16[2,256,256]{2,1,0:T(8,128)(2,1)S(1)}, bf16[2,256,256]{2,1,0:T(8,128)(2,1)S(1)}, bf16[16,8,256]{2,1,0:T(8,128)(2,1)S(1)}, bf16[16,8,256]{2,1,0:T(8,128)(2,1)S(1)}) custom-call(bf16[128,8,128]{2,1,0:T(8,128)(2,1)S(1)} %all-to-all-done.table_ref), custom_call_target="tpu_custom_call" | custom-call | flops 3221225472 | bytes 4194304 | tf_op jit(solution)/shard_map/place_observations/pallas_call | solution.py:484
  36.1 0.9 collective-permute-start.1
  37.0 2.4 %collective-permute-start = (bf16[16,8,256]{2,1,0:T(8,128)(2,1)S(1)}, bf16[16,8,256]{2,1,0:T(8,128)(2,1)S(1)}, u32[]{:S(2)}, u32[]{:S(2)}) collective-permute-start(bf16[16,8,256]{2,1,0:T(8,128)(2,1)S(1)} %get-tuple-element.31), channel_id=1, source_target_pairs={{0,1},{1,2},{2,3},{3,4},{4,5},{5,6},{6,7},{7,8},{8,9},{9,10},{10,1... | collective-permute-start | bytes 196616 | tf_op jit(solution)/shard_map/ppermute | solution.py:383
  39.5 5.4 %forward_zero.2 = (bf16[22,17,16,256]{3,2,1,0:T(8,128)(2,1)S(1)}, bf16[4896,1024]{1,0:T(8,128)(2,1)S(1)}, bf16[4896,256]{1,0:T(8,128)(2,1)S(1)}, f32[4896,128]{1,0:T(8,128)S(1)}) custom-call(bf16[24,8,256]{2,1,0:T(8,128)(2,1)} %collective-permute-done.4.left_ref, bf16[24,256,256]{2,1,0:T(8,128)(2,1)S(1)} %convolution_convert_fusion.main_ref, ...), custom_call_target="tpu_custom_call" | custom-call | flops 5133828096 | bytes 10027008 | tf_op jit(solution)/shard_map/forward_zero/pallas_call | solution.py:392
  44.9 0.9 collective-permute-start.7
  45.9 0.9 collective-permute-start.6
  46.8 12.9 %forward_zero.3 = (bf16[22,17,16,256]{3,2,1,0:T(8,128)(2,1)S(1)}, bf16[4896,1024]{1,0:T(8,128)(2,1)S(1)}, bf16[4896,256]{1,0:T(8,128)(2,1)S(1)}, f32[4896,128]{1,0:T(8,128)S(1)}) custom-call(bf16[24,8,256]{2,1,0:T(8,128)(2,1)} %collective-permute-done.4.left_ref, ...), custom_call_target="tpu_custom_call", output_to_operand_aliasing={{0}: (7, {}), {1}: (8, {}), {2}: (9, {}), {3}: (10, {})} | custom-call | flops 13690208256 | bytes 10027008 | tf_op jit(solution)/shard_map/forward_zero/pallas_call | solution.py:392
  59.7 0.2 collective-permute-done.6.above_ref
  59.9 33.6 %forward_one_and_adjoint.1 = f32[1216,256]{1,0:T(8,128)} custom-call(bf16[2,272,256]{2,1,0:T(8,128)(2,1)S(1)} %collective-permute-done.6.above_ref, bf16[2,272,256]{2,1,0:T(8,128)(2,1)S(1)} %collective-permute-done.7.below_ref, bf16[16,8,256]{2,1,0:T(8,128)(2,1)S(1)} %collective-permute-done.left_ref, f32[16,256,256]{2,1,0:T(8,128)S(1)} %get-tuple-element.44.main_ref, ...), custom_call_target="tpu_custom_call" | custom-call | flops 16542334976 | bytes 10027008 | tf_op jit(solution)/shard_map/forward_one_and_adjoint/pallas_call | solution.py:424
  (30 shorter events, 0.2 us)
Async XLA Ops:
  0.0 7.7 %copy-start.7 = (s32[1,128,12]{1,0,2:T(1,128)S(1)}, s32[1,128,12]{1,0,2:T(1,128)}, u32[]{:S(2)}) copy-start(s32[1,128,12]{1,0,2:T(1,128)} %param.19) | copy-start | bytes 18436
  0.0 19.4 %copy-start.6 = (f32[2,3,3,256]{3,0,2,1:T(2,128)S(1)}, f32[2,3,3,256]{3,0,2,1:T(2,128)}, u32[]{:S(2)}) copy-start(f32[2,3,3,256]{3,0,2,1:T(2,128)} %param.12) | copy-start | bytes 55300
  0.0 19.4 %copy-start.5 = (bf16[256,76]{0,1:T(8,128)(2,1)S(1)}, bf16[256,76]{0,1:T(8,128)(2,1)}, u32[]{:S(2)}) copy-start(bf16[256,76]{0,1:T(8,128)(2,1)} %param.16) | copy-start | bytes 116740
  0.0 19.6 %copy-start = (bf16[76,256]{1,0:T(8,128)(2,1)S(1)}, bf16[76,256]{1,0:T(8,128)(2,1)}, u32[]{:S(2)}) copy-start(bf16[76,256]{1,0:T(8,128)(2,1)} %enc_ref.1) | copy-start | bytes 116740
  1.3 6.4 %copy-start.4 = (bf16[76,16,256]{2,0,1:T(8,128)(2,1)}, bf16[76,16,256]{2,0,1:T(8,128)(2,1)S(1)}, u32[]{:S(2)}) copy-start(bf16[76,16,256]{2,0,1:T(8,128)(2,1)S(1)} %copy.15) | copy-start | bytes 1867780
  1.4 18.2 %collective-permute-start.3 = (bf16[76,4,256]{2,0,1:T(8,128)(2,1)S(1)}, bf16[76,4,256]{2,0,1:T(8,128)(2,1)S(1)}, u32[]{:S(2)}, u32[]{:S(2)}) collective-permute-start(bf16[76,4,256]{2,0,1:T(8,128)(2,1)S(1)} %get-tuple-element.34), channel_id=1, source_target_pairs={{16,0},{32,16},{48,32},{64,48},{80,64},{96,80},{112,96},{0,112},{1... | collective-permute-start | bytes 466952 | tf_op jit(solution)/shard_map/ppermute | solution.py:383
  5.9 13.7 %collective-permute-start.2 = (bf16[76,4,256]{2,0,1:T(8,128)(2,1)S(1)}, bf16[76,4,256]{2,0,1:T(8,128)(2,1)S(1)}, u32[]{:S(2)}, u32[]{:S(2)}) collective-permute-start(bf16[76,4,256]{2,0,1:T(8,128)(2,1)S(1)} %get-tuple-element.33), channel_id=1, source_target_pairs={{0,16},{16,32},{32,48},{48,64},{64,80},{80,96},{96,112},{112,0},{1... | collective-permute-start | bytes 466952 | tf_op jit(solution)/shard_map/ppermute | solution.py:383
  8.7 22.0 %all-to-all-start = ((bf16[128,8,128]{2,1,0:T(8,128)(2,1)}), bf16[128,8,128]{2,1,0:T(8,128)(2,1)S(1)}, u32[]{:S(2)}, u32[]{:S(2)}) async-start(bf16[128,8,128]{2,1,0:T(8,128)(2,1)} %pack_observations.1), calls=%async_computation | async-start | bytes 524288 | tf_op jit(solution)/shard_map/all_to_all | solution.py:473
  22.4 17.0 %collective-permute-start.4 = (bf16[24,8,256]{2,1,0:T(8,128)(2,1)}, bf16[24,8,256]{2,1,0:T(8,128)(2,1)}, u32[]{:S(2)}, u32[]{:S(2)}) collective-permute-start(bf16[24,8,256]{2,1,0:T(8,128)(2,1)} %get-tuple-element.56), channel_id=1, source_target_pairs={{0,1},{1,2},{2,3},{3,4},{4,5},{5,6},{6,7},{7,8},{8,9},{9,10},{10,1... | collective-permute-start | bytes 294920 | tf_op jit(solution)/shard_map/ppermute | solution.py:383
  25.6 13.9 %copy-start.3 = (f32[2,256]{1,0:T(2,128)S(1)}, f32[2,256]{1,0:T(2,128)}, u32[]{:S(2)}) copy-start(f32[2,256]{1,0:T(2,128)} %gain_ref.5) | copy-start | bytes 6148
  25.6 13.9 %collective-permute-start.5 = (bf16[24,8,256]{2,1,0:T(8,128)(2,1)}, bf16[24,8,256]{2,1,0:T(8,128)(2,1)}, u32[]{:S(2)}, u32[]{:S(2)}) collective-permute-start(bf16[24,8,256]{2,1,0:T(8,128)(2,1)} %get-tuple-element.55), channel_id=1, source_target_pairs={{1,0},{2,1},{3,2},{4,3},{5,4},{6,5},{7,6},{8,7},{9,8},{10,9},{11,1... | collective-permute-start | bytes 294920 | tf_op jit(solution)/shard_map/ppermute | solution.py:383
  30.7 8.8 %copy-start.1 = (bf16[2,256,1024]{2,1,0:T(8,128)(2,1)S(1)}, bf16[2,256,1024]{2,1,0:T(8,128)(2,1)}, u32[]{:S(2)}) copy-start(bf16[2,256,1024]{2,1,0:T(8,128)(2,1)} %up_ref.5) | copy-start | bytes 3145732
  30.7 8.8 %copy-start.2 = (bf16[2,1024,256]{2,1,0:T(8,128)(2,1)S(1)}, bf16[2,1024,256]{2,1,0:T(8,128)(2,1)}, u32[]{:S(2)}) copy-start(bf16[2,1024,256]{2,1,0:T(8,128)(2,1)} %down_ref.5) | copy-start | bytes 3145732
  36.1 8.8 %collective-permute-start.1 = (bf16[16,8,256]{2,1,0:T(8,128)(2,1)S(1)}, bf16[16,8,256]{2,1,0:T(8,128)(2,1)S(1)}, u32[]{:S(2)}, u32[]{:S(2)}) collective-permute-start(bf16[16,8,256]{2,1,0:T(8,128)(2,1)S(1)} %get-tuple-element.32), channel_id=1, source_target_pairs={{1,0},{2,1},{3,2},{4,3},{5,4},{6,5},{7,6},{8,7},{9,8},{10,9},{11,1... | collective-permute-start | bytes 196616 | tf_op jit(solution)/shard_map/ppermute | solution.py:383
  37.0 7.9 %collective-permute-start = (bf16[16,8,256]{2,1,0:T(8,128)(2,1)S(1)}, bf16[16,8,256]{2,1,0:T(8,128)(2,1)S(1)}, u32[]{:S(2)}, u32[]{:S(2)}) collective-permute-start(bf16[16,8,256]{2,1,0:T(8,128)(2,1)S(1)} %get-tuple-element.31), channel_id=1, source_target_pairs={{0,1},{1,2},{2,3},{3,4},{4,5},{5,6},{6,7},{7,8},{8,9},{9,10},{10,1... | collective-permute-start | bytes 196616 | tf_op jit(solution)/shard_map/ppermute | solution.py:383
  44.9 14.7 %collective-permute-start.7 = (bf16[2,272,256]{2,1,0:T(8,128)(2,1)S(1)}, bf16[2,272,256]{2,1,0:T(8,128)(2,1)S(1)}, u32[]{:S(2)}, u32[]{:S(2)}) collective-permute-start(bf16[2,272,256]{2,1,0:T(8,128)(2,1)S(1)} %pad_maximum_fusion.1), channel_id=1, source_target_pairs={{16,0},{32,16},{48,32},{64,48},{80,64},{96,80},{112,96},{0,112},{1... | collective-permute-start | bytes 835592 | tf_op jit(solution)/shard_map/ppermute | solution.py:383
  45.9 14.0 %collective-permute-start.6 = (bf16[2,272,256]{2,1,0:T(8,128)(2,1)S(1)}, bf16[2,272,256]{2,1,0:T(8,128)(2,1)S(1)}, u32[]{:S(2)}, u32[]{:S(2)}) collective-permute-start(bf16[2,272,256]{2,1,0:T(8,128)(2,1)S(1)} %pad_maximum_fusion), channel_id=1, source_target_pairs={{0,16},{16,32},{32,48},{48,64},{64,80},{80,96},{96,112},{112,0},{1... | collective-permute-start | bytes 835592 | tf_op jit(solution)/shard_map/ppermute | solution.py:383
